TPU v7x, 32 devices: a whole 2x2x4 slice. The times are simulated.
32 devices in a mesh: blk: 8 (over y, x, core), sims: 4 (over z).
Axes of the slice: x: 2, y: 2, z: 4, core: 2. Of those that a mesh axis runs over, the one named last changes fastest.
Arguments:
- rhs: float32 [4, 8, 256, 512], P(None, 'blk', None, 'sims'), parts along dimension 3, may hold values from -6 to 6
- lower_blocks: float32 [4, 8, 3, 256, 256], P(None, 'blk'), may hold values from -0.16875 to 0.16875
- col_index: int32 [4, 8, 3], P(None, 'blk'), may hold values from -1 to 30, as said below
- diag_inverse: float32 [4, 8, 256, 256], P(None, 'blk'), may hold values from -1.5 to 1.5, as said below
- turnout: float32 [4, 8, 256], P(None, 'blk'), may hold values from 0.2 to 5
- district_of: int32 [4, 8, 256], P(None, 'blk'), may hold values from 0 to 255, as said below
Outputs:
- solution: float32 [4, 8, 256, 512], P(None, 'blk', None, 'sims'), parts along dimension 3
- district_mean: float32 [256, 512], P('blk', 'sims'), parts along dimension 1
There are 4 independent parts, one for each index of `sims`. A program takes and returns all parts, laid end to end along the dimension named above; an argument that names none is the same for every part. Nothing has to cross between parts.
Inputs may be any that keep to these rules, and one draw needn't show every extreme that they name: `col_index`: entry [r, p, k] belongs to block row i = r * 8 + p. Slot 0 holds i - 1 (-1 for i = 0); the other slots hold distinct columns from i - 4 to i - 2, or -1 where the block is absent. `diag_inverse`: each block is lower triangular. `district_of`: each district holds exactly 32 precincts.
All inputs are finite; a program needn't handle non-finite values.
Results may differ from a plain program's by a relative error of at most 0.0002.
Values sent between devices are 32-bit elements; how exact they have to be, the bound alone decides.
No kernel may reach another device: no remote copies, remote signals or barrier semaphores. Data moves between devices by JAX's collectives and lax.ppermute only.
A program may use at most 64 MiB of HBM per device.

v0:
```python
import functools

import jax
import jax.numpy as jnp
from jax import lax
from jax.experimental import pallas as pl
from jax.experimental.pallas import tpu as pltpu
from jax.sharding import PartitionSpec as P

NDIST = 256
F32 = jnp.float32
B16 = jnp.bfloat16
SMEM_SPEC = pl.BlockSpec(memory_space=pltpu.SMEM)
VMEM_SPEC = pl.BlockSpec(memory_space=pltpu.VMEM)
HBM_SPEC = pl.BlockSpec(memory_space=pltpu.HBM)


def params(mib):
    return pltpu.CompilerParams(vmem_limit_bytes=mib * 1024 * 1024)


def cost(flops, moved):
    return pl.CostEstimate(flops=flops, bytes_accessed=moved, transcendentals=0)


def shaped(*shape, dtype=F32):
    return jax.ShapeDtypeStruct(shape, dtype)


def halves(x):
    hi = x.astype(B16)
    lo = (x - hi.astype(F32)).astype(B16)
    return hi, lo


def dot(a, b):
    return jnp.dot(a, b, preferred_element_type=F32)


def dot3(x, y):
    rows = x[0].shape[0]
    both = dot(jnp.concatenate([x[0], x[1]], axis=0), y[0])
    return both[:rows] + both[rows:] + dot(x[0], y[1])


def packed_places(slots, bs, columns):
    rhs_at = (slots + 1) * bs
    col_at = rhs_at + columns
    turnout_at = col_at + 8 * slots
    district_at = turnout_at + 8
    return rhs_at, col_at, turnout_at, district_at, district_at + 8


def chip_now():
    return lax.div(lax.axis_index("blk").astype(jnp.int32), 2)


def upper_here():
    return lax.rem(lax.axis_index("blk").astype(jnp.int32), 2) == 1


def pack_kernel(rows, cols, turnout, district, l_ref, d_ref, r_ref, *refs):
    outs = refs[: len(rows)]
    held, sems = refs[len(rows) :]
    slots, bs = l_ref.shape[2], l_ref.shape[3]
    columns = r_ref.shape[3]
    rhs_at, col_at, turnout_at, district_at, _ = packed_places(slots, bs, columns)
    copies = []

    def copy(source, target):
        copies.append(pltpu.make_async_copy(source, target, sems.at[len(copies)]))
        copies[-1].start()

    for i, r in enumerate(rows):
        copy(r_ref.at[r, 0], held.at[i])
    for out, r in zip(outs, rows):
        for k in range(slots):
            copy(l_ref.at[r, 0, k], out.at[pl.ds(k * bs, bs)])
        copy(d_ref.at[r, 0], out.at[pl.ds(slots * bs, bs)])
    for out, r in zip(outs, rows):
        for k in range(slots):
            at = col_at + 8 * k
            out[at : at + 8] = jnp.full((8, bs), cols[k, 0, r].astype(F32))
        out[turnout_at : turnout_at + 8] = jnp.broadcast_to(turnout[r], (8, bs))
        out[district_at : district_at + 8] = jnp.broadcast_to(
            district[r].astype(F32), (8, bs)
        )
    for i, out in enumerate(outs):
        copies[i].wait()
        out[rhs_at:col_at] = held[i].T
    for started in copies[len(rows) :]:
        started.wait()


def put(high, low, i, j, value):
    bs = value.shape[0]
    hi, lo = halves(value)
    high[i * bs : (i + 1) * bs, j * bs : (j + 1) * bs] = hi
    low[i * bs : (i + 1) * bs, j * bs : (j + 1) * bs] = lo


def blocks_of(r, n, slots, columns, own, oth):
    is_a = upper_here()
    bs = own.shape[1]
    _, col_at, _, _, _ = packed_places(slots, bs, columns)
    row_b = r * n + 2 * chip_now()
    row_a = row_b + 1

    def upper(at, size):
        return jnp.where(is_a, own[at : at + size], oth[at : at + size])

    def lower(at, size):
        return jnp.where(is_a, oth[at : at + size], own[at : at + size])

    def at_distance(side, row, d):
        found = jnp.zeros((bs, bs), F32)
        column = (row - d).astype(F32)
        for k in range(1, slots):
            col = side(col_at + 8 * k, 1)
            here = (col == column) & (col >= 0.0)
            found = jnp.where(here, side(k * bs, bs), found)
        return halves(found)

    return upper, lower, lambda d: at_distance(upper, row_a, d), lambda d: at_distance(lower, row_b, d)


def near_setup_kernel(r, n, slots, columns, own, oth, gh, gl, mh, ml, rt):
    bs = own.shape[1]
    half = columns // 2
    rhs_at, col_at, _, _, _ = packed_places(slots, bs, columns)
    upper, lower, upper_at, lower_at = blocks_of(r, n, slots, columns, own, oth)
    is_a = upper_here()
    da, db = halves(upper(slots * bs, bs)), halves(lower(slots * bs, bs))
    la1 = halves(upper(0, bs))
    lb1 = halves(jnp.where(lower(col_at, 1) >= 0.0, lower(0, bs), 0.0))
    w = dot3(da, la1)
    wh = halves(w)
    for place, pair in enumerate((da, db, la1, wh)):
        mh[place] = pair[0]
        ml[place] = pair[1]
    for j, (la, lb) in enumerate(((upper_at(2), lb1), (upper_at(3), lower_at(2)))):
        from_b = dot3(db, lb)
        put(gh, gl, 1, j, from_b)
        put(gh, gl, 0, j, dot3(da, la) - dot3(wh, halves(from_b)))
    ra, rb = upper(rhs_at, columns), lower(rhs_at, columns)
    rt[:, :bs] = jnp.where(is_a, ra[half:], ra[:half])
    rt[:, bs:] = jnp.where(is_a, rb[half:], rb[:half])


def far_setup_kernel(r, n, slots, columns, own, oth, mh, ml, fh, fl):
    _, _, upper_at, lower_at = blocks_of(r, n, slots, columns, own, oth)
    da, db, w = ((mh[k], ml[k]) for k in (0, 1, 3))
    for j, lb in enumerate((lower_at(3), lower_at(4))):
        from_b = dot3(db, lb)
        put(fh, fl, 1, j, from_b)
        from_a = -dot3(w, halves(from_b))
        if j == 0:
            from_a = from_a + dot3(da, upper_at(4))
        put(fh, fl, 0, j, from_a)


def place_of(lead, pairs, pieces):
    ahead = lax.rem(chip_now() - lead % pairs + pairs, pairs)
    piece = jnp.minimum(lax.div(ahead, 2), pieces - 1)
    return piece, lead + ahead


def choose(choices, pair, split, run):
    if len(choices) == 1:
        run(*choices[0])
        return

    @pl.when(pair < split)
    def _():
        run(*choices[0])

    @pl.when(pair >= split)
    def _():
        run(*choices[1])


def near_kernel(lead, pairs, pieces, split, ordered, received, has_near, *refs):
    refs = refs[ordered:]
    taken = refs[:received]
    outs = refs[-2:] if has_near else refs[-1:]
    refs = refs[received : -len(outs)]
    each = 3 if has_near else 1
    choices = [refs[i : i + each] for i in range(0, len(refs), each)]
    v_out = outs[0]
    width = v_out.shape[0]
    piece, pair = place_of(lead, pairs, pieces)
    rows = pl.ds(pl.multiple_of(piece * width, width), width)

    def run(rt, gh=None, gl=None):
        v = rt[rows, :]
        for x in taken:
            v = v - x[...]
        v_out[...] = v
        if has_near:
            outs[1][...] = dot3(halves(v), (gh[...], gl[...]))

    choose(choices, pair, split, run)


def far_kernel(lead, pairs, pieces, split, v_ref, *refs):
    out = refs[-1]
    refs = refs[:-1]
    _, pair = place_of(lead, pairs, pieces)

    def run(fh, fl):
        out[...] = dot3(halves(v_ref[...]), (fh[...], fl[...]))

    choose([refs[i : i + 2] for i in range(0, len(refs), 2)], pair, split, run)


def finish_kernel(slots, pairs, pieces, window, has_total, is_last, *refs):
    values = refs[:window]
    mh, ml, own, oth = refs[window : window + 4]
    refs = refs[window + 4 :]
    start = refs[0][...] if has_total else None
    keep, give, *outs = refs[1:] if has_total else refs
    chip, is_a = chip_now(), upper_here()
    bs = mh.shape[1]
    half = keep.shape[0]
    _, _, turnout_at, district_at, _ = packed_places(slots, bs, 2 * half)
    parts = []
    for m in range(pieces):
        v = values[pairs - 1 + 2 * m][...]
        for q in range(1, pairs):
            v = jnp.where(chip == q, values[pairs - 1 - q + 2 * m][...], v)
        parts.append(v)
    v = jnp.concatenate(parts, axis=0)

    def m(k):
        return mh[k], ml[k]

    xa = dot3(halves(v[:, :bs]), m(0))
    xb = dot3(halves(v[:, bs:] - dot3(halves(xa), m(2))), m(1))
    kept, given = jnp.where(is_a, xa, xb), jnp.where(is_a, xb, xa)
    keep[...] = kept
    give[...] = given
    names = lax.broadcasted_iota(jnp.int32, (NDIST, bs), 0).astype(F32)
    sums = jnp.zeros((NDIST, 2 * half), F32) if start is None else start
    for x, pack in ((kept, own), (given, oth)):
        weight = pack[turnout_at : turnout_at + 1]
        member = names == pack[district_at : district_at + 1]
        member = member.astype(F32).astype(B16)
        terms = jnp.concatenate([x * weight, jnp.broadcast_to(weight, (half, bs))], axis=0)
        for part in halves(terms):
            sums = sums + lax.dot_general(
                member, part, (((1,), (1,)), ((), ())), preferred_element_type=F32
            )
    if not is_last:
        outs[0][...] = sums
        return
    held = outs.pop()
    held[...] = sums
    rows = NDIST // pairs
    for by, part in enumerate(outs):
        to = lax.rem(chip + by, pairs)
        part[...] = held[pl.ds(pl.multiple_of(to * rows, rows), rows), :]


def add_kernel(*refs):
    mine, theirs = refs[-2:]
    total = refs[0][...]
    for part in refs[1:-2]:
        total = total + part[...]
    rows = mine.shape[0]
    is_a = upper_here()
    mine[...] = jnp.where(is_a, total[rows:], total[:rows])
    theirs[...] = jnp.where(is_a, total[:rows], total[rows:])


def mean_kernel(mine, got, out):
    half = out.shape[1] // 2
    own, oth = (x[:, :half] / x[:, half:] for x in (mine, got))
    is_a = upper_here()
    out[...] = jnp.concatenate(
        [jnp.where(is_a, oth, own), jnp.where(is_a, own, oth)], axis=1
    )


def field_kernel(rows_here, *refs):
    keeps = refs[:rows_here]
    gots = refs[rows_here : 2 * rows_here]
    out = refs[2 * rows_here]
    is_a = upper_here()
    for r in range(rows_here):
        top = jnp.where(is_a, gots[r][...], keeps[r][...])
        bottom = jnp.where(is_a, keeps[r][...], gots[r][...])
        out[r, 0] = jnp.concatenate([top, bottom], axis=0).T


def body(rhs, lower_blocks, col_index, diag_inverse, turnout, district_of):
    n = lax.axis_size("blk")
    pairs = n // 2
    pieces = 1
    rows_here, _, bs, columns = rhs.shape
    slots = lower_blocks.shape[2]
    half = columns // 2
    width = half // pieces
    count = rows_here * pairs
    packed_rows = packed_places(slots, bs, columns)[-1]
    wide = shaped(width, 2 * bs)
    square = shaped(2 * bs, 2 * bs, dtype=B16)

    def call(kernel, name, outs, operands, mib, flops=0, moved=0, **more):
        several = isinstance(outs, tuple)
        return pl.pallas_call(
            kernel,
            out_shape=outs,
            in_specs=more.pop("in_specs", [VMEM_SPEC] * len(operands)),
            out_specs=(VMEM_SPEC,) * len(outs) if several else VMEM_SPEC,
            compiler_params=params(mib),
            cost_estimate=cost(flops, moved),
            name=name,
            **more,
        )(*operands)

    def swap(x):
        return lax.ppermute(x, "blk", [(i, i ^ 1) for i in range(n)])

    def shift(x, by):
        return lax.ppermute(x, "blk", [(i, (i + 2 * by) % n) for i in range(n)])

    def pass_on(x, lead, by):
        perm = []
        for k in range(lead, lead + 2 * pieces, 2):
            if by <= k < count:
                sender, target = k % pairs, (k - by) % pairs
                perm += [(2 * sender + c, 2 * target + c) for c in range(2)]
        return lax.ppermute(x, "blk", perm)

    def pack(rows, turnout=turnout):
        return call(
            functools.partial(pack_kernel, rows),
            "pack",
            (shaped(packed_rows, bs),) * len(rows),
            (jnp.transpose(col_index, (2, 1, 0)), turnout, district_of, lower_blocks, diag_inverse, rhs),
            56,
            moved=8 * packed_rows * bs * len(rows),
            in_specs=[SMEM_SPEC, VMEM_SPEC, VMEM_SPEC] + [HBM_SPEC] * 3,
            scratch_shapes=[
                pltpu.VMEM((len(rows), bs, columns), F32),
                pltpu.SemaphoreType.DMA((len(rows) * (slots + 2),)),
            ],
        )

    def setup(r):
        args = (r, n, slots, columns)
        held = shaped(4, bs, bs, dtype=B16)
        gh, gl, mh, ml, rt = call(
            functools.partial(near_setup_kernel, *args),
            "near_setup",
            (square, square, held, held, shaped(half, 2 * bs)),
            packs[r],
            10,
            14 * 3 * bs**3,
            24 * bs * bs * 4,
        )
        fh, fl = call(
            functools.partial(far_setup_kernel, *args),
            "far_setup",
            (square, square),
            (*packs[r], mh, ml),
            10,
            10 * 3 * bs**3,
            24 * bs * bs * 4,
        )
        return gh, gl, mh, ml, rt, fh, fl

    def finish(r, values, total):
        first = count - 1 - (r * pairs + pairs - 1)
        window = values[first : first + pairs + 2 * (pieces - 1)]
        is_last = r == 0
        outs = (shaped(half, bs), shaped(half, bs))
        outs += (shaped(NDIST // pairs, columns),) * pairs if is_last else (shaped(NDIST, columns),)
        extra = () if total is None else (total,)
        return call(
            functools.partial(
                finish_kernel, slots, pairs, pieces, len(window), total is not None, is_last
            ),
            "finish",
            outs,
            (*window, *fixed[r][2:4], *packs[r], *extra),
            8,
            6 * 3 * half * bs * bs,
            16 * bs * bs,
            scratch_shapes=[pltpu.VMEM((NDIST, columns), F32)] if is_last else [],
        )

    top = rows_here - 1
    packs, fixed = {}, {}
    (own,) = pack((top,))
    packs[top] = (own, swap(own))
    later, _ = lax.optimization_barrier((turnout, own))
    packed = pack(tuple(range(top)), later) if top else ()
    for r in range(top - 1, -1, -1):
        packs[r] = (packed[r], swap(packed[r]))
    fixed[top] = setup(top)

    keeps, gots = {}, {}
    values = []
    ordered = ()
    total = near = far_now = far_next = None
    steps = count + 2 * (pieces - 1)
    for step in range(steps):
        lead = count - 1 - step
        low = max(lead, 0) // pairs
        high = min(lead + 2 * (pieces - 1), count - 1) // pairs
        rows = range(low, high + 1)
        taken = [x for x in (far_now, near) if x is not None]
        has_near = step + 1 < steps
        has_far = step + 2 < steps
        operands = []
        for r in rows:
            gh, gl, _, _, rt, _, _ = fixed[r]
            operands += [rt, gh, gl] if has_near else [rt]
        place = (lead, pairs, pieces, high * pairs)
        v, *near_out = call(
            functools.partial(near_kernel, *place, len(ordered), len(taken), has_near),
            "near_terms",
            (wide, wide) if has_near else (wide,),
            (*ordered, *taken, *operands),
            4,
            6 * width * 4 * bs * bs,
            6 * width * bs * 4,
        )
        values.append(v)
        near = pass_on(near_out[0], lead, 1) if has_near else None
        far_now, far_next, ordered = far_next, None, ()
        if has_far:
            operands = [x for r in rows for x in fixed[r][5:]]
            far_out = call(
                functools.partial(far_kernel, *place),
                "far_terms",
                wide,
                (v, *operands),
                4,
                6 * width * 4 * bs * bs,
                6 * width * bs * 4,
            )
            ordered = (far_out,)
            r, chip = lead // pairs, lead % pairs
            if chip == pairs - 1 and r > 0:
                fixed[r - 1] = setup(r - 1)
            far_next = pass_on(far_out, lead, 2)
        done = lead + 2 * (pieces - 1)
        if done % pairs == 0 and 0 < done // pairs <= top:
            r = done // pairs
            keeps[r], give, total = finish(r, values, total)
            gots[r] = swap(give)
            near, total = lax.optimization_barrier((near, total))

    keeps[0], give, *parts = finish(0, values, total)
    gots[0] = swap(give)
    parts = [parts[0]] + [shift(parts[by], by) for by in range(1, pairs)]
    order = range(rows_here)
    field = call(
        functools.partial(field_kernel, rows_here),
        "field",
        shaped(rows_here, 1, bs, columns),
        (*[keeps[r] for r in order], *[gots[r] for r in order]),
        4,
        0,
        8 * rows_here * bs * columns,
    )
    parts, field = lax.optimization_barrier((parts, field))
    held = shaped(NDIST // n, columns)
    mine, theirs = call(add_kernel, "district_add", (held, held), tuple(parts), 4)
    mean = call(mean_kernel, "district_mean", held, (mine, swap(theirs)), 4)
    return field, mean


def solution(mesh):
    placed = (
        P(None, "blk", None, "sims"),
        P(None, "blk", None, None, None),
        P(None, "blk", None),
        P(None, "blk", None, None),
        P(None, "blk", None),
        P(None, "blk", None),
    )
    return jax.shard_map(
        body,
        mesh=mesh,
        in_specs=placed,
        out_specs=(P(None, "blk", None, "sims"), P("blk", "sims")),
        check_vma=False,
    )
```

profile of v0, /device:TPU:0, one launch (start us, length us, event | category | flops | bytes accessed | tf_op | source)
XLA Modules:
  0.0 110.7 jit_solution(9159081618552174491)
XLA Ops:
  0.6 3.1 %pack.2.own.refs_6_ = f32[1192,256]{1,0:T(8,128)} custom-call(s32[3,1,4]{2,1,0:T(1,128)} %bitcast.1, f32[4,1,256]{2,1,0:T(1,128)} %turnout.2, s32[4,1,256]{2,1,0:T(1,128)} %district.3, f32[4,1,3,256,256]{4,3,2,1,0:T(8,128)} %l_ref.3, f32[4,1,256,256]{3,2,1,0:T(8,128)} %d_ref.3, f32[4,1,256,128]{3,2,1,0:T(8,128)} %r_ref.3), custom_call_target="tpu_custom_call" | custom-call | bytes 2441216 | tf_op jit(solution)/shard_map/pack/pallas_call | solution.py:310
  4.2 4.7 %pack.3 = (f32[1192,256]{1,0:T(8,128)}, f32[1192,256]{1,0:T(8,128)}, f32[1192,256]{1,0:T(8,128)}) custom-call(s32[3,1,4]{2,1,0:T(1,128)} %bitcast.2, f32[4,1,256]{2,1,0:T(1,128)} %turnout.2, s32[4,1,256]{2,1,0:T(1,128)} %district.3, f32[4,1,3,256,256]{4,3,2,1,0:T(8,128)} %l_ref.3, f32[4,1,256,256]{3,2,1,0:T(8,128)} %d_ref.3, f32[4,1,256,128]{3,2,1,0:T(8,128)} %r_ref.3), custom_call_target="tpu_custom_call" | custom-call | bytes 7323648 | tf_op jit(solution)/shard_map/pack/pallas_call | solution.py:310
  9.6 1.2 %near_setup.4 = (bf16[512,512]{1,0:T(8,128)(2,1)S(1)}, bf16[512,512]{1,0:T(8,128)(2,1)S(1)}, bf16[4,256,256]{2,1,0:T(8,128)(2,1)S(1)}, bf16[4,256,256]{2,1,0:T(8,128)(2,1)S(1)}, f32[64,512]{1,0:T(8,128)S(1)}) custom-call(f32[1192,256]{1,0:T(8,128)S(1)} %copy-done, f32[1192,256]{1,0:T(8,128)S(1)} %collective-permute-done.oth.refs_7_), custom_call_target="tpu_custom_call" | custom-call | flops 704643072 | bytes 6291456 | tf_op jit(solution)/shard_map/near_setup/pallas_call | solution.py:310
  11.0 0.7 collective-permute-start.1
  11.7 1.2 %far_setup.4 = (bf16[512,512]{1,0:T(8,128)(2,1)S(1)}, bf16[512,512]{1,0:T(8,128)(2,1)S(1)}) custom-call(f32[1192,256]{1,0:T(8,128)S(1)} %copy-done, f32[1192,256]{1,0:T(8,128)S(1)} %collective-permute-done.oth.refs_7_, bf16[4,256,256]{2,1,0:T(8,128)(2,1)S(1)} %get-tuple-element.96.mh.refs_4_, bf16[4,256,256]{2,1,0:T(8,128)(2,1)S(1)} %get-tuple-element.97.ml.refs_5_), custom_call_target="tpu_custom_call" | custom-call | flops 503316480 | bytes 6291456 | tf_op jit(solution)/shard_map/far_setup/pallas_call | solution.py:310
  13.2 0.7 collective-permute-start.2
  14.2 0.7 collective-permute-start.3
  15.2 1.4 %collective-permute-start.4 = (f32[64,512]{1,0:T(8,128)S(1)}, f32[64,512]{1,0:T(8,128)S(1)}, u32[]{:S(2)}, u32[]{:S(2)}) collective-permute-start(f32[64,512]{1,0:T(8,128)S(1)} %far_terms.15.refs_0_), channel_id=1, source_target_pairs={{16,0},{20,4},{17,1},{21,5},{18,2},{22,6},{19,3},{23,7}} | collective-permute-start | bytes 393224 | tf_op jit(solution)/shard_map/ppermute | solution.py:333
  16.9 1.3 %collective-permute-start.5 = (f32[64,512]{1,0:T(8,128)S(1)}, f32[64,512]{1,0:T(8,128)S(1)}, u32[]{:S(2)}, u32[]{:S(2)}) collective-permute-start(f32[64,512]{1,0:T(8,128)S(1)} %get-tuple-element.104), channel_id=1, source_target_pairs={{8,0},{12,4},{9,1},{13,5},{10,2},{14,6},{11,3},{15,7}} | collective-permute-start | bytes 393224 | tf_op jit(solution)/shard_map/ppermute | solution.py:333
  18.8 9.1 %collective-permute-done.4.refs_1_ = f32[64,512]{1,0:T(8,128)S(1)} collective-permute-done((f32[64,512]{1,0:T(8,128)S(1)}, f32[64,512]{1,0:T(8,128)S(1)}, u32[]{:S(2)}, u32[]{:S(2)}) %collective-permute-start.4) | collective-permute-done | bytes 131104 | tf_op jit(solution)/shard_map/ppermute | solution.py:333
  27.9 4.2 %collective-permute-done.5.refs_2_ = f32[64,512]{1,0:T(8,128)S(1)} collective-permute-done((f32[64,512]{1,0:T(8,128)S(1)}, f32[64,512]{1,0:T(8,128)S(1)}, u32[]{:S(2)}, u32[]{:S(2)}) %collective-permute-start.5) | collective-permute-done | bytes 131104 | tf_op jit(solution)/shard_map/ppermute | solution.py:333
  32.4 1.3 %collective-permute-start.7 = (f32[64,512]{1,0:T(8,128)S(1)}, f32[64,512]{1,0:T(8,128)S(1)}, u32[]{:S(2)}, u32[]{:S(2)}) collective-permute-start(f32[64,512]{1,0:T(8,128)S(1)} %get-tuple-element.106), channel_id=1, source_target_pairs={{0,24},{4,28},{1,25},{5,29},{2,26},{6,30},{3,27},{7,31}} | collective-permute-start | bytes 393224 | tf_op jit(solution)/shard_map/ppermute | solution.py:333
  33.7 0.7 collective-permute-start.6
  34.4 1.2 %near_setup.5 = (bf16[512,512]{1,0:T(8,128)(2,1)S(1)}, bf16[512,512]{1,0:T(8,128)(2,1)S(1)}, bf16[4,256,256]{2,1,0:T(8,128)(2,1)S(1)}, bf16[4,256,256]{2,1,0:T(8,128)(2,1)S(1)}, f32[64,512]{1,0:T(8,128)S(1)}) custom-call(f32[1192,256]{1,0:T(8,128)S(1)} %copy-done.3, f32[1192,256]{1,0:T(8,128)S(1)} %collective-permute-done.8.oth.refs_7_), custom_call_target="tpu_custom_call" | custom-call | flops 704643072 | bytes 6291456 | tf_op jit(solution)/shard_map/near_setup/pallas_call | solution.py:310
  35.9 1.3 %collective-permute-start.9 = (f32[64,512]{1,0:T(8,128)S(1)}, f32[64,512]{1,0:T(8,128)S(1)}, u32[]{:S(2)}, u32[]{:S(2)}) collective-permute-start(f32[64,512]{1,0:T(8,128)S(1)} %far_terms.17.refs_0_), channel_id=1, source_target_pairs={{0,16},{4,20},{1,17},{5,21},{2,18},{6,22},{3,19},{7,23}} | collective-permute-start | bytes 393224 | tf_op jit(solution)/shard_map/ppermute | solution.py:333
  37.2 0.9 finish.4
  39.1 1.2 %far_setup.5 = (bf16[512,512]{1,0:T(8,128)(2,1)S(1)}, bf16[512,512]{1,0:T(8,128)(2,1)S(1)}) custom-call(f32[1192,256]{1,0:T(8,128)S(1)} %copy-done.3, f32[1192,256]{1,0:T(8,128)S(1)} %collective-permute-done.8.oth.refs_7_, bf16[4,256,256]{2,1,0:T(8,128)(2,1)S(1)} %get-tuple-element.115.mh.refs_4_, bf16[4,256,256]{2,1,0:T(8,128)(2,1)S(1)} %get-tuple-element.116.ml.refs_5_), custom_call_target="tpu_custom_call" | custom-call | flops 503316480 | bytes 6291456 | tf_op jit(solution)/shard_map/far_setup/pallas_call | solution.py:310
  41.6 0.7 collective-permute-start.12
  42.5 1.3 %collective-permute-start.13 = (f32[64,512]{1,0:T(8,128)S(1)}, f32[64,512]{1,0:T(8,128)S(1)}, u32[]{:S(2)}, u32[]{:S(2)}) collective-permute-start(f32[64,512]{1,0:T(8,128)S(1)} %far_terms.19.refs_0_), channel_id=1, source_target_pairs={{16,0},{20,4},{17,1},{21,5},{18,2},{22,6},{19,3},{23,7}} | collective-permute-start | bytes 393224 | tf_op jit(solution)/shard_map/ppermute | solution.py:333
  44.1 1.3 %collective-permute-start.14 = (f32[64,512]{1,0:T(8,128)S(1)}, f32[64,512]{1,0:T(8,128)S(1)}, u32[]{:S(2)}, u32[]{:S(2)}) collective-permute-start(f32[64,512]{1,0:T(8,128)S(1)} %get-tuple-element.123), channel_id=1, source_target_pairs={{8,0},{12,4},{9,1},{13,5},{10,2},{14,6},{11,3},{15,7}} | collective-permute-start | bytes 393224 | tf_op jit(solution)/shard_map/ppermute | solution.py:333
  45.7 5.7 %collective-permute-done.13.refs_1_ = f32[64,512]{1,0:T(8,128)S(1)} collective-permute-done((f32[64,512]{1,0:T(8,128)S(1)}, f32[64,512]{1,0:T(8,128)S(1)}, u32[]{:S(2)}, u32[]{:S(2)}) %collective-permute-start.13) | collective-permute-done | bytes 131104 | tf_op jit(solution)/shard_map/ppermute | solution.py:333
  51.5 4.4 %collective-permute-done.14.refs_2_ = f32[64,512]{1,0:T(8,128)S(1)} collective-permute-done((f32[64,512]{1,0:T(8,128)S(1)}, f32[64,512]{1,0:T(8,128)S(1)}, u32[]{:S(2)}, u32[]{:S(2)}) %collective-permute-start.14) | collective-permute-done | bytes 131104 | tf_op jit(solution)/shard_map/ppermute | solution.py:333
  56.2 1.3 %collective-permute-start.16 = (f32[64,512]{1,0:T(8,128)S(1)}, f32[64,512]{1,0:T(8,128)S(1)}, u32[]{:S(2)}, u32[]{:S(2)}) collective-permute-start(f32[64,512]{1,0:T(8,128)S(1)} %get-tuple-element.125), channel_id=1, source_target_pairs={{0,24},{4,28},{1,25},{5,29},{2,26},{6,30},{3,27},{7,31}} | collective-permute-start | bytes 393224 | tf_op jit(solution)/shard_map/ppermute | solution.py:333
  58.2 1.2 %near_setup.6 = (bf16[512,512]{1,0:T(8,128)(2,1)S(1)}, bf16[512,512]{1,0:T(8,128)(2,1)S(1)}, bf16[4,256,256]{2,1,0:T(8,128)(2,1)S(1)}, bf16[4,256,256]{2,1,0:T(8,128)(2,1)S(1)}, f32[64,512]{1,0:T(8,128)S(1)}) custom-call(f32[1192,256]{1,0:T(8,128)S(1)} %copy-done.2, f32[1192,256]{1,0:T(8,128)S(1)} %collective-permute-done.17.oth.refs_7_), custom_call_target="tpu_custom_call" | custom-call | flops 704643072 | bytes 6291456 | tf_op jit(solution)/shard_map/near_setup/pallas_call | solution.py:310
  59.7 1.3 %collective-permute-start.18 = (f32[64,512]{1,0:T(8,128)S(1)}, f32[64,512]{1,0:T(8,128)S(1)}, u32[]{:S(2)}, u32[]{:S(2)}) collective-permute-start(f32[64,512]{1,0:T(8,128)S(1)} %far_terms.21.refs_0_), channel_id=1, source_target_pairs={{0,16},{4,20},{1,17},{5,21},{2,18},{6,22},{3,19},{7,23}} | collective-permute-start | bytes 393224 | tf_op jit(solution)/shard_map/ppermute | solution.py:333
  61.0 0.9 finish.5
  62.8 1.2 %far_setup.6 = (bf16[512,512]{1,0:T(8,128)(2,1)S(1)}, bf16[512,512]{1,0:T(8,128)(2,1)S(1)}) custom-call(f32[1192,256]{1,0:T(8,128)S(1)} %copy-done.2, f32[1192,256]{1,0:T(8,128)S(1)} %collective-permute-done.17.oth.refs_7_, bf16[4,256,256]{2,1,0:T(8,128)(2,1)S(1)} %get-tuple-element.134.mh.refs_4_, bf16[4,256,256]{2,1,0:T(8,128)(2,1)S(1)} %get-tuple-element.135.ml.refs_5_), custom_call_target="tpu_custom_call" | custom-call | flops 503316480 | bytes 6291456 | tf_op jit(solution)/shard_map/far_setup/pallas_call | solution.py:310
  66.3 1.3 %collective-permute-start.22 = (f32[64,512]{1,0:T(8,128)S(1)}, f32[64,512]{1,0:T(8,128)S(1)}, u32[]{:S(2)}, u32[]{:S(2)}) collective-permute-start(f32[64,512]{1,0:T(8,128)S(1)} %far_terms.23.refs_0_), channel_id=1, source_target_pairs={{16,0},{20,4},{17,1},{21,5},{18,2},{22,6},{19,3},{23,7}} | collective-permute-start | bytes 393224 | tf_op jit(solution)/shard_map/ppermute | solution.py:333
  67.9 1.3 %collective-permute-start.23 = (f32[64,512]{1,0:T(8,128)S(1)}, f32[64,512]{1,0:T(8,128)S(1)}, u32[]{:S(2)}, u32[]{:S(2)}) collective-permute-start(f32[64,512]{1,0:T(8,128)S(1)} %get-tuple-element.142), channel_id=1, source_target_pairs={{8,0},{12,4},{9,1},{13,5},{10,2},{14,6},{11,3},{15,7}} | collective-permute-start | bytes 393224 | tf_op jit(solution)/shard_map/ppermute | solution.py:333
  69.5 5.2 %collective-permute-done.22.refs_1_ = f32[64,512]{1,0:T(8,128)S(1)} collective-permute-done((f32[64,512]{1,0:T(8,128)S(1)}, f32[64,512]{1,0:T(8,128)S(1)}, u32[]{:S(2)}, u32[]{:S(2)}) %collective-permute-start.22) | collective-permute-done | bytes 131104 | tf_op jit(solution)/shard_map/ppermute | solution.py:333
  74.7 4.4 %collective-permute-done.23.refs_2_ = f32[64,512]{1,0:T(8,128)S(1)} collective-permute-done((f32[64,512]{1,0:T(8,128)S(1)}, f32[64,512]{1,0:T(8,128)S(1)}, u32[]{:S(2)}, u32[]{:S(2)}) %collective-permute-start.23) | collective-permute-done | bytes 131104 | tf_op jit(solution)/shard_map/ppermute | solution.py:333
  79.4 1.3 %collective-permute-start.25 = (f32[64,512]{1,0:T(8,128)S(1)}, f32[64,512]{1,0:T(8,128)S(1)}, u32[]{:S(2)}, u32[]{:S(2)}) collective-permute-start(f32[64,512]{1,0:T(8,128)S(1)} %get-tuple-element.144), channel_id=1, source_target_pairs={{0,24},{4,28},{1,25},{5,29},{2,26},{6,30},{3,27},{7,31}} | collective-permute-start | bytes 393224 | tf_op jit(solution)/shard_map/ppermute | solution.py:333
  80.7 0.8 collective-permute-start.24
  81.5 1.2 %near_setup.7 = (bf16[512,512]{1,0:T(8,128)(2,1)S(1)}, bf16[512,512]{1,0:T(8,128)(2,1)S(1)}, bf16[4,256,256]{2,1,0:T(8,128)(2,1)S(1)}, bf16[4,256,256]{2,1,0:T(8,128)(2,1)S(1)}, f32[64,512]{1,0:T(8,128)S(1)}) custom-call(f32[1192,256]{1,0:T(8,128)S(1)} %copy-done.1, f32[1192,256]{1,0:T(8,128)S(1)} %collective-permute-done.26.oth.refs_7_), custom_call_target="tpu_custom_call" | custom-call | flops 704643072 | bytes 6291456 | tf_op jit(solution)/shard_map/near_setup/pallas_call | solution.py:310
  83.0 1.3 %collective-permute-start.27 = (f32[64,512]{1,0:T(8,128)S(1)}, f32[64,512]{1,0:T(8,128)S(1)}, u32[]{:S(2)}, u32[]{:S(2)}) collective-permute-start(f32[64,512]{1,0:T(8,128)S(1)} %far_terms.25.refs_0_), channel_id=1, source_target_pairs={{0,16},{4,20},{1,17},{5,21},{2,18},{6,22},{3,19},{7,23}} | collective-permute-start | bytes 393224 | tf_op jit(solution)/shard_map/ppermute | solution.py:333
  84.3 0.9 finish.6
  86.2 1.2 %far_setup.7 = (bf16[512,512]{1,0:T(8,128)(2,1)S(1)}, bf16[512,512]{1,0:T(8,128)(2,1)S(1)}) custom-call(f32[1192,256]{1,0:T(8,128)S(1)} %copy-done.1, f32[1192,256]{1,0:T(8,128)S(1)} %collective-permute-done.26.oth.refs_7_, bf16[4,256,256]{2,1,0:T(8,128)(2,1)S(1)} %get-tuple-element.153.mh.refs_4_, bf16[4,256,256]{2,1,0:T(8,128)(2,1)S(1)} %get-tuple-element.154.ml.refs_5_), custom_call_target="tpu_custom_call" | custom-call | flops 503316480 | bytes 6291456 | tf_op jit(solution)/shard_map/far_setup/pallas_call | solution.py:310
  87.7 0.7 collective-permute-start.29
  89.6 1.3 %collective-permute-start.31 = (f32[64,512]{1,0:T(8,128)S(1)}, f32[64,512]{1,0:T(8,128)S(1)}, u32[]{:S(2)}, u32[]{:S(2)}) collective-permute-start(f32[64,512]{1,0:T(8,128)S(1)} %far_terms.27.refs_0_), channel_id=1, source_target_pairs={{16,0},{20,4},{17,1},{21,5},{18,2},{22,6},{19,3},{23,7}} | collective-permute-start | bytes 393224 | tf_op jit(solution)/shard_map/ppermute | solution.py:333
  91.3 1.3 %collective-permute-start.32 = (f32[64,512]{1,0:T(8,128)S(1)}, f32[64,512]{1,0:T(8,128)S(1)}, u32[]{:S(2)}, u32[]{:S(2)}) collective-permute-start(f32[64,512]{1,0:T(8,128)S(1)} %get-tuple-element.161), channel_id=1, source_target_pairs={{8,0},{12,4},{9,1},{13,5},{10,2},{14,6},{11,3},{15,7}} | collective-permute-start | bytes 393224 | tf_op jit(solution)/shard_map/ppermute | solution.py:333
  93.2 4.7 %collective-permute-done.31.refs_0_ = f32[64,512]{1,0:T(8,128)S(1)} collective-permute-done((f32[64,512]{1,0:T(8,128)S(1)}, f32[64,512]{1,0:T(8,128)S(1)}, u32[]{:S(2)}, u32[]{:S(2)}) %collective-permute-start.31) | collective-permute-done | bytes 131104 | tf_op jit(solution)/shard_map/ppermute | solution.py:333
  97.9 4.4 %collective-permute-done.32.refs_1_ = f32[64,512]{1,0:T(8,128)S(1)} collective-permute-done((f32[64,512]{1,0:T(8,128)S(1)}, f32[64,512]{1,0:T(8,128)S(1)}, u32[]{:S(2)}, u32[]{:S(2)}) %collective-permute-start.32) | collective-permute-done | bytes 131104 | tf_op jit(solution)/shard_map/ppermute | solution.py:333
  102.3 0.9 finish.7
  103.4 2.9 %collective-permute-start.35 = (f32[64,128]{1,0:T(8,128)S(1)}, f32[64,128]{1,0:T(8,128)S(1)}, u32[]{:S(2)}, u32[]{:S(2)}) collective-permute-start(f32[64,128]{1,0:T(8,128)S(1)} %get-tuple-element.166), channel_id=1, source_target_pairs={{0,24},{4,28},{8,0},{12,4},{16,8},{20,12},{24,16},{28,20},{1,25},{... | collective-permute-start | bytes 98312 | tf_op jit(solution)/shard_map/ppermute | solution.py:325
  106.3 1.0 field.1
  107.3 1.0 collective-permute-done.33.refs_1_
  108.8 1.2 %collective-permute-done.40.got = f32[32,128]{1,0:T(8,128)S(1)} collective-permute-done((f32[32,128]{1,0:T(8,128)S(1)}, f32[32,128]{1,0:T(8,128)S(1)}, u32[]{:S(2)}, u32[]{:S(2)}) %collective-permute-start.40) | collective-permute-done | bytes 16416 | tf_op jit(solution)/shard_map/ppermute | solution.py:322
  110.0 0.8 district_mean.1
  (89 shorter events, 16.4 us)
Async XLA Ops:
  3.7 5.8 %copy-start = (f32[1192,256]{1,0:T(8,128)S(1)}, f32[1192,256]{1,0:T(8,128)}, u32[]{:S(2)}) copy-start(f32[1192,256]{1,0:T(8,128)} %pack.2.own.refs_6_) | copy-start | bytes 3661828
  3.7 5.8 %collective-permute-start = (f32[1192,256]{1,0:T(8,128)}, f32[1192,256]{1,0:T(8,128)S(1)}, u32[]{:S(2)}, u32[]{:S(2)}) collective-permute-start(f32[1192,256]{1,0:T(8,128)} %pack.2.own.refs_6_), channel_id=1, source_target_pairs={{0,4},{4,0},{8,12},{12,8},{16,20},{20,16},{24,28},{28,24},{1,5},{5... | collective-permute-start | bytes 3661832 | tf_op jit(solution)/shard_map/ppermute | solution.py:322
  9.0 25.4 %collective-permute-start.8 = (f32[1192,256]{1,0:T(8,128)}, f32[1192,256]{1,0:T(8,128)S(1)}, u32[]{:S(2)}, u32[]{:S(2)}) collective-permute-start(f32[1192,256]{1,0:T(8,128)} %get-tuple-element.110.own.refs_6_), channel_id=1, source_target_pairs={{0,4},{4,0},{8,12},{12,8},{16,20},{20,16},{24,28},{28,24},{1,5},{5... | collective-permute-start | bytes 3661832 | tf_op jit(solution)/shard_map/ppermute | solution.py:322
  9.2 48.9 %collective-permute-start.17 = (f32[1192,256]{1,0:T(8,128)}, f32[1192,256]{1,0:T(8,128)S(1)}, u32[]{:S(2)}, u32[]{:S(2)}) collective-permute-start(f32[1192,256]{1,0:T(8,128)} %get-tuple-element.129.own.refs_6_), channel_id=1, source_target_pairs={{0,4},{4,0},{8,12},{12,8},{16,20},{20,16},{24,28},{28,24},{1,5},{5... | collective-permute-start | bytes 3661832 | tf_op jit(solution)/shard_map/ppermute | solution.py:322
  11.0 2.9 %collective-permute-start.1 = (f32[64,512]{1,0:T(8,128)S(1)}, f32[64,512]{1,0:T(8,128)S(1)}, u32[]{:S(2)}, u32[]{:S(2)}) collective-permute-start(f32[64,512]{1,0:T(8,128)S(1)} %get-tuple-element.100), channel_id=1, source_target_pairs={{24,16},{28,20},{25,17},{29,21},{26,18},{30,22},{27,19},{31,23}} | collective-permute-start | bytes 393224 | tf_op jit(solution)/shard_map/ppermute | solution.py:333
  13.2 3.4 %collective-permute-start.2 = (f32[64,512]{1,0:T(8,128)S(1)}, f32[64,512]{1,0:T(8,128)S(1)}, u32[]{:S(2)}, u32[]{:S(2)}) collective-permute-start(f32[64,512]{1,0:T(8,128)S(1)} %far_terms.14.refs_0_), channel_id=1, source_target_pairs={{24,8},{28,12},{25,9},{29,13},{26,10},{30,14},{27,11},{31,15}} | collective-permute-start | bytes 393224 | tf_op jit(solution)/shard_map/ppermute | solution.py:333
  14.2 2.4 %collective-permute-start.3 = (f32[64,512]{1,0:T(8,128)S(1)}, f32[64,512]{1,0:T(8,128)S(1)}, u32[]{:S(2)}, u32[]{:S(2)}) collective-permute-start(f32[64,512]{1,0:T(8,128)S(1)} %get-tuple-element.102), channel_id=1, source_target_pairs={{16,8},{20,12},{17,9},{21,13},{18,10},{22,14},{19,11},{23,15}} | collective-permute-start | bytes 393224 | tf_op jit(solution)/shard_map/ppermute | solution.py:333
  14.9 3.4 %copy-start.1 = (f32[1192,256]{1,0:T(8,128)S(1)}, f32[1192,256]{1,0:T(8,128)}, u32[]{:S(2)}) copy-start(f32[1192,256]{1,0:T(8,128)} %get-tuple-element.148.own.refs_6_) | copy-start | bytes 3661828
  15.2 12.7 %collective-permute-start.4 = (f32[64,512]{1,0:T(8,128)S(1)}, f32[64,512]{1,0:T(8,128)S(1)}, u32[]{:S(2)}, u32[]{:S(2)}) collective-permute-start(f32[64,512]{1,0:T(8,128)S(1)} %far_terms.15.refs_0_), channel_id=1, source_target_pairs={{16,0},{20,4},{17,1},{21,5},{18,2},{22,6},{19,3},{23,7}} | collective-permute-start | bytes 393224 | tf_op jit(solution)/shard_map/ppermute | solution.py:333
  16.9 15.2 %collective-permute-start.5 = (f32[64,512]{1,0:T(8,128)S(1)}, f32[64,512]{1,0:T(8,128)S(1)}, u32[]{:S(2)}, u32[]{:S(2)}) collective-permute-start(f32[64,512]{1,0:T(8,128)S(1)} %get-tuple-element.104), channel_id=1, source_target_pairs={{8,0},{12,4},{9,1},{13,5},{10,2},{14,6},{11,3},{15,7}} | collective-permute-start | bytes 393224 | tf_op jit(solution)/shard_map/ppermute | solution.py:333
  18.3 63.3 %collective-permute-start.26 = (f32[1192,256]{1,0:T(8,128)S(1)}, f32[1192,256]{1,0:T(8,128)S(1)}, u32[]{:S(2)}, u32[]{:S(2)}) collective-permute-start(f32[1192,256]{1,0:T(8,128)S(1)} %copy-done.1), channel_id=1, source_target_pairs={{0,4},{4,0},{8,12},{12,8},{16,20},{20,16},{24,28},{28,24},{1,5},{5... | collective-permute-start | bytes 3661832 | tf_op jit(solution)/shard_map/ppermute | solution.py:322
  18.5 15.9 %copy-start.3 = (f32[1192,256]{1,0:T(8,128)S(1)}, f32[1192,256]{1,0:T(8,128)}, u32[]{:S(2)}) copy-start(f32[1192,256]{1,0:T(8,128)} %get-tuple-element.110.own.refs_6_) | copy-start | bytes 3661828
  32.4 5.7 %collective-permute-start.7 = (f32[64,512]{1,0:T(8,128)S(1)}, f32[64,512]{1,0:T(8,128)S(1)}, u32[]{:S(2)}, u32[]{:S(2)}) collective-permute-start(f32[64,512]{1,0:T(8,128)S(1)} %get-tuple-element.106), channel_id=1, source_target_pairs={{0,24},{4,28},{1,25},{5,29},{2,26},{6,30},{3,27},{7,31}} | collective-permute-start | bytes 393224 | tf_op jit(solution)/shard_map/ppermute | solution.py:333
  33.7 4.4 %collective-permute-start.6 = (f32[64,512]{1,0:T(8,128)S(1)}, f32[64,512]{1,0:T(8,128)S(1)}, u32[]{:S(2)}, u32[]{:S(2)}) collective-permute-start(f32[64,512]{1,0:T(8,128)S(1)} %far_terms.16.refs_0_), channel_id=1, source_target_pairs={{8,24},{12,28},{9,25},{13,29},{10,26},{14,30},{11,27},{15,31}} | collective-permute-start | bytes 393224 | tf_op jit(solution)/shard_map/ppermute | solution.py:333
  35.9 5.3 %collective-permute-start.9 = (f32[64,512]{1,0:T(8,128)S(1)}, f32[64,512]{1,0:T(8,128)S(1)}, u32[]{:S(2)}, u32[]{:S(2)}) collective-permute-start(f32[64,512]{1,0:T(8,128)S(1)} %far_terms.17.refs_0_), channel_id=1, source_target_pairs={{0,16},{4,20},{1,17},{5,21},{2,18},{6,22},{3,19},{7,23}} | collective-permute-start | bytes 393224 | tf_op jit(solution)/shard_map/ppermute | solution.py:333
  38.4 2.8 %collective-permute-start.10 = (f32[64,512]{1,0:T(8,128)S(1)}, f32[64,512]{1,0:T(8,128)S(1)}, u32[]{:S(2)}, u32[]{:S(2)}) collective-permute-start(f32[64,512]{1,0:T(8,128)S(1)} %get-tuple-element.119), channel_id=1, source_target_pairs={{24,16},{28,20},{25,17},{29,21},{26,18},{30,22},{27,19},{31,23}} | collective-permute-start | bytes 393224 | tf_op jit(solution)/shard_map/ppermute | solution.py:333
  40.6 3.3 %collective-permute-start.11 = (f32[64,512]{1,0:T(8,128)S(1)}, f32[64,512]{1,0:T(8,128)S(1)}, u32[]{:S(2)}, u32[]{:S(2)}) collective-permute-start(f32[64,512]{1,0:T(8,128)S(1)} %far_terms.18.refs_0_), channel_id=1, source_target_pairs={{24,8},{28,12},{25,9},{29,13},{26,10},{30,14},{27,11},{31,15}} | collective-permute-start | bytes 393224 | tf_op jit(solution)/shard_map/ppermute | solution.py:333
  41.6 2.3 %collective-permute-start.12 = (f32[64,512]{1,0:T(8,128)S(1)}, f32[64,512]{1,0:T(8,128)S(1)}, u32[]{:S(2)}, u32[]{:S(2)}) collective-permute-start(f32[64,512]{1,0:T(8,128)S(1)} %get-tuple-element.121), channel_id=1, source_target_pairs={{16,8},{20,12},{17,9},{21,13},{18,10},{22,14},{19,11},{23,15}} | collective-permute-start | bytes 393224 | tf_op jit(solution)/shard_map/ppermute | solution.py:333
  42.5 9.0 %collective-permute-start.13 = (f32[64,512]{1,0:T(8,128)S(1)}, f32[64,512]{1,0:T(8,128)S(1)}, u32[]{:S(2)}, u32[]{:S(2)}) collective-permute-start(f32[64,512]{1,0:T(8,128)S(1)} %far_terms.19.refs_0_), channel_id=1, source_target_pairs={{16,0},{20,4},{17,1},{21,5},{18,2},{22,6},{19,3},{23,7}} | collective-permute-start | bytes 393224 | tf_op jit(solution)/shard_map/ppermute | solution.py:333
  44.1 11.7 %collective-permute-start.14 = (f32[64,512]{1,0:T(8,128)S(1)}, f32[64,512]{1,0:T(8,128)S(1)}, u32[]{:S(2)}, u32[]{:S(2)}) collective-permute-start(f32[64,512]{1,0:T(8,128)S(1)} %get-tuple-element.123), channel_id=1, source_target_pairs={{8,0},{12,4},{9,1},{13,5},{10,2},{14,6},{11,3},{15,7}} | collective-permute-start | bytes 393224 | tf_op jit(solution)/shard_map/ppermute | solution.py:333
  45.4 12.7 %copy-start.2 = (f32[1192,256]{1,0:T(8,128)S(1)}, f32[1192,256]{1,0:T(8,128)}, u32[]{:S(2)}) copy-start(f32[1192,256]{1,0:T(8,128)} %get-tuple-element.129.own.refs_6_) | copy-start | bytes 3661828
  56.2 5.7 %collective-permute-start.16 = (f32[64,512]{1,0:T(8,128)S(1)}, f32[64,512]{1,0:T(8,128)S(1)}, u32[]{:S(2)}, u32[]{:S(2)}) collective-permute-start(f32[64,512]{1,0:T(8,128)S(1)} %get-tuple-element.125), channel_id=1, source_target_pairs={{0,24},{4,28},{1,25},{5,29},{2,26},{6,30},{3,27},{7,31}} | collective-permute-start | bytes 393224 | tf_op jit(solution)/shard_map/ppermute | solution.py:333
  57.5 4.4 %collective-permute-start.15 = (f32[64,512]{1,0:T(8,128)S(1)}, f32[64,512]{1,0:T(8,128)S(1)}, u32[]{:S(2)}, u32[]{:S(2)}) collective-permute-start(f32[64,512]{1,0:T(8,128)S(1)} %far_terms.20.refs_0_), channel_id=1, source_target_pairs={{8,24},{12,28},{9,25},{13,29},{10,26},{14,30},{11,27},{15,31}} | collective-permute-start | bytes 393224 | tf_op jit(solution)/shard_map/ppermute | solution.py:333
  59.7 5.3 %collective-permute-start.18 = (f32[64,512]{1,0:T(8,128)S(1)}, f32[64,512]{1,0:T(8,128)S(1)}, u32[]{:S(2)}, u32[]{:S(2)}) collective-permute-start(f32[64,512]{1,0:T(8,128)S(1)} %far_terms.21.refs_0_), channel_id=1, source_target_pairs={{0,16},{4,20},{1,17},{5,21},{2,18},{6,22},{3,19},{7,23}} | collective-permute-start | bytes 393224 | tf_op jit(solution)/shard_map/ppermute | solution.py:333
  62.1 2.8 %collective-permute-start.19 = (f32[64,512]{1,0:T(8,128)S(1)}, f32[64,512]{1,0:T(8,128)S(1)}, u32[]{:S(2)}, u32[]{:S(2)}) collective-permute-start(f32[64,512]{1,0:T(8,128)S(1)} %get-tuple-element.138), channel_id=1, source_target_pairs={{24,16},{28,20},{25,17},{29,21},{26,18},{30,22},{27,19},{31,23}} | collective-permute-start | bytes 393224 | tf_op jit(solution)/shard_map/ppermute | solution.py:333
  64.3 3.3 %collective-permute-start.20 = (f32[64,512]{1,0:T(8,128)S(1)}, f32[64,512]{1,0:T(8,128)S(1)}, u32[]{:S(2)}, u32[]{:S(2)}) collective-permute-start(f32[64,512]{1,0:T(8,128)S(1)} %far_terms.22.refs_0_), channel_id=1, source_target_pairs={{24,8},{28,12},{25,9},{29,13},{26,10},{30,14},{27,11},{31,15}} | collective-permute-start | bytes 393224 | tf_op jit(solution)/shard_map/ppermute | solution.py:333
  65.3 2.3 %collective-permute-start.21 = (f32[64,512]{1,0:T(8,128)S(1)}, f32[64,512]{1,0:T(8,128)S(1)}, u32[]{:S(2)}, u32[]{:S(2)}) collective-permute-start(f32[64,512]{1,0:T(8,128)S(1)} %get-tuple-element.140), channel_id=1, source_target_pairs={{16,8},{20,12},{17,9},{21,13},{18,10},{22,14},{19,11},{23,15}} | collective-permute-start | bytes 393224 | tf_op jit(solution)/shard_map/ppermute | solution.py:333
  66.3 8.4 %collective-permute-start.22 = (f32[64,512]{1,0:T(8,128)S(1)}, f32[64,512]{1,0:T(8,128)S(1)}, u32[]{:S(2)}, u32[]{:S(2)}) collective-permute-start(f32[64,512]{1,0:T(8,128)S(1)} %far_terms.23.refs_0_), channel_id=1, source_target_pairs={{16,0},{20,4},{17,1},{21,5},{18,2},{22,6},{19,3},{23,7}} | collective-permute-start | bytes 393224 | tf_op jit(solution)/shard_map/ppermute | solution.py:333
  67.9 11.2 %collective-permute-start.23 = (f32[64,512]{1,0:T(8,128)S(1)}, f32[64,512]{1,0:T(8,128)S(1)}, u32[]{:S(2)}, u32[]{:S(2)}) collective-permute-start(f32[64,512]{1,0:T(8,128)S(1)} %get-tuple-element.142), channel_id=1, source_target_pairs={{8,0},{12,4},{9,1},{13,5},{10,2},{14,6},{11,3},{15,7}} | collective-permute-start | bytes 393224 | tf_op jit(solution)/shard_map/ppermute | solution.py:333
  79.4 5.8 %collective-permute-start.25 = (f32[64,512]{1,0:T(8,128)S(1)}, f32[64,512]{1,0:T(8,128)S(1)}, u32[]{:S(2)}, u32[]{:S(2)}) collective-permute-start(f32[64,512]{1,0:T(8,128)S(1)} %get-tuple-element.144), channel_id=1, source_target_pairs={{0,24},{4,28},{1,25},{5,29},{2,26},{6,30},{3,27},{7,31}} | collective-permute-start | bytes 393224 | tf_op jit(solution)/shard_map/ppermute | solution.py:333
  80.7 4.6 %collective-permute-start.24 = (f32[64,512]{1,0:T(8,128)S(1)}, f32[64,512]{1,0:T(8,128)S(1)}, u32[]{:S(2)}, u32[]{:S(2)}) collective-permute-start(f32[64,512]{1,0:T(8,128)S(1)} %far_terms.24.refs_0_), channel_id=1, source_target_pairs={{8,24},{12,28},{9,25},{13,29},{10,26},{14,30},{11,27},{15,31}} | collective-permute-start | bytes 393224 | tf_op jit(solution)/shard_map/ppermute | solution.py:333
  83.0 5.3 %collective-permute-start.27 = (f32[64,512]{1,0:T(8,128)S(1)}, f32[64,512]{1,0:T(8,128)S(1)}, u32[]{:S(2)}, u32[]{:S(2)}) collective-permute-start(f32[64,512]{1,0:T(8,128)S(1)} %far_terms.25.refs_0_), channel_id=1, source_target_pairs={{0,16},{4,20},{1,17},{5,21},{2,18},{6,22},{3,19},{7,23}} | collective-permute-start | bytes 393224 | tf_op jit(solution)/shard_map/ppermute | solution.py:333
  85.5 2.8 %collective-permute-start.28 = (f32[64,512]{1,0:T(8,128)S(1)}, f32[64,512]{1,0:T(8,128)S(1)}, u32[]{:S(2)}, u32[]{:S(2)}) collective-permute-start(f32[64,512]{1,0:T(8,128)S(1)} %get-tuple-element.157), channel_id=1, source_target_pairs={{24,16},{28,20},{25,17},{29,21},{26,18},{30,22},{27,19},{31,23}} | collective-permute-start | bytes 393224 | tf_op jit(solution)/shard_map/ppermute | solution.py:333
  87.7 3.3 %collective-permute-start.29 = (f32[64,512]{1,0:T(8,128)S(1)}, f32[64,512]{1,0:T(8,128)S(1)}, u32[]{:S(2)}, u32[]{:S(2)}) collective-permute-start(f32[64,512]{1,0:T(8,128)S(1)} %far_terms.26.refs_0_), channel_id=1, source_target_pairs={{24,8},{28,12},{25,9},{29,13},{26,10},{30,14},{27,11},{31,15}} | collective-permute-start | bytes 393224 | tf_op jit(solution)/shard_map/ppermute | solution.py:333
  88.7 2.3 %collective-permute-start.30 = (f32[64,512]{1,0:T(8,128)S(1)}, f32[64,512]{1,0:T(8,128)S(1)}, u32[]{:S(2)}, u32[]{:S(2)}) collective-permute-start(f32[64,512]{1,0:T(8,128)S(1)} %get-tuple-element.159), channel_id=1, source_target_pairs={{16,8},{20,12},{17,9},{21,13},{18,10},{22,14},{19,11},{23,15}} | collective-permute-start | bytes 393224 | tf_op jit(solution)/shard_map/ppermute | solution.py:333
  89.6 8.3 %collective-permute-start.31 = (f32[64,512]{1,0:T(8,128)S(1)}, f32[64,512]{1,0:T(8,128)S(1)}, u32[]{:S(2)}, u32[]{:S(2)}) collective-permute-start(f32[64,512]{1,0:T(8,128)S(1)} %far_terms.27.refs_0_), channel_id=1, source_target_pairs={{16,0},{20,4},{17,1},{21,5},{18,2},{22,6},{19,3},{23,7}} | collective-permute-start | bytes 393224 | tf_op jit(solution)/shard_map/ppermute | solution.py:333
  91.3 11.0 %collective-permute-start.32 = (f32[64,512]{1,0:T(8,128)S(1)}, f32[64,512]{1,0:T(8,128)S(1)}, u32[]{:S(2)}, u32[]{:S(2)}) collective-permute-start(f32[64,512]{1,0:T(8,128)S(1)} %get-tuple-element.161), channel_id=1, source_target_pairs={{8,0},{12,4},{9,1},{13,5},{10,2},{14,6},{11,3},{15,7}} | collective-permute-start | bytes 393224 | tf_op jit(solution)/shard_map/ppermute | solution.py:333
  92.6 10.8 %collective-permute-start.39 = (f32[64,256]{1,0:T(8,128)S(1)}, f32[64,256]{1,0:T(8,128)S(1)}, u32[]{:S(2)}, u32[]{:S(2)}) collective-permute-start(f32[64,256]{1,0:T(8,128)S(1)} %get-tuple-element.174), channel_id=1, source_target_pairs={{0,4},{4,0},{8,12},{12,8},{16,20},{20,16},{24,28},{28,24},{1,5},{5... | collective-permute-start | bytes 196616 | tf_op jit(solution)/shard_map/ppermute | solution.py:322
  92.6 10.8 %collective-permute-start.38 = (f32[64,256]{1,0:T(8,128)S(1)}, f32[64,256]{1,0:T(8,128)S(1)}, u32[]{:S(2)}, u32[]{:S(2)}) collective-permute-start(f32[64,256]{1,0:T(8,128)S(1)} %get-tuple-element.173), channel_id=1, source_target_pairs={{0,4},{4,0},{8,12},{12,8},{16,20},{20,16},{24,28},{28,24},{1,5},{5... | collective-permute-start | bytes 196616 | tf_op jit(solution)/shard_map/ppermute | solution.py:322
  93.1 13.2 %collective-permute-start.37 = (f32[64,256]{1,0:T(8,128)S(1)}, f32[64,256]{1,0:T(8,128)S(1)}, u32[]{:S(2)}, u32[]{:S(2)}) collective-permute-start(f32[64,256]{1,0:T(8,128)S(1)} %get-tuple-element.172), channel_id=1, source_target_pairs={{0,4},{4,0},{8,12},{12,8},{16,20},{20,16},{24,28},{28,24},{1,5},{5... | collective-permute-start | bytes 196616 | tf_op jit(solution)/shard_map/ppermute | solution.py:322
  103.2 3.1 %collective-permute-start.36 = (f32[64,256]{1,0:T(8,128)S(1)}, f32[64,256]{1,0:T(8,128)S(1)}, u32[]{:S(2)}, u32[]{:S(2)}) collective-permute-start(f32[64,256]{1,0:T(8,128)S(1)} %get-tuple-element.171), channel_id=1, source_target_pairs={{0,4},{4,0},{8,12},{12,8},{16,20},{20,16},{24,28},{28,24},{1,5},{5... | collective-permute-start | bytes 196616 | tf_op jit(solution)/shard_map/ppermute | solution.py:322
  103.3 5.0 %collective-permute-start.33 = (f32[64,128]{1,0:T(8,128)S(1)}, f32[64,128]{1,0:T(8,128)S(1)}, u32[]{:S(2)}, u32[]{:S(2)}) collective-permute-start(f32[64,128]{1,0:T(8,128)S(1)} %get-tuple-element.164), channel_id=1, source_target_pairs={{0,8},{4,12},{8,16},{12,20},{16,24},{20,28},{24,0},{28,4},{1,9},{5... | collective-permute-start | bytes 98312 | tf_op jit(solution)/shard_map/ppermute | solution.py:325
  103.4 5.0 %collective-permute-start.34 = (f32[64,128]{1,0:T(8,128)S(1)}, f32[64,128]{1,0:T(8,128)S(1)}, u32[]{:S(2)}, u32[]{:S(2)}) collective-permute-start(f32[64,128]{1,0:T(8,128)S(1)} %get-tuple-element.165), channel_id=1, source_target_pairs={{0,16},{4,20},{8,24},{12,28},{16,0},{20,4},{24,8},{28,12},{1,17},{... | collective-permute-start | bytes 98312 | tf_op jit(solution)/shard_map/ppermute | solution.py:325
  103.4 5.3 %collective-permute-start.35 = (f32[64,128]{1,0:T(8,128)S(1)}, f32[64,128]{1,0:T(8,128)S(1)}, u32[]{:S(2)}, u32[]{:S(2)}) collective-permute-start(f32[64,128]{1,0:T(8,128)S(1)} %get-tuple-element.166), channel_id=1, source_target_pairs={{0,24},{4,28},{8,0},{12,4},{16,8},{20,12},{24,16},{28,20},{1,25},{... | collective-permute-start | bytes 98312 | tf_op jit(solution)/shard_map/ppermute | solution.py:325
  108.7 1.2 %collective-permute-start.40 = (f32[32,128]{1,0:T(8,128)S(1)}, f32[32,128]{1,0:T(8,128)S(1)}, u32[]{:S(2)}, u32[]{:S(2)}) collective-permute-start(f32[32,128]{1,0:T(8,128)S(1)} %get-tuple-element.181), channel_id=1, source_target_pairs={{0,4},{4,0},{8,12},{12,8},{16,20},{20,16},{24,28},{28,24},{1,5},{5... | collective-permute-start | bytes 49160 | tf_op jit(solution)/shard_map/ppermute | solution.py:322
where the time goes:
time: 112 us; the launch traced here: 111 us
  waiting for transfers between devices  44.8 us (40%)
  starting transfers between devices  33.6 us (30%)
  Pallas kernels  30.9 us (28%)
  between operations  1.49 us (1%)
    ppermute x29, waiting for transfers between devices, pass_on(): return lax.ppermute(x, 'blk', perm)  42.2 us
    pallas_call x47, Pallas kernels, call(): pl.pallas_call(kernel, out_shape=outs, in_specs=more.pop('in_specs', [VME...  30.9 us
    ppermute x29, starting transfers between devices, pass_on(): return lax.ppermute(x, 'blk', perm)  28.5 us
    ppermute x3, starting transfers between devices, shift(): return lax.ppermute(x, 'blk', [(i, (i + 2 * by) % n) for i in range(n)])  3 us
  transfers between devices with their start and end apart: 41, of which 11 were waited for; matrix products, arithmetic and copies ran while one was open for 0% of the time, Pallas kernels for 24%

commit v1 on v0

--- a/solution.py
+++ b/solution.py
@@ -325,11 +325,10 @@
         return lax.ppermute(x, "blk", [(i, (i + 2 * by) % n) for i in range(n)])
 
     def pass_on(x, lead, by):
-        perm = []
-        for k in range(lead, lead + 2 * pieces, 2):
-            if by <= k < count:
-                sender, target = k % pairs, (k - by) % pairs
-                perm += [(2 * sender + c, 2 * target + c) for c in range(2)]
+        ring = [(lead - i) % pairs for i in range(0, 3, by)]
+        target = {q: q for q in range(pairs)}
+        target.update(zip(ring, ring[1:] + ring[:1]))
+        perm = [(2 * q + c, 2 * to + c) for q, to in target.items() for c in range(2)]
         return lax.ppermute(x, "blk", perm)
 
     def pack(rows, turnout=turnout):

time: 112 us -> 141 us (1.26)
  starting transfers between devices: 33.6 us -> 85.4 us
  waiting for transfers between devices: 44.8 us -> 22 us
    ppermute x29, starting transfers between devices: 28.5 us -> 79.9 us  [pass_on(): return lax.ppermute(x, 'blk', perm)]
    ppermute x29, waiting for transfers between devices: 42.2 us -> 19.4 us  [pass_on(): return lax.ppermute(x, 'blk', perm)]
  transfers between devices with their start and end apart: 41 -> 41, of which waited for: 11 -> 12; matrix products, arithmetic and copies ran while one was open for 0% -> 0% of each run, Pallas kernels for 24% -> 19%
where the time goes in v1:
time: 141 us; the launch traced here: 140 us
  starting transfers between devices  85.4 us (61%)
  Pallas kernels  30.9 us (22%)
  waiting for transfers between devices  22 us (16%)
  between operations  1.46 us (1%)
    ppermute x29, starting transfers between devices, pass_on(): return lax.ppermute(x, 'blk', perm)  79.9 us
    pallas_call x47, Pallas kernels, call(): pl.pallas_call(kernel, out_shape=outs, in_specs=more.pop('in_specs', [VME...  30.9 us
    ppermute x29, waiting for transfers between devices, pass_on(): return lax.ppermute(x, 'blk', perm)  19.4 us
    ppermute x3, starting transfers between devices, shift(): return lax.ppermute(x, 'blk', [(i, (i + 2 * by) % n) for i in range(n)])  3.62 us
  transfers between devices with their start and end apart: 41, of which 12 were waited for; matrix products, arithmetic and copies ran while one was open for 0% of the time, Pallas kernels for 19%

profile of v1, /device:TPU:0, one launch (start us, length us, event | category | flops | bytes accessed | tf_op | source)
XLA Modules:
  0.0 139.8 jit_solution(9112166744361726895)
XLA Ops:
  0.6 3.1 %pack.2.own.refs_6_ = f32[1192,256]{1,0:T(8,128)} custom-call(s32[3,1,4]{2,1,0:T(1,128)} %bitcast.1, f32[4,1,256]{2,1,0:T(1,128)} %turnout.2, s32[4,1,256]{2,1,0:T(1,128)} %district.3, f32[4,1,3,256,256]{4,3,2,1,0:T(8,128)} %l_ref.3, f32[4,1,256,256]{3,2,1,0:T(8,128)} %d_ref.3, f32[4,1,256,128]{3,2,1,0:T(8,128)} %r_ref.3), custom_call_target="tpu_custom_call" | custom-call | bytes 2441216 | tf_op jit(solution)/shard_map/pack/pallas_call | solution.py:310
  4.2 4.7 %pack.3 = (f32[1192,256]{1,0:T(8,128)}, f32[1192,256]{1,0:T(8,128)}, f32[1192,256]{1,0:T(8,128)}) custom-call(s32[3,1,4]{2,1,0:T(1,128)} %bitcast.2, f32[4,1,256]{2,1,0:T(1,128)} %turnout.2, s32[4,1,256]{2,1,0:T(1,128)} %district.3, f32[4,1,3,256,256]{4,3,2,1,0:T(8,128)} %l_ref.3, f32[4,1,256,256]{3,2,1,0:T(8,128)} %d_ref.3, f32[4,1,256,128]{3,2,1,0:T(8,128)} %r_ref.3), custom_call_target="tpu_custom_call" | custom-call | bytes 7323648 | tf_op jit(solution)/shard_map/pack/pallas_call | solution.py:310
  9.6 1.2 near_setup.4
  11.7 1.2 far_setup.4
  14.2 9.4 %collective-permute-start.3 = (f32[64,512]{1,0:T(8,128)S(1)}, f32[64,512]{1,0:T(8,128)S(1)}, u32[]{:S(2)}, u32[]{:S(2)}) collective-permute-start(f32[64,512]{1,0:T(8,128)S(1)} %get-tuple-element.102), channel_id=1, source_target_pairs={{0,16},{4,20},{8,0},{12,4},{16,8},{20,12},{24,24},{28,28},{1,17},{... | collective-permute-start | bytes 393224 | tf_op jit(solution)/shard_map/ppermute | solution.py:332
  23.9 4.4 %collective-permute-start.4 = (f32[64,512]{1,0:T(8,128)S(1)}, f32[64,512]{1,0:T(8,128)S(1)}, u32[]{:S(2)}, u32[]{:S(2)}) collective-permute-start(f32[64,512]{1,0:T(8,128)S(1)} %far_terms.15.refs_0_), channel_id=1, source_target_pairs={{0,16},{4,20},{8,8},{12,12},{16,0},{20,4},{24,24},{28,28},{1,17},{... | collective-permute-start | bytes 393224 | tf_op jit(solution)/shard_map/ppermute | solution.py:332
  28.6 1.9 %collective-permute-start.5 = (f32[64,512]{1,0:T(8,128)S(1)}, f32[64,512]{1,0:T(8,128)S(1)}, u32[]{:S(2)}, u32[]{:S(2)}) collective-permute-start(f32[64,512]{1,0:T(8,128)S(1)} %get-tuple-element.104), channel_id=1, source_target_pairs={{0,24},{4,28},{8,0},{12,4},{16,16},{20,20},{24,8},{28,12},{1,25},{... | collective-permute-start | bytes 393224 | tf_op jit(solution)/shard_map/ppermute | solution.py:332
  31.2 4.2 %collective-permute-done.5.refs_2_ = f32[64,512]{1,0:T(8,128)S(1)} collective-permute-done((f32[64,512]{1,0:T(8,128)S(1)}, f32[64,512]{1,0:T(8,128)S(1)}, u32[]{:S(2)}, u32[]{:S(2)}) %collective-permute-start.5) | collective-permute-done | bytes 131104 | tf_op jit(solution)/shard_map/ppermute | solution.py:332
  35.7 2.9 %collective-permute-start.7 = (f32[64,512]{1,0:T(8,128)S(1)}, f32[64,512]{1,0:T(8,128)S(1)}, u32[]{:S(2)}, u32[]{:S(2)}) collective-permute-start(f32[64,512]{1,0:T(8,128)S(1)} %get-tuple-element.106), channel_id=1, source_target_pairs={{0,24},{4,28},{8,8},{12,12},{16,0},{20,4},{24,16},{28,20},{1,25},{... | collective-permute-start | bytes 393224 | tf_op jit(solution)/shard_map/ppermute | solution.py:332
  38.7 0.7 collective-permute-start.6
  39.4 1.2 near_setup.5
  40.9 2.9 %collective-permute-start.9 = (f32[64,512]{1,0:T(8,128)S(1)}, f32[64,512]{1,0:T(8,128)S(1)}, u32[]{:S(2)}, u32[]{:S(2)}) collective-permute-start(f32[64,512]{1,0:T(8,128)S(1)} %far_terms.17.refs_0_), channel_id=1, source_target_pairs={{0,16},{4,20},{8,8},{12,12},{16,0},{20,4},{24,24},{28,28},{1,17},{... | collective-permute-start | bytes 393224 | tf_op jit(solution)/shard_map/ppermute | solution.py:332
  43.8 0.9 finish.4
  45.0 0.7 collective-permute-start.10
  45.6 1.2 far_setup.5
  48.1 6.9 %collective-permute-start.12 = (f32[64,512]{1,0:T(8,128)S(1)}, f32[64,512]{1,0:T(8,128)S(1)}, u32[]{:S(2)}, u32[]{:S(2)}) collective-permute-start(f32[64,512]{1,0:T(8,128)S(1)} %get-tuple-element.121), channel_id=1, source_target_pairs={{0,16},{4,20},{8,0},{12,4},{16,8},{20,12},{24,24},{28,28},{1,17},{... | collective-permute-start | bytes 393224 | tf_op jit(solution)/shard_map/ppermute | solution.py:332
  55.3 3.9 %collective-permute-start.13 = (f32[64,512]{1,0:T(8,128)S(1)}, f32[64,512]{1,0:T(8,128)S(1)}, u32[]{:S(2)}, u32[]{:S(2)}) collective-permute-start(f32[64,512]{1,0:T(8,128)S(1)} %far_terms.19.refs_0_), channel_id=1, source_target_pairs={{0,16},{4,20},{8,8},{12,12},{16,0},{20,4},{24,24},{28,28},{1,17},{... | collective-permute-start | bytes 393224 | tf_op jit(solution)/shard_map/ppermute | solution.py:332
  59.5 1.9 %collective-permute-start.14 = (f32[64,512]{1,0:T(8,128)S(1)}, f32[64,512]{1,0:T(8,128)S(1)}, u32[]{:S(2)}, u32[]{:S(2)}) collective-permute-start(f32[64,512]{1,0:T(8,128)S(1)} %get-tuple-element.123), channel_id=1, source_target_pairs={{0,24},{4,28},{8,0},{12,4},{16,16},{20,20},{24,8},{28,12},{1,25},{... | collective-permute-start | bytes 393224 | tf_op jit(solution)/shard_map/ppermute | solution.py:332
  62.2 4.3 %collective-permute-done.14.refs_2_ = f32[64,512]{1,0:T(8,128)S(1)} collective-permute-done((f32[64,512]{1,0:T(8,128)S(1)}, f32[64,512]{1,0:T(8,128)S(1)}, u32[]{:S(2)}, u32[]{:S(2)}) %collective-permute-start.14) | collective-permute-done | bytes 131104 | tf_op jit(solution)/shard_map/ppermute | solution.py:332
  66.8 2.9 %collective-permute-start.16 = (f32[64,512]{1,0:T(8,128)S(1)}, f32[64,512]{1,0:T(8,128)S(1)}, u32[]{:S(2)}, u32[]{:S(2)}) collective-permute-start(f32[64,512]{1,0:T(8,128)S(1)} %get-tuple-element.125), channel_id=1, source_target_pairs={{0,24},{4,28},{8,8},{12,12},{16,0},{20,4},{24,16},{28,20},{1,25},{... | collective-permute-start | bytes 393224 | tf_op jit(solution)/shard_map/ppermute | solution.py:332
  69.8 0.7 collective-permute-start.15
  70.5 1.2 near_setup.6
  72.0 2.9 %collective-permute-start.18 = (f32[64,512]{1,0:T(8,128)S(1)}, f32[64,512]{1,0:T(8,128)S(1)}, u32[]{:S(2)}, u32[]{:S(2)}) collective-permute-start(f32[64,512]{1,0:T(8,128)S(1)} %far_terms.21.refs_0_), channel_id=1, source_target_pairs={{0,16},{4,20},{8,8},{12,12},{16,0},{20,4},{24,24},{28,28},{1,17},{... | collective-permute-start | bytes 393224 | tf_op jit(solution)/shard_map/ppermute | solution.py:332
  74.9 0.9 finish.5
  76.7 1.2 far_setup.6
  78.2 0.7 collective-permute-start.20
  79.2 6.9 %collective-permute-start.21 = (f32[64,512]{1,0:T(8,128)S(1)}, f32[64,512]{1,0:T(8,128)S(1)}, u32[]{:S(2)}, u32[]{:S(2)}) collective-permute-start(f32[64,512]{1,0:T(8,128)S(1)} %get-tuple-element.140), channel_id=1, source_target_pairs={{0,16},{4,20},{8,0},{12,4},{16,8},{20,12},{24,24},{28,28},{1,17},{... | collective-permute-start | bytes 393224 | tf_op jit(solution)/shard_map/ppermute | solution.py:332
  86.4 3.9 %collective-permute-start.22 = (f32[64,512]{1,0:T(8,128)S(1)}, f32[64,512]{1,0:T(8,128)S(1)}, u32[]{:S(2)}, u32[]{:S(2)}) collective-permute-start(f32[64,512]{1,0:T(8,128)S(1)} %far_terms.23.refs_0_), channel_id=1, source_target_pairs={{0,16},{4,20},{8,8},{12,12},{16,0},{20,4},{24,24},{28,28},{1,17},{... | collective-permute-start | bytes 393224 | tf_op jit(solution)/shard_map/ppermute | solution.py:332
  90.6 1.9 %collective-permute-start.23 = (f32[64,512]{1,0:T(8,128)S(1)}, f32[64,512]{1,0:T(8,128)S(1)}, u32[]{:S(2)}, u32[]{:S(2)}) collective-permute-start(f32[64,512]{1,0:T(8,128)S(1)} %get-tuple-element.142), channel_id=1, source_target_pairs={{0,24},{4,28},{8,0},{12,4},{16,16},{20,20},{24,8},{28,12},{1,25},{... | collective-permute-start | bytes 393224 | tf_op jit(solution)/shard_map/ppermute | solution.py:332
  93.3 4.4 %collective-permute-done.23.refs_2_ = f32[64,512]{1,0:T(8,128)S(1)} collective-permute-done((f32[64,512]{1,0:T(8,128)S(1)}, f32[64,512]{1,0:T(8,128)S(1)}, u32[]{:S(2)}, u32[]{:S(2)}) %collective-permute-start.23) | collective-permute-done | bytes 131104 | tf_op jit(solution)/shard_map/ppermute | solution.py:332
  98.0 3.7 %collective-permute-start.25 = (f32[64,512]{1,0:T(8,128)S(1)}, f32[64,512]{1,0:T(8,128)S(1)}, u32[]{:S(2)}, u32[]{:S(2)}) collective-permute-start(f32[64,512]{1,0:T(8,128)S(1)} %get-tuple-element.144), channel_id=1, source_target_pairs={{0,24},{4,28},{8,8},{12,12},{16,0},{20,4},{24,16},{28,20},{1,25},{... | collective-permute-start | bytes 393224 | tf_op jit(solution)/shard_map/ppermute | solution.py:332
  101.8 0.8 collective-permute-start.24
  102.7 1.2 near_setup.7
  104.1 2.1 %collective-permute-start.27 = (f32[64,512]{1,0:T(8,128)S(1)}, f32[64,512]{1,0:T(8,128)S(1)}, u32[]{:S(2)}, u32[]{:S(2)}) collective-permute-start(f32[64,512]{1,0:T(8,128)S(1)} %far_terms.25.refs_0_), channel_id=1, source_target_pairs={{0,16},{4,20},{8,8},{12,12},{16,0},{20,4},{24,24},{28,28},{1,17},{... | collective-permute-start | bytes 393224 | tf_op jit(solution)/shard_map/ppermute | solution.py:332
  106.3 0.9 finish.6
  108.1 1.2 far_setup.7
  110.3 0.7 collective-permute-done.27.refs_1_
  111.3 7.0 %collective-permute-start.30 = (f32[64,512]{1,0:T(8,128)S(1)}, f32[64,512]{1,0:T(8,128)S(1)}, u32[]{:S(2)}, u32[]{:S(2)}) collective-permute-start(f32[64,512]{1,0:T(8,128)S(1)} %get-tuple-element.159), channel_id=1, source_target_pairs={{0,16},{4,20},{8,0},{12,4},{16,8},{20,12},{24,24},{28,28},{1,17},{... | collective-permute-start | bytes 393224 | tf_op jit(solution)/shard_map/ppermute | solution.py:332
  118.6 4.8 %collective-permute-start.31 = (f32[64,512]{1,0:T(8,128)S(1)}, f32[64,512]{1,0:T(8,128)S(1)}, u32[]{:S(2)}, u32[]{:S(2)}) collective-permute-start(f32[64,512]{1,0:T(8,128)S(1)} %far_terms.27.refs_0_), channel_id=1, source_target_pairs={{0,16},{4,20},{8,8},{12,12},{16,0},{20,4},{24,24},{28,28},{1,17},{... | collective-permute-start | bytes 393224 | tf_op jit(solution)/shard_map/ppermute | solution.py:332
  123.7 1.9 %collective-permute-start.32 = (f32[64,512]{1,0:T(8,128)S(1)}, f32[64,512]{1,0:T(8,128)S(1)}, u32[]{:S(2)}, u32[]{:S(2)}) collective-permute-start(f32[64,512]{1,0:T(8,128)S(1)} %get-tuple-element.161), channel_id=1, source_target_pairs={{0,24},{4,28},{8,0},{12,4},{16,16},{20,20},{24,8},{28,12},{1,25},{... | collective-permute-start | bytes 393224 | tf_op jit(solution)/shard_map/ppermute | solution.py:332
  126.3 4.4 %collective-permute-done.32.refs_1_ = f32[64,512]{1,0:T(8,128)S(1)} collective-permute-done((f32[64,512]{1,0:T(8,128)S(1)}, f32[64,512]{1,0:T(8,128)S(1)}, u32[]{:S(2)}, u32[]{:S(2)}) %collective-permute-start.32) | collective-permute-done | bytes 131104 | tf_op jit(solution)/shard_map/ppermute | solution.py:332
  130.7 0.9 finish.7
  131.7 2.1 %collective-permute-start.33 = (f32[64,128]{1,0:T(8,128)S(1)}, f32[64,128]{1,0:T(8,128)S(1)}, u32[]{:S(2)}, u32[]{:S(2)}) collective-permute-start(f32[64,128]{1,0:T(8,128)S(1)} %get-tuple-element.164), channel_id=1, source_target_pairs={{0,8},{4,12},{8,16},{12,20},{16,24},{20,28},{24,0},{28,4},{1,9},{5... | collective-permute-start | bytes 98312 | tf_op jit(solution)/shard_map/ppermute | solution.py:325
  133.8 1.6 %collective-permute-start.35 = (f32[64,128]{1,0:T(8,128)S(1)}, f32[64,128]{1,0:T(8,128)S(1)}, u32[]{:S(2)}, u32[]{:S(2)}) collective-permute-start(f32[64,128]{1,0:T(8,128)S(1)} %get-tuple-element.166), channel_id=1, source_target_pairs={{0,24},{4,28},{8,0},{12,4},{16,8},{20,12},{24,16},{28,20},{1,25},{... | collective-permute-start | bytes 98312 | tf_op jit(solution)/shard_map/ppermute | solution.py:325
  135.4 1.0 field.1
  136.6 1.1 collective-permute-done.34.refs_2_
  137.9 1.2 collective-permute-done.40.got
  139.0 0.8 district_mean.1
  (89 shorter events, 15.9 us)
Async XLA Ops:
  3.7 5.8 %copy-start = (f32[1192,256]{1,0:T(8,128)S(1)}, f32[1192,256]{1,0:T(8,128)}, u32[]{:S(2)}) copy-start(f32[1192,256]{1,0:T(8,128)} %pack.2.own.refs_6_) | copy-start | bytes 3661828
  3.7 5.8 %collective-permute-start = (f32[1192,256]{1,0:T(8,128)}, f32[1192,256]{1,0:T(8,128)S(1)}, u32[]{:S(2)}, u32[]{:S(2)}) collective-permute-start(f32[1192,256]{1,0:T(8,128)} %pack.2.own.refs_6_), channel_id=1, source_target_pairs={{0,4},{4,0},{8,12},{12,8},{16,20},{20,16},{24,28},{28,24},{1,5},{5... | collective-permute-start | bytes 3661832 | tf_op jit(solution)/shard_map/ppermute | solution.py:322
  9.0 30.4 %collective-permute-start.8 = (f32[1192,256]{1,0:T(8,128)}, f32[1192,256]{1,0:T(8,128)S(1)}, u32[]{:S(2)}, u32[]{:S(2)}) collective-permute-start(f32[1192,256]{1,0:T(8,128)} %get-tuple-element.110.own.refs_6_), channel_id=1, source_target_pairs={{0,4},{4,0},{8,12},{12,8},{16,20},{20,16},{24,28},{28,24},{1,5},{5... | collective-permute-start | bytes 3661832 | tf_op jit(solution)/shard_map/ppermute | solution.py:322
  9.2 61.2 %collective-permute-start.17 = (f32[1192,256]{1,0:T(8,128)}, f32[1192,256]{1,0:T(8,128)S(1)}, u32[]{:S(2)}, u32[]{:S(2)}) collective-permute-start(f32[1192,256]{1,0:T(8,128)} %get-tuple-element.129.own.refs_6_), channel_id=1, source_target_pairs={{0,4},{4,0},{8,12},{12,8},{16,20},{20,16},{24,28},{28,24},{1,5},{5... | collective-permute-start | bytes 3661832 | tf_op jit(solution)/shard_map/ppermute | solution.py:322
  11.0 2.9 %collective-permute-start.1 = (f32[64,512]{1,0:T(8,128)S(1)}, f32[64,512]{1,0:T(8,128)S(1)}, u32[]{:S(2)}, u32[]{:S(2)}) collective-permute-start(f32[64,512]{1,0:T(8,128)S(1)} %get-tuple-element.100), channel_id=1, source_target_pairs={{0,0},{4,4},{8,24},{12,28},{16,8},{20,12},{24,16},{28,20},{1,1},{5... | collective-permute-start | bytes 393224 | tf_op jit(solution)/shard_map/ppermute | solution.py:332
  13.2 15.0 %collective-permute-start.2 = (f32[64,512]{1,0:T(8,128)S(1)}, f32[64,512]{1,0:T(8,128)S(1)}, u32[]{:S(2)}, u32[]{:S(2)}) collective-permute-start(f32[64,512]{1,0:T(8,128)S(1)} %far_terms.14.refs_0_), channel_id=1, source_target_pairs={{0,0},{4,4},{8,24},{12,28},{16,16},{20,20},{24,8},{28,12},{1,1},{5... | collective-permute-start | bytes 393224 | tf_op jit(solution)/shard_map/ppermute | solution.py:332
  14.2 14.1 %collective-permute-start.3 = (f32[64,512]{1,0:T(8,128)S(1)}, f32[64,512]{1,0:T(8,128)S(1)}, u32[]{:S(2)}, u32[]{:S(2)}) collective-permute-start(f32[64,512]{1,0:T(8,128)S(1)} %get-tuple-element.102), channel_id=1, source_target_pairs={{0,16},{4,20},{8,0},{12,4},{16,8},{20,12},{24,24},{28,28},{1,17},{... | collective-permute-start | bytes 393224 | tf_op jit(solution)/shard_map/ppermute | solution.py:332
  23.6 6.9 %copy-start.1 = (f32[1192,256]{1,0:T(8,128)S(1)}, f32[1192,256]{1,0:T(8,128)}, u32[]{:S(2)}) copy-start(f32[1192,256]{1,0:T(8,128)} %get-tuple-element.148.own.refs_6_) | copy-start | bytes 3661828
  23.9 7.3 %collective-permute-start.4 = (f32[64,512]{1,0:T(8,128)S(1)}, f32[64,512]{1,0:T(8,128)S(1)}, u32[]{:S(2)}, u32[]{:S(2)}) collective-permute-start(f32[64,512]{1,0:T(8,128)S(1)} %far_terms.15.refs_0_), channel_id=1, source_target_pairs={{0,16},{4,20},{8,8},{12,12},{16,0},{20,4},{24,24},{28,28},{1,17},{... | collective-permute-start | bytes 393224 | tf_op jit(solution)/shard_map/ppermute | solution.py:332
  28.6 6.9 %collective-permute-start.5 = (f32[64,512]{1,0:T(8,128)S(1)}, f32[64,512]{1,0:T(8,128)S(1)}, u32[]{:S(2)}, u32[]{:S(2)}) collective-permute-start(f32[64,512]{1,0:T(8,128)S(1)} %get-tuple-element.104), channel_id=1, source_target_pairs={{0,24},{4,28},{8,0},{12,4},{16,16},{20,20},{24,8},{28,12},{1,25},{... | collective-permute-start | bytes 393224 | tf_op jit(solution)/shard_map/ppermute | solution.py:332
  30.5 72.1 %collective-permute-start.26 = (f32[1192,256]{1,0:T(8,128)S(1)}, f32[1192,256]{1,0:T(8,128)S(1)}, u32[]{:S(2)}, u32[]{:S(2)}) collective-permute-start(f32[1192,256]{1,0:T(8,128)S(1)} %copy-done.1), channel_id=1, source_target_pairs={{0,4},{4,0},{8,12},{12,8},{16,20},{20,16},{24,28},{28,24},{1,5},{5... | collective-permute-start | bytes 3661832 | tf_op jit(solution)/shard_map/ppermute | solution.py:322
  30.6 8.8 %copy-start.3 = (f32[1192,256]{1,0:T(8,128)S(1)}, f32[1192,256]{1,0:T(8,128)}, u32[]{:S(2)}) copy-start(f32[1192,256]{1,0:T(8,128)} %get-tuple-element.110.own.refs_6_) | copy-start | bytes 3661828
  35.7 8.9 %collective-permute-start.7 = (f32[64,512]{1,0:T(8,128)S(1)}, f32[64,512]{1,0:T(8,128)S(1)}, u32[]{:S(2)}, u32[]{:S(2)}) collective-permute-start(f32[64,512]{1,0:T(8,128)S(1)} %get-tuple-element.106), channel_id=1, source_target_pairs={{0,24},{4,28},{8,8},{12,12},{16,0},{20,4},{24,16},{28,20},{1,25},{... | collective-permute-start | bytes 393224 | tf_op jit(solution)/shard_map/ppermute | solution.py:332
  38.7 6.0 %collective-permute-start.6 = (f32[64,512]{1,0:T(8,128)S(1)}, f32[64,512]{1,0:T(8,128)S(1)}, u32[]{:S(2)}, u32[]{:S(2)}) collective-permute-start(f32[64,512]{1,0:T(8,128)S(1)} %far_terms.16.refs_0_), channel_id=1, source_target_pairs={{0,0},{4,4},{8,24},{12,28},{16,16},{20,20},{24,8},{28,12},{1,1},{5... | collective-permute-start | bytes 393224 | tf_op jit(solution)/shard_map/ppermute | solution.py:332
  40.9 6.9 %collective-permute-start.9 = (f32[64,512]{1,0:T(8,128)S(1)}, f32[64,512]{1,0:T(8,128)S(1)}, u32[]{:S(2)}, u32[]{:S(2)}) collective-permute-start(f32[64,512]{1,0:T(8,128)S(1)} %far_terms.17.refs_0_), channel_id=1, source_target_pairs={{0,16},{4,20},{8,8},{12,12},{16,0},{20,4},{24,24},{28,28},{1,17},{... | collective-permute-start | bytes 393224 | tf_op jit(solution)/shard_map/ppermute | solution.py:332
  45.0 2.8 %collective-permute-start.10 = (f32[64,512]{1,0:T(8,128)S(1)}, f32[64,512]{1,0:T(8,128)S(1)}, u32[]{:S(2)}, u32[]{:S(2)}) collective-permute-start(f32[64,512]{1,0:T(8,128)S(1)} %get-tuple-element.119), channel_id=1, source_target_pairs={{0,0},{4,4},{8,24},{12,28},{16,8},{20,12},{24,16},{28,20},{1,1},{5... | collective-permute-start | bytes 393224 | tf_op jit(solution)/shard_map/ppermute | solution.py:332
  47.1 12.1 %collective-permute-start.11 = (f32[64,512]{1,0:T(8,128)S(1)}, f32[64,512]{1,0:T(8,128)S(1)}, u32[]{:S(2)}, u32[]{:S(2)}) collective-permute-start(f32[64,512]{1,0:T(8,128)S(1)} %far_terms.18.refs_0_), channel_id=1, source_target_pairs={{0,0},{4,4},{8,24},{12,28},{16,16},{20,20},{24,8},{28,12},{1,1},{5... | collective-permute-start | bytes 393224 | tf_op jit(solution)/shard_map/ppermute | solution.py:332
  48.1 11.1 %collective-permute-start.12 = (f32[64,512]{1,0:T(8,128)S(1)}, f32[64,512]{1,0:T(8,128)S(1)}, u32[]{:S(2)}, u32[]{:S(2)}) collective-permute-start(f32[64,512]{1,0:T(8,128)S(1)} %get-tuple-element.121), channel_id=1, source_target_pairs={{0,16},{4,20},{8,0},{12,4},{16,8},{20,12},{24,24},{28,28},{1,17},{... | collective-permute-start | bytes 393224 | tf_op jit(solution)/shard_map/ppermute | solution.py:332
  55.3 6.9 %collective-permute-start.13 = (f32[64,512]{1,0:T(8,128)S(1)}, f32[64,512]{1,0:T(8,128)S(1)}, u32[]{:S(2)}, u32[]{:S(2)}) collective-permute-start(f32[64,512]{1,0:T(8,128)S(1)} %far_terms.19.refs_0_), channel_id=1, source_target_pairs={{0,16},{4,20},{8,8},{12,12},{16,0},{20,4},{24,24},{28,28},{1,17},{... | collective-permute-start | bytes 393224 | tf_op jit(solution)/shard_map/ppermute | solution.py:332
  59.5 7.0 %collective-permute-start.14 = (f32[64,512]{1,0:T(8,128)S(1)}, f32[64,512]{1,0:T(8,128)S(1)}, u32[]{:S(2)}, u32[]{:S(2)}) collective-permute-start(f32[64,512]{1,0:T(8,128)S(1)} %get-tuple-element.123), channel_id=1, source_target_pairs={{0,24},{4,28},{8,0},{12,4},{16,16},{20,20},{24,8},{28,12},{1,25},{... | collective-permute-start | bytes 393224 | tf_op jit(solution)/shard_map/ppermute | solution.py:332
  61.5 9.0 %copy-start.2 = (f32[1192,256]{1,0:T(8,128)S(1)}, f32[1192,256]{1,0:T(8,128)}, u32[]{:S(2)}) copy-start(f32[1192,256]{1,0:T(8,128)} %get-tuple-element.129.own.refs_6_) | copy-start | bytes 3661828
  66.8 8.9 %collective-permute-start.16 = (f32[64,512]{1,0:T(8,128)S(1)}, f32[64,512]{1,0:T(8,128)S(1)}, u32[]{:S(2)}, u32[]{:S(2)}) collective-permute-start(f32[64,512]{1,0:T(8,128)S(1)} %get-tuple-element.125), channel_id=1, source_target_pairs={{0,24},{4,28},{8,8},{12,12},{16,0},{20,4},{24,16},{28,20},{1,25},{... | collective-permute-start | bytes 393224 | tf_op jit(solution)/shard_map/ppermute | solution.py:332
  69.8 6.0 %collective-permute-start.15 = (f32[64,512]{1,0:T(8,128)S(1)}, f32[64,512]{1,0:T(8,128)S(1)}, u32[]{:S(2)}, u32[]{:S(2)}) collective-permute-start(f32[64,512]{1,0:T(8,128)S(1)} %far_terms.20.refs_0_), channel_id=1, source_target_pairs={{0,0},{4,4},{8,24},{12,28},{16,16},{20,20},{24,8},{28,12},{1,1},{5... | collective-permute-start | bytes 393224 | tf_op jit(solution)/shard_map/ppermute | solution.py:332
  72.0 6.9 %collective-permute-start.18 = (f32[64,512]{1,0:T(8,128)S(1)}, f32[64,512]{1,0:T(8,128)S(1)}, u32[]{:S(2)}, u32[]{:S(2)}) collective-permute-start(f32[64,512]{1,0:T(8,128)S(1)} %far_terms.21.refs_0_), channel_id=1, source_target_pairs={{0,16},{4,20},{8,8},{12,12},{16,0},{20,4},{24,24},{28,28},{1,17},{... | collective-permute-start | bytes 393224 | tf_op jit(solution)/shard_map/ppermute | solution.py:332
  76.1 2.8 %collective-permute-start.19 = (f32[64,512]{1,0:T(8,128)S(1)}, f32[64,512]{1,0:T(8,128)S(1)}, u32[]{:S(2)}, u32[]{:S(2)}) collective-permute-start(f32[64,512]{1,0:T(8,128)S(1)} %get-tuple-element.138), channel_id=1, source_target_pairs={{0,0},{4,4},{8,24},{12,28},{16,8},{20,12},{24,16},{28,20},{1,1},{5... | collective-permute-start | bytes 393224 | tf_op jit(solution)/shard_map/ppermute | solution.py:332
  78.2 12.1 %collective-permute-start.20 = (f32[64,512]{1,0:T(8,128)S(1)}, f32[64,512]{1,0:T(8,128)S(1)}, u32[]{:S(2)}, u32[]{:S(2)}) collective-permute-start(f32[64,512]{1,0:T(8,128)S(1)} %far_terms.22.refs_0_), channel_id=1, source_target_pairs={{0,0},{4,4},{8,24},{12,28},{16,16},{20,20},{24,8},{28,12},{1,1},{5... | collective-permute-start | bytes 393224 | tf_op jit(solution)/shard_map/ppermute | solution.py:332
  79.2 11.1 %collective-permute-start.21 = (f32[64,512]{1,0:T(8,128)S(1)}, f32[64,512]{1,0:T(8,128)S(1)}, u32[]{:S(2)}, u32[]{:S(2)}) collective-permute-start(f32[64,512]{1,0:T(8,128)S(1)} %get-tuple-element.140), channel_id=1, source_target_pairs={{0,16},{4,20},{8,0},{12,4},{16,8},{20,12},{24,24},{28,28},{1,17},{... | collective-permute-start | bytes 393224 | tf_op jit(solution)/shard_map/ppermute | solution.py:332
  86.4 6.9 %collective-permute-start.22 = (f32[64,512]{1,0:T(8,128)S(1)}, f32[64,512]{1,0:T(8,128)S(1)}, u32[]{:S(2)}, u32[]{:S(2)}) collective-permute-start(f32[64,512]{1,0:T(8,128)S(1)} %far_terms.23.refs_0_), channel_id=1, source_target_pairs={{0,16},{4,20},{8,8},{12,12},{16,0},{20,4},{24,24},{28,28},{1,17},{... | collective-permute-start | bytes 393224 | tf_op jit(solution)/shard_map/ppermute | solution.py:332
  90.6 7.1 %collective-permute-start.23 = (f32[64,512]{1,0:T(8,128)S(1)}, f32[64,512]{1,0:T(8,128)S(1)}, u32[]{:S(2)}, u32[]{:S(2)}) collective-permute-start(f32[64,512]{1,0:T(8,128)S(1)} %get-tuple-element.142), channel_id=1, source_target_pairs={{0,24},{4,28},{8,0},{12,4},{16,16},{20,20},{24,8},{28,12},{1,25},{... | collective-permute-start | bytes 393224 | tf_op jit(solution)/shard_map/ppermute | solution.py:332
  98.0 9.1 %collective-permute-start.25 = (f32[64,512]{1,0:T(8,128)S(1)}, f32[64,512]{1,0:T(8,128)S(1)}, u32[]{:S(2)}, u32[]{:S(2)}) collective-permute-start(f32[64,512]{1,0:T(8,128)S(1)} %get-tuple-element.144), channel_id=1, source_target_pairs={{0,24},{4,28},{8,8},{12,12},{16,0},{20,4},{24,16},{28,20},{1,25},{... | collective-permute-start | bytes 393224 | tf_op jit(solution)/shard_map/ppermute | solution.py:332
  101.8 5.4 %collective-permute-start.24 = (f32[64,512]{1,0:T(8,128)S(1)}, f32[64,512]{1,0:T(8,128)S(1)}, u32[]{:S(2)}, u32[]{:S(2)}) collective-permute-start(f32[64,512]{1,0:T(8,128)S(1)} %far_terms.24.refs_0_), channel_id=1, source_target_pairs={{0,0},{4,4},{8,24},{12,28},{16,16},{20,20},{24,8},{28,12},{1,1},{5... | collective-permute-start | bytes 393224 | tf_op jit(solution)/shard_map/ppermute | solution.py:332
  104.1 6.9 %collective-permute-start.27 = (f32[64,512]{1,0:T(8,128)S(1)}, f32[64,512]{1,0:T(8,128)S(1)}, u32[]{:S(2)}, u32[]{:S(2)}) collective-permute-start(f32[64,512]{1,0:T(8,128)S(1)} %far_terms.25.refs_0_), channel_id=1, source_target_pairs={{0,16},{4,20},{8,8},{12,12},{16,0},{20,4},{24,24},{28,28},{1,17},{... | collective-permute-start | bytes 393224 | tf_op jit(solution)/shard_map/ppermute | solution.py:332
  107.4 3.6 %collective-permute-start.28 = (f32[64,512]{1,0:T(8,128)S(1)}, f32[64,512]{1,0:T(8,128)S(1)}, u32[]{:S(2)}, u32[]{:S(2)}) collective-permute-start(f32[64,512]{1,0:T(8,128)S(1)} %get-tuple-element.157), channel_id=1, source_target_pairs={{0,0},{4,4},{8,24},{12,28},{16,8},{20,12},{24,16},{28,20},{1,1},{5... | collective-permute-start | bytes 393224 | tf_op jit(solution)/shard_map/ppermute | solution.py:332
  109.6 13.8 %collective-permute-start.29 = (f32[64,512]{1,0:T(8,128)S(1)}, f32[64,512]{1,0:T(8,128)S(1)}, u32[]{:S(2)}, u32[]{:S(2)}) collective-permute-start(f32[64,512]{1,0:T(8,128)S(1)} %far_terms.26.refs_0_), channel_id=1, source_target_pairs={{0,0},{4,4},{8,24},{12,28},{16,16},{20,20},{24,8},{28,12},{1,1},{5... | collective-permute-start | bytes 393224 | tf_op jit(solution)/shard_map/ppermute | solution.py:332
  111.3 12.1 %collective-permute-start.30 = (f32[64,512]{1,0:T(8,128)S(1)}, f32[64,512]{1,0:T(8,128)S(1)}, u32[]{:S(2)}, u32[]{:S(2)}) collective-permute-start(f32[64,512]{1,0:T(8,128)S(1)} %get-tuple-element.159), channel_id=1, source_target_pairs={{0,16},{4,20},{8,0},{12,4},{16,8},{20,12},{24,24},{28,28},{1,17},{... | collective-permute-start | bytes 393224 | tf_op jit(solution)/shard_map/ppermute | solution.py:332
  118.6 7.7 %collective-permute-start.31 = (f32[64,512]{1,0:T(8,128)S(1)}, f32[64,512]{1,0:T(8,128)S(1)}, u32[]{:S(2)}, u32[]{:S(2)}) collective-permute-start(f32[64,512]{1,0:T(8,128)S(1)} %far_terms.27.refs_0_), channel_id=1, source_target_pairs={{0,16},{4,20},{8,8},{12,12},{16,0},{20,4},{24,24},{28,28},{1,17},{... | collective-permute-start | bytes 393224 | tf_op jit(solution)/shard_map/ppermute | solution.py:332
  123.7 7.0 %collective-permute-start.32 = (f32[64,512]{1,0:T(8,128)S(1)}, f32[64,512]{1,0:T(8,128)S(1)}, u32[]{:S(2)}, u32[]{:S(2)}) collective-permute-start(f32[64,512]{1,0:T(8,128)S(1)} %get-tuple-element.161), channel_id=1, source_target_pairs={{0,24},{4,28},{8,0},{12,4},{16,16},{20,20},{24,8},{28,12},{1,25},{... | collective-permute-start | bytes 393224 | tf_op jit(solution)/shard_map/ppermute | solution.py:332
  125.7 8.1 %collective-permute-start.39 = (f32[64,256]{1,0:T(8,128)S(1)}, f32[64,256]{1,0:T(8,128)S(1)}, u32[]{:S(2)}, u32[]{:S(2)}) collective-permute-start(f32[64,256]{1,0:T(8,128)S(1)} %get-tuple-element.174), channel_id=1, source_target_pairs={{0,4},{4,0},{8,12},{12,8},{16,20},{20,16},{24,28},{28,24},{1,5},{5... | collective-permute-start | bytes 196616 | tf_op jit(solution)/shard_map/ppermute | solution.py:322
  125.7 8.1 %collective-permute-start.38 = (f32[64,256]{1,0:T(8,128)S(1)}, f32[64,256]{1,0:T(8,128)S(1)}, u32[]{:S(2)}, u32[]{:S(2)}) collective-permute-start(f32[64,256]{1,0:T(8,128)S(1)} %get-tuple-element.173), channel_id=1, source_target_pairs={{0,4},{4,0},{8,12},{12,8},{16,20},{20,16},{24,28},{28,24},{1,5},{5... | collective-permute-start | bytes 196616 | tf_op jit(solution)/shard_map/ppermute | solution.py:322
  126.2 9.1 %collective-permute-start.37 = (f32[64,256]{1,0:T(8,128)S(1)}, f32[64,256]{1,0:T(8,128)S(1)}, u32[]{:S(2)}, u32[]{:S(2)}) collective-permute-start(f32[64,256]{1,0:T(8,128)S(1)} %get-tuple-element.172), channel_id=1, source_target_pairs={{0,4},{4,0},{8,12},{12,8},{16,20},{20,16},{24,28},{28,24},{1,5},{5... | collective-permute-start | bytes 196616 | tf_op jit(solution)/shard_map/ppermute | solution.py:322
  131.6 3.7 %collective-permute-start.36 = (f32[64,256]{1,0:T(8,128)S(1)}, f32[64,256]{1,0:T(8,128)S(1)}, u32[]{:S(2)}, u32[]{:S(2)}) collective-permute-start(f32[64,256]{1,0:T(8,128)S(1)} %get-tuple-element.171), channel_id=1, source_target_pairs={{0,4},{4,0},{8,12},{12,8},{16,20},{20,16},{24,28},{28,24},{1,5},{5... | collective-permute-start | bytes 196616 | tf_op jit(solution)/shard_map/ppermute | solution.py:322
  131.7 4.9 %collective-permute-start.33 = (f32[64,128]{1,0:T(8,128)S(1)}, f32[64,128]{1,0:T(8,128)S(1)}, u32[]{:S(2)}, u32[]{:S(2)}) collective-permute-start(f32[64,128]{1,0:T(8,128)S(1)} %get-tuple-element.164), channel_id=1, source_target_pairs={{0,8},{4,12},{8,16},{12,20},{16,24},{20,28},{24,0},{28,4},{1,9},{5... | collective-permute-start | bytes 98312 | tf_op jit(solution)/shard_map/ppermute | solution.py:325
  133.8 3.9 %collective-permute-start.34 = (f32[64,128]{1,0:T(8,128)S(1)}, f32[64,128]{1,0:T(8,128)S(1)}, u32[]{:S(2)}, u32[]{:S(2)}) collective-permute-start(f32[64,128]{1,0:T(8,128)S(1)} %get-tuple-element.165), channel_id=1, source_target_pairs={{0,16},{4,20},{8,24},{12,28},{16,0},{20,4},{24,8},{28,12},{1,17},{... | collective-permute-start | bytes 98312 | tf_op jit(solution)/shard_map/ppermute | solution.py:325
  133.8 4.0 %collective-permute-start.35 = (f32[64,128]{1,0:T(8,128)S(1)}, f32[64,128]{1,0:T(8,128)S(1)}, u32[]{:S(2)}, u32[]{:S(2)}) collective-permute-start(f32[64,128]{1,0:T(8,128)S(1)} %get-tuple-element.166), channel_id=1, source_target_pairs={{0,24},{4,28},{8,0},{12,4},{16,8},{20,12},{24,16},{28,20},{1,25},{... | collective-permute-start | bytes 98312 | tf_op jit(solution)/shard_map/ppermute | solution.py:325
  137.8 1.2 collective-permute-start.40

commit v2 on v0

--- a/solution.py
+++ b/solution.py
@@ -61,35 +61,43 @@
 
 def pack_kernel(rows, cols, turnout, district, l_ref, d_ref, r_ref, *refs):
     outs = refs[: len(rows)]
-    held, sems = refs[len(rows) :]
+    held, passing, sems = refs[len(rows) :]
     slots, bs = l_ref.shape[2], l_ref.shape[3]
     columns = r_ref.shape[3]
-    rhs_at, col_at, turnout_at, district_at, _ = packed_places(slots, bs, columns)
-    copies = []
+    rhs_at, col_at, turnout_at, district_at, end = packed_places(slots, bs, columns)
+    places = [pl.ds(k * bs, bs) for k in range(slots + 1)]
+    tail = pl.ds(rhs_at, end - rhs_at)
+    made = []
 
     def copy(source, target):
-        copies.append(pltpu.make_async_copy(source, target, sems.at[len(copies)]))
-        copies[-1].start()
-
+        made.append(pltpu.make_async_copy(source, target, sems.at[len(made)]))
+        made[-1].start()
+        return made[-1]
+
+    arrivals = []
     for i, r in enumerate(rows):
-        copy(r_ref.at[r, 0], held.at[i])
-    for out, r in zip(outs, rows):
-        for k in range(slots):
-            copy(l_ref.at[r, 0, k], out.at[pl.ds(k * bs, bs)])
-        copy(d_ref.at[r, 0], out.at[pl.ds(slots * bs, bs)])
-    for out, r in zip(outs, rows):
+        blocks = [l_ref.at[r, 0, k] for k in range(slots)] + [d_ref.at[r, 0]]
+        first = copy(r_ref.at[r, 0], held.at[i])
+        rest = [copy(x, passing.at[i, at]) for x, at in zip(blocks, places)]
+        arrivals.append((first, rest))
+    for i, r in enumerate(rows):
         for k in range(slots):
             at = col_at + 8 * k
-            out[at : at + 8] = jnp.full((8, bs), cols[k, 0, r].astype(F32))
-        out[turnout_at : turnout_at + 8] = jnp.broadcast_to(turnout[r], (8, bs))
-        out[district_at : district_at + 8] = jnp.broadcast_to(
+            passing[i, at : at + 8] = jnp.full((8, bs), cols[k, 0, r].astype(F32))
+        passing[i, turnout_at : turnout_at + 8] = jnp.broadcast_to(turnout[r], (8, bs))
+        passing[i, district_at : district_at + 8] = jnp.broadcast_to(
             district[r].astype(F32), (8, bs)
         )
-    for i, out in enumerate(outs):
-        copies[i].wait()
-        out[rhs_at:col_at] = held[i].T
-    for started in copies[len(rows) :]:
-        started.wait()
+    leaving = []
+    for i, (first, rest) in enumerate(arrivals):
+        first.wait()
+        passing[i, rhs_at:col_at] = held[i].T
+        leaving.append(copy(passing.at[i, tail], outs[i].at[tail]))
+        for arriving, at in zip(rest, places):
+            arriving.wait()
+            leaving.append(copy(passing.at[i, at], outs[i].at[at]))
+    for x in leaving:
+        x.wait()
 
 
 def put(high, low, i, j, value):
@@ -311,7 +319,7 @@
             kernel,
             out_shape=outs,
             in_specs=more.pop("in_specs", [VMEM_SPEC] * len(operands)),
-            out_specs=(VMEM_SPEC,) * len(outs) if several else VMEM_SPEC,
+            out_specs=more.pop("out_specs", (VMEM_SPEC,) * len(outs) if several else VMEM_SPEC),
             compiler_params=params(mib),
             cost_estimate=cost(flops, moved),
             name=name,
@@ -341,9 +349,11 @@
             56,
             moved=8 * packed_rows * bs * len(rows),
             in_specs=[SMEM_SPEC, VMEM_SPEC, VMEM_SPEC] + [HBM_SPEC] * 3,
+            out_specs=(HBM_SPEC,) * len(rows),
             scratch_shapes=[
                 pltpu.VMEM((len(rows), bs, columns), F32),
-                pltpu.SemaphoreType.DMA((len(rows) * (slots + 2),)),
+                pltpu.VMEM((len(rows), packed_rows, bs), F32),
+                pltpu.SemaphoreType.DMA((len(rows) * (2 * slots + 4),)),
             ],
         )
 

time: 112 us -> 111 us (level)
  no operation moved by 1% of the time
where the time goes in v2:
time: 111 us; the launch traced here: 110 us
  waiting for transfers between devices  44.8 us (40%)
  starting transfers between devices  33.6 us (30%)
  Pallas kernels  29.8 us (27%)
  between operations  1.49 us (1%)
    ppermute x29, waiting for transfers between devices, pass_on(): return lax.ppermute(x, 'blk', perm)  42.2 us
    pallas_call x47, Pallas kernels, call(): pl.pallas_call(kernel, out_shape=outs, in_specs=more.pop('in_specs', [VME...  29.8 us
    ppermute x29, starting transfers between devices, pass_on(): return lax.ppermute(x, 'blk', perm)  28.5 us
    ppermute x3, starting transfers between devices, shift(): return lax.ppermute(x, 'blk', [(i, (i + 2 * by) % n) for i in range(n)])  3 us
  transfers between devices with their start and end apart: 41, of which 11 were waited for; matrix products, arithmetic and copies ran while one was open for 0% of the time, Pallas kernels for 24%

profile of v2, /device:TPU:0, one launch (start us, length us, event | category | flops | bytes accessed | tf_op | source)
XLA Modules:
  0.0 109.7 jit_solution(5330178222442284579)
XLA Ops:
  0.6 2.9 %pack.2.own.refs_6_ = f32[1192,256]{1,0:T(8,128)} custom-call(s32[3,1,4]{2,1,0:T(1,128)} %bitcast.1, f32[4,1,256]{2,1,0:T(1,128)} %turnout.2, s32[4,1,256]{2,1,0:T(1,128)} %district.3, f32[4,1,3,256,256]{4,3,2,1,0:T(8,128)} %l_ref.3, f32[4,1,256,256]{3,2,1,0:T(8,128)} %d_ref.3, f32[4,1,256,128]{3,2,1,0:T(8,128)} %r_ref.3), custom_call_target="tpu_custom_call" | custom-call | bytes 2441216 | tf_op jit(solution)/shard_map/pack/pallas_call | solution.py:318
  4.1 3.8 %pack.3 = (f32[1192,256]{1,0:T(8,128)}, f32[1192,256]{1,0:T(8,128)}, f32[1192,256]{1,0:T(8,128)}) custom-call(s32[3,1,4]{2,1,0:T(1,128)} %bitcast.2, f32[4,1,256]{2,1,0:T(1,128)} %turnout.2, s32[4,1,256]{2,1,0:T(1,128)} %district.3, f32[4,1,3,256,256]{4,3,2,1,0:T(8,128)} %l_ref.3, f32[4,1,256,256]{3,2,1,0:T(8,128)} %d_ref.3, f32[4,1,256,128]{3,2,1,0:T(8,128)} %r_ref.3), custom_call_target="tpu_custom_call" | custom-call | bytes 7323648 | tf_op jit(solution)/shard_map/pack/pallas_call | solution.py:318
  8.5 1.2 %near_setup.4 = (bf16[512,512]{1,0:T(8,128)(2,1)S(1)}, bf16[512,512]{1,0:T(8,128)(2,1)S(1)}, bf16[4,256,256]{2,1,0:T(8,128)(2,1)S(1)}, bf16[4,256,256]{2,1,0:T(8,128)(2,1)S(1)}, f32[64,512]{1,0:T(8,128)S(1)}) custom-call(f32[1192,256]{1,0:T(8,128)S(1)} %copy-done, f32[1192,256]{1,0:T(8,128)S(1)} %collective-permute-done.oth.refs_7_), custom_call_target="tpu_custom_call" | custom-call | flops 704643072 | bytes 6291456 | tf_op jit(solution)/shard_map/near_setup/pallas_call | solution.py:318
  10.0 0.7 collective-permute-start.1
  10.6 1.2 %far_setup.4 = (bf16[512,512]{1,0:T(8,128)(2,1)S(1)}, bf16[512,512]{1,0:T(8,128)(2,1)S(1)}) custom-call(f32[1192,256]{1,0:T(8,128)S(1)} %copy-done, f32[1192,256]{1,0:T(8,128)S(1)} %collective-permute-done.oth.refs_7_, bf16[4,256,256]{2,1,0:T(8,128)(2,1)S(1)} %get-tuple-element.96.mh.refs_4_, bf16[4,256,256]{2,1,0:T(8,128)(2,1)S(1)} %get-tuple-element.97.ml.refs_5_), custom_call_target="tpu_custom_call" | custom-call | flops 503316480 | bytes 6291456 | tf_op jit(solution)/shard_map/far_setup/pallas_call | solution.py:318
  12.2 0.7 collective-permute-start.2
  13.1 0.7 collective-permute-start.3
  14.1 1.4 %collective-permute-start.4 = (f32[64,512]{1,0:T(8,128)S(1)}, f32[64,512]{1,0:T(8,128)S(1)}, u32[]{:S(2)}, u32[]{:S(2)}) collective-permute-start(f32[64,512]{1,0:T(8,128)S(1)} %far_terms.15.refs_0_), channel_id=1, source_target_pairs={{16,0},{20,4},{17,1},{21,5},{18,2},{22,6},{19,3},{23,7}} | collective-permute-start | bytes 393224 | tf_op jit(solution)/shard_map/ppermute | solution.py:341
  15.9 1.3 %collective-permute-start.5 = (f32[64,512]{1,0:T(8,128)S(1)}, f32[64,512]{1,0:T(8,128)S(1)}, u32[]{:S(2)}, u32[]{:S(2)}) collective-permute-start(f32[64,512]{1,0:T(8,128)S(1)} %get-tuple-element.104), channel_id=1, source_target_pairs={{8,0},{12,4},{9,1},{13,5},{10,2},{14,6},{11,3},{15,7}} | collective-permute-start | bytes 393224 | tf_op jit(solution)/shard_map/ppermute | solution.py:341
  17.7 9.1 %collective-permute-done.4.refs_1_ = f32[64,512]{1,0:T(8,128)S(1)} collective-permute-done((f32[64,512]{1,0:T(8,128)S(1)}, f32[64,512]{1,0:T(8,128)S(1)}, u32[]{:S(2)}, u32[]{:S(2)}) %collective-permute-start.4) | collective-permute-done | bytes 131104 | tf_op jit(solution)/shard_map/ppermute | solution.py:341
  26.8 4.2 %collective-permute-done.5.refs_2_ = f32[64,512]{1,0:T(8,128)S(1)} collective-permute-done((f32[64,512]{1,0:T(8,128)S(1)}, f32[64,512]{1,0:T(8,128)S(1)}, u32[]{:S(2)}, u32[]{:S(2)}) %collective-permute-start.5) | collective-permute-done | bytes 131104 | tf_op jit(solution)/shard_map/ppermute | solution.py:341
  31.4 1.3 %collective-permute-start.7 = (f32[64,512]{1,0:T(8,128)S(1)}, f32[64,512]{1,0:T(8,128)S(1)}, u32[]{:S(2)}, u32[]{:S(2)}) collective-permute-start(f32[64,512]{1,0:T(8,128)S(1)} %get-tuple-element.106), channel_id=1, source_target_pairs={{0,24},{4,28},{1,25},{5,29},{2,26},{6,30},{3,27},{7,31}} | collective-permute-start | bytes 393224 | tf_op jit(solution)/shard_map/ppermute | solution.py:341
  32.7 0.7 collective-permute-start.6
  33.4 1.2 %near_setup.5 = (bf16[512,512]{1,0:T(8,128)(2,1)S(1)}, bf16[512,512]{1,0:T(8,128)(2,1)S(1)}, bf16[4,256,256]{2,1,0:T(8,128)(2,1)S(1)}, bf16[4,256,256]{2,1,0:T(8,128)(2,1)S(1)}, f32[64,512]{1,0:T(8,128)S(1)}) custom-call(f32[1192,256]{1,0:T(8,128)S(1)} %copy-done.3, f32[1192,256]{1,0:T(8,128)S(1)} %collective-permute-done.8.oth.refs_7_), custom_call_target="tpu_custom_call" | custom-call | flops 704643072 | bytes 6291456 | tf_op jit(solution)/shard_map/near_setup/pallas_call | solution.py:318
  34.9 1.3 %collective-permute-start.9 = (f32[64,512]{1,0:T(8,128)S(1)}, f32[64,512]{1,0:T(8,128)S(1)}, u32[]{:S(2)}, u32[]{:S(2)}) collective-permute-start(f32[64,512]{1,0:T(8,128)S(1)} %far_terms.17.refs_0_), channel_id=1, source_target_pairs={{0,16},{4,20},{1,17},{5,21},{2,18},{6,22},{3,19},{7,23}} | collective-permute-start | bytes 393224 | tf_op jit(solution)/shard_map/ppermute | solution.py:341
  36.2 0.9 finish.4
  38.0 1.2 %far_setup.5 = (bf16[512,512]{1,0:T(8,128)(2,1)S(1)}, bf16[512,512]{1,0:T(8,128)(2,1)S(1)}) custom-call(f32[1192,256]{1,0:T(8,128)S(1)} %copy-done.3, f32[1192,256]{1,0:T(8,128)S(1)} %collective-permute-done.8.oth.refs_7_, bf16[4,256,256]{2,1,0:T(8,128)(2,1)S(1)} %get-tuple-element.115.mh.refs_4_, bf16[4,256,256]{2,1,0:T(8,128)(2,1)S(1)} %get-tuple-element.116.ml.refs_5_), custom_call_target="tpu_custom_call" | custom-call | flops 503316480 | bytes 6291456 | tf_op jit(solution)/shard_map/far_setup/pallas_call | solution.py:318
  40.5 0.7 collective-permute-start.12
  41.4 1.3 %collective-permute-start.13 = (f32[64,512]{1,0:T(8,128)S(1)}, f32[64,512]{1,0:T(8,128)S(1)}, u32[]{:S(2)}, u32[]{:S(2)}) collective-permute-start(f32[64,512]{1,0:T(8,128)S(1)} %far_terms.19.refs_0_), channel_id=1, source_target_pairs={{16,0},{20,4},{17,1},{21,5},{18,2},{22,6},{19,3},{23,7}} | collective-permute-start | bytes 393224 | tf_op jit(solution)/shard_map/ppermute | solution.py:341
  43.1 1.3 %collective-permute-start.14 = (f32[64,512]{1,0:T(8,128)S(1)}, f32[64,512]{1,0:T(8,128)S(1)}, u32[]{:S(2)}, u32[]{:S(2)}) collective-permute-start(f32[64,512]{1,0:T(8,128)S(1)} %get-tuple-element.123), channel_id=1, source_target_pairs={{8,0},{12,4},{9,1},{13,5},{10,2},{14,6},{11,3},{15,7}} | collective-permute-start | bytes 393224 | tf_op jit(solution)/shard_map/ppermute | solution.py:341
  44.7 5.7 %collective-permute-done.13.refs_1_ = f32[64,512]{1,0:T(8,128)S(1)} collective-permute-done((f32[64,512]{1,0:T(8,128)S(1)}, f32[64,512]{1,0:T(8,128)S(1)}, u32[]{:S(2)}, u32[]{:S(2)}) %collective-permute-start.13) | collective-permute-done | bytes 131104 | tf_op jit(solution)/shard_map/ppermute | solution.py:341
  50.4 4.4 %collective-permute-done.14.refs_2_ = f32[64,512]{1,0:T(8,128)S(1)} collective-permute-done((f32[64,512]{1,0:T(8,128)S(1)}, f32[64,512]{1,0:T(8,128)S(1)}, u32[]{:S(2)}, u32[]{:S(2)}) %collective-permute-start.14) | collective-permute-done | bytes 131104 | tf_op jit(solution)/shard_map/ppermute | solution.py:341
  55.1 1.3 %collective-permute-start.16 = (f32[64,512]{1,0:T(8,128)S(1)}, f32[64,512]{1,0:T(8,128)S(1)}, u32[]{:S(2)}, u32[]{:S(2)}) collective-permute-start(f32[64,512]{1,0:T(8,128)S(1)} %get-tuple-element.125), channel_id=1, source_target_pairs={{0,24},{4,28},{1,25},{5,29},{2,26},{6,30},{3,27},{7,31}} | collective-permute-start | bytes 393224 | tf_op jit(solution)/shard_map/ppermute | solution.py:341
  56.4 0.7 collective-permute-start.15
  57.1 1.2 %near_setup.6 = (bf16[512,512]{1,0:T(8,128)(2,1)S(1)}, bf16[512,512]{1,0:T(8,128)(2,1)S(1)}, bf16[4,256,256]{2,1,0:T(8,128)(2,1)S(1)}, bf16[4,256,256]{2,1,0:T(8,128)(2,1)S(1)}, f32[64,512]{1,0:T(8,128)S(1)}) custom-call(f32[1192,256]{1,0:T(8,128)S(1)} %copy-done.2, f32[1192,256]{1,0:T(8,128)S(1)} %collective-permute-done.17.oth.refs_7_), custom_call_target="tpu_custom_call" | custom-call | flops 704643072 | bytes 6291456 | tf_op jit(solution)/shard_map/near_setup/pallas_call | solution.py:318
  58.6 1.3 %collective-permute-start.18 = (f32[64,512]{1,0:T(8,128)S(1)}, f32[64,512]{1,0:T(8,128)S(1)}, u32[]{:S(2)}, u32[]{:S(2)}) collective-permute-start(f32[64,512]{1,0:T(8,128)S(1)} %far_terms.21.refs_0_), channel_id=1, source_target_pairs={{0,16},{4,20},{1,17},{5,21},{2,18},{6,22},{3,19},{7,23}} | collective-permute-start | bytes 393224 | tf_op jit(solution)/shard_map/ppermute | solution.py:341
  59.9 0.9 finish.5
  61.8 1.2 %far_setup.6 = (bf16[512,512]{1,0:T(8,128)(2,1)S(1)}, bf16[512,512]{1,0:T(8,128)(2,1)S(1)}) custom-call(f32[1192,256]{1,0:T(8,128)S(1)} %copy-done.2, f32[1192,256]{1,0:T(8,128)S(1)} %collective-permute-done.17.oth.refs_7_, bf16[4,256,256]{2,1,0:T(8,128)(2,1)S(1)} %get-tuple-element.134.mh.refs_4_, bf16[4,256,256]{2,1,0:T(8,128)(2,1)S(1)} %get-tuple-element.135.ml.refs_5_), custom_call_target="tpu_custom_call" | custom-call | flops 503316480 | bytes 6291456 | tf_op jit(solution)/shard_map/far_setup/pallas_call | solution.py:318
  65.2 1.3 %collective-permute-start.22 = (f32[64,512]{1,0:T(8,128)S(1)}, f32[64,512]{1,0:T(8,128)S(1)}, u32[]{:S(2)}, u32[]{:S(2)}) collective-permute-start(f32[64,512]{1,0:T(8,128)S(1)} %far_terms.23.refs_0_), channel_id=1, source_target_pairs={{16,0},{20,4},{17,1},{21,5},{18,2},{22,6},{19,3},{23,7}} | collective-permute-start | bytes 393224 | tf_op jit(solution)/shard_map/ppermute | solution.py:341
  66.8 1.3 %collective-permute-start.23 = (f32[64,512]{1,0:T(8,128)S(1)}, f32[64,512]{1,0:T(8,128)S(1)}, u32[]{:S(2)}, u32[]{:S(2)}) collective-permute-start(f32[64,512]{1,0:T(8,128)S(1)} %get-tuple-element.142), channel_id=1, source_target_pairs={{8,0},{12,4},{9,1},{13,5},{10,2},{14,6},{11,3},{15,7}} | collective-permute-start | bytes 393224 | tf_op jit(solution)/shard_map/ppermute | solution.py:341
  68.4 5.2 %collective-permute-done.22.refs_1_ = f32[64,512]{1,0:T(8,128)S(1)} collective-permute-done((f32[64,512]{1,0:T(8,128)S(1)}, f32[64,512]{1,0:T(8,128)S(1)}, u32[]{:S(2)}, u32[]{:S(2)}) %collective-permute-start.22) | collective-permute-done | bytes 131104 | tf_op jit(solution)/shard_map/ppermute | solution.py:341
  73.6 4.4 %collective-permute-done.23.refs_2_ = f32[64,512]{1,0:T(8,128)S(1)} collective-permute-done((f32[64,512]{1,0:T(8,128)S(1)}, f32[64,512]{1,0:T(8,128)S(1)}, u32[]{:S(2)}, u32[]{:S(2)}) %collective-permute-start.23) | collective-permute-done | bytes 131104 | tf_op jit(solution)/shard_map/ppermute | solution.py:341
  78.3 1.3 %collective-permute-start.25 = (f32[64,512]{1,0:T(8,128)S(1)}, f32[64,512]{1,0:T(8,128)S(1)}, u32[]{:S(2)}, u32[]{:S(2)}) collective-permute-start(f32[64,512]{1,0:T(8,128)S(1)} %get-tuple-element.144), channel_id=1, source_target_pairs={{0,24},{4,28},{1,25},{5,29},{2,26},{6,30},{3,27},{7,31}} | collective-permute-start | bytes 393224 | tf_op jit(solution)/shard_map/ppermute | solution.py:341
  79.6 0.8 collective-permute-start.24
  80.5 1.2 %near_setup.7 = (bf16[512,512]{1,0:T(8,128)(2,1)S(1)}, bf16[512,512]{1,0:T(8,128)(2,1)S(1)}, bf16[4,256,256]{2,1,0:T(8,128)(2,1)S(1)}, bf16[4,256,256]{2,1,0:T(8,128)(2,1)S(1)}, f32[64,512]{1,0:T(8,128)S(1)}) custom-call(f32[1192,256]{1,0:T(8,128)S(1)} %copy-done.1, f32[1192,256]{1,0:T(8,128)S(1)} %collective-permute-done.26.oth.refs_7_), custom_call_target="tpu_custom_call" | custom-call | flops 704643072 | bytes 6291456 | tf_op jit(solution)/shard_map/near_setup/pallas_call | solution.py:318
  82.0 1.3 %collective-permute-start.27 = (f32[64,512]{1,0:T(8,128)S(1)}, f32[64,512]{1,0:T(8,128)S(1)}, u32[]{:S(2)}, u32[]{:S(2)}) collective-permute-start(f32[64,512]{1,0:T(8,128)S(1)} %far_terms.25.refs_0_), channel_id=1, source_target_pairs={{0,16},{4,20},{1,17},{5,21},{2,18},{6,22},{3,19},{7,23}} | collective-permute-start | bytes 393224 | tf_op jit(solution)/shard_map/ppermute | solution.py:341
  83.3 0.9 finish.6
  85.1 1.2 %far_setup.7 = (bf16[512,512]{1,0:T(8,128)(2,1)S(1)}, bf16[512,512]{1,0:T(8,128)(2,1)S(1)}) custom-call(f32[1192,256]{1,0:T(8,128)S(1)} %copy-done.1, f32[1192,256]{1,0:T(8,128)S(1)} %collective-permute-done.26.oth.refs_7_, bf16[4,256,256]{2,1,0:T(8,128)(2,1)S(1)} %get-tuple-element.153.mh.refs_4_, bf16[4,256,256]{2,1,0:T(8,128)(2,1)S(1)} %get-tuple-element.154.ml.refs_5_), custom_call_target="tpu_custom_call" | custom-call | flops 503316480 | bytes 6291456 | tf_op jit(solution)/shard_map/far_setup/pallas_call | solution.py:318
  88.6 1.3 %collective-permute-start.31 = (f32[64,512]{1,0:T(8,128)S(1)}, f32[64,512]{1,0:T(8,128)S(1)}, u32[]{:S(2)}, u32[]{:S(2)}) collective-permute-start(f32[64,512]{1,0:T(8,128)S(1)} %far_terms.27.refs_0_), channel_id=1, source_target_pairs={{16,0},{20,4},{17,1},{21,5},{18,2},{22,6},{19,3},{23,7}} | collective-permute-start | bytes 393224 | tf_op jit(solution)/shard_map/ppermute | solution.py:341
  90.2 1.3 %collective-permute-start.32 = (f32[64,512]{1,0:T(8,128)S(1)}, f32[64,512]{1,0:T(8,128)S(1)}, u32[]{:S(2)}, u32[]{:S(2)}) collective-permute-start(f32[64,512]{1,0:T(8,128)S(1)} %get-tuple-element.161), channel_id=1, source_target_pairs={{8,0},{12,4},{9,1},{13,5},{10,2},{14,6},{11,3},{15,7}} | collective-permute-start | bytes 393224 | tf_op jit(solution)/shard_map/ppermute | solution.py:341
  92.1 4.7 %collective-permute-done.31.refs_0_ = f32[64,512]{1,0:T(8,128)S(1)} collective-permute-done((f32[64,512]{1,0:T(8,128)S(1)}, f32[64,512]{1,0:T(8,128)S(1)}, u32[]{:S(2)}, u32[]{:S(2)}) %collective-permute-start.31) | collective-permute-done | bytes 131104 | tf_op jit(solution)/shard_map/ppermute | solution.py:341
  96.8 4.4 %collective-permute-done.32.refs_1_ = f32[64,512]{1,0:T(8,128)S(1)} collective-permute-done((f32[64,512]{1,0:T(8,128)S(1)}, f32[64,512]{1,0:T(8,128)S(1)}, u32[]{:S(2)}, u32[]{:S(2)}) %collective-permute-start.32) | collective-permute-done | bytes 131104 | tf_op jit(solution)/shard_map/ppermute | solution.py:341
  101.2 0.9 finish.7
  102.4 2.9 %collective-permute-start.35 = (f32[64,128]{1,0:T(8,128)S(1)}, f32[64,128]{1,0:T(8,128)S(1)}, u32[]{:S(2)}, u32[]{:S(2)}) collective-permute-start(f32[64,128]{1,0:T(8,128)S(1)} %get-tuple-element.166), channel_id=1, source_target_pairs={{0,24},{4,28},{8,0},{12,4},{16,8},{20,12},{24,16},{28,20},{1,25},{... | collective-permute-start | bytes 98312 | tf_op jit(solution)/shard_map/ppermute | solution.py:333
  105.2 1.0 field.1
  106.2 1.0 collective-permute-done.33.refs_1_
  107.7 1.2 %collective-permute-done.40.got = f32[32,128]{1,0:T(8,128)S(1)} collective-permute-done((f32[32,128]{1,0:T(8,128)S(1)}, f32[32,128]{1,0:T(8,128)S(1)}, u32[]{:S(2)}, u32[]{:S(2)}) %collective-permute-start.40) | collective-permute-done | bytes 16416 | tf_op jit(solution)/shard_map/ppermute | solution.py:330
  108.9 0.8 district_mean.1
  (89 shorter events, 16.4 us)
Async XLA Ops:
  3.5 5.0 %copy-start = (f32[1192,256]{1,0:T(8,128)S(1)}, f32[1192,256]{1,0:T(8,128)}, u32[]{:S(2)}) copy-start(f32[1192,256]{1,0:T(8,128)} %pack.2.own.refs_6_) | copy-start | bytes 3661828
  3.5 4.9 %collective-permute-start = (f32[1192,256]{1,0:T(8,128)}, f32[1192,256]{1,0:T(8,128)S(1)}, u32[]{:S(2)}, u32[]{:S(2)}) collective-permute-start(f32[1192,256]{1,0:T(8,128)} %pack.2.own.refs_6_), channel_id=1, source_target_pairs={{0,4},{4,0},{8,12},{12,8},{16,20},{20,16},{24,28},{28,24},{1,5},{5... | collective-permute-start | bytes 3661832 | tf_op jit(solution)/shard_map/ppermute | solution.py:330
  7.9 25.4 %collective-permute-start.8 = (f32[1192,256]{1,0:T(8,128)}, f32[1192,256]{1,0:T(8,128)S(1)}, u32[]{:S(2)}, u32[]{:S(2)}) collective-permute-start(f32[1192,256]{1,0:T(8,128)} %get-tuple-element.110.own.refs_6_), channel_id=1, source_target_pairs={{0,4},{4,0},{8,12},{12,8},{16,20},{20,16},{24,28},{28,24},{1,5},{5... | collective-permute-start | bytes 3661832 | tf_op jit(solution)/shard_map/ppermute | solution.py:330
  8.1 48.9 %collective-permute-start.17 = (f32[1192,256]{1,0:T(8,128)}, f32[1192,256]{1,0:T(8,128)S(1)}, u32[]{:S(2)}, u32[]{:S(2)}) collective-permute-start(f32[1192,256]{1,0:T(8,128)} %get-tuple-element.129.own.refs_6_), channel_id=1, source_target_pairs={{0,4},{4,0},{8,12},{12,8},{16,20},{20,16},{24,28},{28,24},{1,5},{5... | collective-permute-start | bytes 3661832 | tf_op jit(solution)/shard_map/ppermute | solution.py:330
  10.0 2.9 %collective-permute-start.1 = (f32[64,512]{1,0:T(8,128)S(1)}, f32[64,512]{1,0:T(8,128)S(1)}, u32[]{:S(2)}, u32[]{:S(2)}) collective-permute-start(f32[64,512]{1,0:T(8,128)S(1)} %get-tuple-element.100), channel_id=1, source_target_pairs={{24,16},{28,20},{25,17},{29,21},{26,18},{30,22},{27,19},{31,23}} | collective-permute-start | bytes 393224 | tf_op jit(solution)/shard_map/ppermute | solution.py:341
  12.2 3.4 %collective-permute-start.2 = (f32[64,512]{1,0:T(8,128)S(1)}, f32[64,512]{1,0:T(8,128)S(1)}, u32[]{:S(2)}, u32[]{:S(2)}) collective-permute-start(f32[64,512]{1,0:T(8,128)S(1)} %far_terms.14.refs_0_), channel_id=1, source_target_pairs={{24,8},{28,12},{25,9},{29,13},{26,10},{30,14},{27,11},{31,15}} | collective-permute-start | bytes 393224 | tf_op jit(solution)/shard_map/ppermute | solution.py:341
  13.1 2.4 %collective-permute-start.3 = (f32[64,512]{1,0:T(8,128)S(1)}, f32[64,512]{1,0:T(8,128)S(1)}, u32[]{:S(2)}, u32[]{:S(2)}) collective-permute-start(f32[64,512]{1,0:T(8,128)S(1)} %get-tuple-element.102), channel_id=1, source_target_pairs={{16,8},{20,12},{17,9},{21,13},{18,10},{22,14},{19,11},{23,15}} | collective-permute-start | bytes 393224 | tf_op jit(solution)/shard_map/ppermute | solution.py:341
  13.8 3.3 %copy-start.1 = (f32[1192,256]{1,0:T(8,128)S(1)}, f32[1192,256]{1,0:T(8,128)}, u32[]{:S(2)}) copy-start(f32[1192,256]{1,0:T(8,128)} %get-tuple-element.148.own.refs_6_) | copy-start | bytes 3661828
  14.1 12.7 %collective-permute-start.4 = (f32[64,512]{1,0:T(8,128)S(1)}, f32[64,512]{1,0:T(8,128)S(1)}, u32[]{:S(2)}, u32[]{:S(2)}) collective-permute-start(f32[64,512]{1,0:T(8,128)S(1)} %far_terms.15.refs_0_), channel_id=1, source_target_pairs={{16,0},{20,4},{17,1},{21,5},{18,2},{22,6},{19,3},{23,7}} | collective-permute-start | bytes 393224 | tf_op jit(solution)/shard_map/ppermute | solution.py:341
  15.9 15.2 %collective-permute-start.5 = (f32[64,512]{1,0:T(8,128)S(1)}, f32[64,512]{1,0:T(8,128)S(1)}, u32[]{:S(2)}, u32[]{:S(2)}) collective-permute-start(f32[64,512]{1,0:T(8,128)S(1)} %get-tuple-element.104), channel_id=1, source_target_pairs={{8,0},{12,4},{9,1},{13,5},{10,2},{14,6},{11,3},{15,7}} | collective-permute-start | bytes 393224 | tf_op jit(solution)/shard_map/ppermute | solution.py:341
  17.2 63.3 %collective-permute-start.26 = (f32[1192,256]{1,0:T(8,128)S(1)}, f32[1192,256]{1,0:T(8,128)S(1)}, u32[]{:S(2)}, u32[]{:S(2)}) collective-permute-start(f32[1192,256]{1,0:T(8,128)S(1)} %copy-done.1), channel_id=1, source_target_pairs={{0,4},{4,0},{8,12},{12,8},{16,20},{20,16},{24,28},{28,24},{1,5},{5... | collective-permute-start | bytes 3661832 | tf_op jit(solution)/shard_map/ppermute | solution.py:330
  17.4 15.9 %copy-start.3 = (f32[1192,256]{1,0:T(8,128)S(1)}, f32[1192,256]{1,0:T(8,128)}, u32[]{:S(2)}) copy-start(f32[1192,256]{1,0:T(8,128)} %get-tuple-element.110.own.refs_6_) | copy-start | bytes 3661828
  31.4 5.7 %collective-permute-start.7 = (f32[64,512]{1,0:T(8,128)S(1)}, f32[64,512]{1,0:T(8,128)S(1)}, u32[]{:S(2)}, u32[]{:S(2)}) collective-permute-start(f32[64,512]{1,0:T(8,128)S(1)} %get-tuple-element.106), channel_id=1, source_target_pairs={{0,24},{4,28},{1,25},{5,29},{2,26},{6,30},{3,27},{7,31}} | collective-permute-start | bytes 393224 | tf_op jit(solution)/shard_map/ppermute | solution.py:341
  32.7 4.4 %collective-permute-start.6 = (f32[64,512]{1,0:T(8,128)S(1)}, f32[64,512]{1,0:T(8,128)S(1)}, u32[]{:S(2)}, u32[]{:S(2)}) collective-permute-start(f32[64,512]{1,0:T(8,128)S(1)} %far_terms.16.refs_0_), channel_id=1, source_target_pairs={{8,24},{12,28},{9,25},{13,29},{10,26},{14,30},{11,27},{15,31}} | collective-permute-start | bytes 393224 | tf_op jit(solution)/shard_map/ppermute | solution.py:341
  34.9 5.3 %collective-permute-start.9 = (f32[64,512]{1,0:T(8,128)S(1)}, f32[64,512]{1,0:T(8,128)S(1)}, u32[]{:S(2)}, u32[]{:S(2)}) collective-permute-start(f32[64,512]{1,0:T(8,128)S(1)} %far_terms.17.refs_0_), channel_id=1, source_target_pairs={{0,16},{4,20},{1,17},{5,21},{2,18},{6,22},{3,19},{7,23}} | collective-permute-start | bytes 393224 | tf_op jit(solution)/shard_map/ppermute | solution.py:341
  37.3 2.8 %collective-permute-start.10 = (f32[64,512]{1,0:T(8,128)S(1)}, f32[64,512]{1,0:T(8,128)S(1)}, u32[]{:S(2)}, u32[]{:S(2)}) collective-permute-start(f32[64,512]{1,0:T(8,128)S(1)} %get-tuple-element.119), channel_id=1, source_target_pairs={{24,16},{28,20},{25,17},{29,21},{26,18},{30,22},{27,19},{31,23}} | collective-permute-start | bytes 393224 | tf_op jit(solution)/shard_map/ppermute | solution.py:341
  39.5 3.3 %collective-permute-start.11 = (f32[64,512]{1,0:T(8,128)S(1)}, f32[64,512]{1,0:T(8,128)S(1)}, u32[]{:S(2)}, u32[]{:S(2)}) collective-permute-start(f32[64,512]{1,0:T(8,128)S(1)} %far_terms.18.refs_0_), channel_id=1, source_target_pairs={{24,8},{28,12},{25,9},{29,13},{26,10},{30,14},{27,11},{31,15}} | collective-permute-start | bytes 393224 | tf_op jit(solution)/shard_map/ppermute | solution.py:341
  40.5 2.3 %collective-permute-start.12 = (f32[64,512]{1,0:T(8,128)S(1)}, f32[64,512]{1,0:T(8,128)S(1)}, u32[]{:S(2)}, u32[]{:S(2)}) collective-permute-start(f32[64,512]{1,0:T(8,128)S(1)} %get-tuple-element.121), channel_id=1, source_target_pairs={{16,8},{20,12},{17,9},{21,13},{18,10},{22,14},{19,11},{23,15}} | collective-permute-start | bytes 393224 | tf_op jit(solution)/shard_map/ppermute | solution.py:341
  41.4 9.0 %collective-permute-start.13 = (f32[64,512]{1,0:T(8,128)S(1)}, f32[64,512]{1,0:T(8,128)S(1)}, u32[]{:S(2)}, u32[]{:S(2)}) collective-permute-start(f32[64,512]{1,0:T(8,128)S(1)} %far_terms.19.refs_0_), channel_id=1, source_target_pairs={{16,0},{20,4},{17,1},{21,5},{18,2},{22,6},{19,3},{23,7}} | collective-permute-start | bytes 393224 | tf_op jit(solution)/shard_map/ppermute | solution.py:341
  43.1 11.7 %collective-permute-start.14 = (f32[64,512]{1,0:T(8,128)S(1)}, f32[64,512]{1,0:T(8,128)S(1)}, u32[]{:S(2)}, u32[]{:S(2)}) collective-permute-start(f32[64,512]{1,0:T(8,128)S(1)} %get-tuple-element.123), channel_id=1, source_target_pairs={{8,0},{12,4},{9,1},{13,5},{10,2},{14,6},{11,3},{15,7}} | collective-permute-start | bytes 393224 | tf_op jit(solution)/shard_map/ppermute | solution.py:341
  44.4 12.7 %copy-start.2 = (f32[1192,256]{1,0:T(8,128)S(1)}, f32[1192,256]{1,0:T(8,128)}, u32[]{:S(2)}) copy-start(f32[1192,256]{1,0:T(8,128)} %get-tuple-element.129.own.refs_6_) | copy-start | bytes 3661828
  55.1 5.7 %collective-permute-start.16 = (f32[64,512]{1,0:T(8,128)S(1)}, f32[64,512]{1,0:T(8,128)S(1)}, u32[]{:S(2)}, u32[]{:S(2)}) collective-permute-start(f32[64,512]{1,0:T(8,128)S(1)} %get-tuple-element.125), channel_id=1, source_target_pairs={{0,24},{4,28},{1,25},{5,29},{2,26},{6,30},{3,27},{7,31}} | collective-permute-start | bytes 393224 | tf_op jit(solution)/shard_map/ppermute | solution.py:341
  56.4 4.4 %collective-permute-start.15 = (f32[64,512]{1,0:T(8,128)S(1)}, f32[64,512]{1,0:T(8,128)S(1)}, u32[]{:S(2)}, u32[]{:S(2)}) collective-permute-start(f32[64,512]{1,0:T(8,128)S(1)} %far_terms.20.refs_0_), channel_id=1, source_target_pairs={{8,24},{12,28},{9,25},{13,29},{10,26},{14,30},{11,27},{15,31}} | collective-permute-start | bytes 393224 | tf_op jit(solution)/shard_map/ppermute | solution.py:341
  58.6 5.3 %collective-permute-start.18 = (f32[64,512]{1,0:T(8,128)S(1)}, f32[64,512]{1,0:T(8,128)S(1)}, u32[]{:S(2)}, u32[]{:S(2)}) collective-permute-start(f32[64,512]{1,0:T(8,128)S(1)} %far_terms.21.refs_0_), channel_id=1, source_target_pairs={{0,16},{4,20},{1,17},{5,21},{2,18},{6,22},{3,19},{7,23}} | collective-permute-start | bytes 393224 | tf_op jit(solution)/shard_map/ppermute | solution.py:341
  61.1 2.8 %collective-permute-start.19 = (f32[64,512]{1,0:T(8,128)S(1)}, f32[64,512]{1,0:T(8,128)S(1)}, u32[]{:S(2)}, u32[]{:S(2)}) collective-permute-start(f32[64,512]{1,0:T(8,128)S(1)} %get-tuple-element.138), channel_id=1, source_target_pairs={{24,16},{28,20},{25,17},{29,21},{26,18},{30,22},{27,19},{31,23}} | collective-permute-start | bytes 393224 | tf_op jit(solution)/shard_map/ppermute | solution.py:341
  63.2 3.3 %collective-permute-start.20 = (f32[64,512]{1,0:T(8,128)S(1)}, f32[64,512]{1,0:T(8,128)S(1)}, u32[]{:S(2)}, u32[]{:S(2)}) collective-permute-start(f32[64,512]{1,0:T(8,128)S(1)} %far_terms.22.refs_0_), channel_id=1, source_target_pairs={{24,8},{28,12},{25,9},{29,13},{26,10},{30,14},{27,11},{31,15}} | collective-permute-start | bytes 393224 | tf_op jit(solution)/shard_map/ppermute | solution.py:341
  64.2 2.3 %collective-permute-start.21 = (f32[64,512]{1,0:T(8,128)S(1)}, f32[64,512]{1,0:T(8,128)S(1)}, u32[]{:S(2)}, u32[]{:S(2)}) collective-permute-start(f32[64,512]{1,0:T(8,128)S(1)} %get-tuple-element.140), channel_id=1, source_target_pairs={{16,8},{20,12},{17,9},{21,13},{18,10},{22,14},{19,11},{23,15}} | collective-permute-start | bytes 393224 | tf_op jit(solution)/shard_map/ppermute | solution.py:341
  65.2 8.4 %collective-permute-start.22 = (f32[64,512]{1,0:T(8,128)S(1)}, f32[64,512]{1,0:T(8,128)S(1)}, u32[]{:S(2)}, u32[]{:S(2)}) collective-permute-start(f32[64,512]{1,0:T(8,128)S(1)} %far_terms.23.refs_0_), channel_id=1, source_target_pairs={{16,0},{20,4},{17,1},{21,5},{18,2},{22,6},{19,3},{23,7}} | collective-permute-start | bytes 393224 | tf_op jit(solution)/shard_map/ppermute | solution.py:341
  66.8 11.2 %collective-permute-start.23 = (f32[64,512]{1,0:T(8,128)S(1)}, f32[64,512]{1,0:T(8,128)S(1)}, u32[]{:S(2)}, u32[]{:S(2)}) collective-permute-start(f32[64,512]{1,0:T(8,128)S(1)} %get-tuple-element.142), channel_id=1, source_target_pairs={{8,0},{12,4},{9,1},{13,5},{10,2},{14,6},{11,3},{15,7}} | collective-permute-start | bytes 393224 | tf_op jit(solution)/shard_map/ppermute | solution.py:341
  78.3 5.8 %collective-permute-start.25 = (f32[64,512]{1,0:T(8,128)S(1)}, f32[64,512]{1,0:T(8,128)S(1)}, u32[]{:S(2)}, u32[]{:S(2)}) collective-permute-start(f32[64,512]{1,0:T(8,128)S(1)} %get-tuple-element.144), channel_id=1, source_target_pairs={{0,24},{4,28},{1,25},{5,29},{2,26},{6,30},{3,27},{7,31}} | collective-permute-start | bytes 393224 | tf_op jit(solution)/shard_map/ppermute | solution.py:341
  79.6 4.6 %collective-permute-start.24 = (f32[64,512]{1,0:T(8,128)S(1)}, f32[64,512]{1,0:T(8,128)S(1)}, u32[]{:S(2)}, u32[]{:S(2)}) collective-permute-start(f32[64,512]{1,0:T(8,128)S(1)} %far_terms.24.refs_0_), channel_id=1, source_target_pairs={{8,24},{12,28},{9,25},{13,29},{10,26},{14,30},{11,27},{15,31}} | collective-permute-start | bytes 393224 | tf_op jit(solution)/shard_map/ppermute | solution.py:341
  82.0 5.3 %collective-permute-start.27 = (f32[64,512]{1,0:T(8,128)S(1)}, f32[64,512]{1,0:T(8,128)S(1)}, u32[]{:S(2)}, u32[]{:S(2)}) collective-permute-start(f32[64,512]{1,0:T(8,128)S(1)} %far_terms.25.refs_0_), channel_id=1, source_target_pairs={{0,16},{4,20},{1,17},{5,21},{2,18},{6,22},{3,19},{7,23}} | collective-permute-start | bytes 393224 | tf_op jit(solution)/shard_map/ppermute | solution.py:341
  84.5 2.8 %collective-permute-start.28 = (f32[64,512]{1,0:T(8,128)S(1)}, f32[64,512]{1,0:T(8,128)S(1)}, u32[]{:S(2)}, u32[]{:S(2)}) collective-permute-start(f32[64,512]{1,0:T(8,128)S(1)} %get-tuple-element.157), channel_id=1, source_target_pairs={{24,16},{28,20},{25,17},{29,21},{26,18},{30,22},{27,19},{31,23}} | collective-permute-start | bytes 393224 | tf_op jit(solution)/shard_map/ppermute | solution.py:341
  86.6 3.3 %collective-permute-start.29 = (f32[64,512]{1,0:T(8,128)S(1)}, f32[64,512]{1,0:T(8,128)S(1)}, u32[]{:S(2)}, u32[]{:S(2)}) collective-permute-start(f32[64,512]{1,0:T(8,128)S(1)} %far_terms.26.refs_0_), channel_id=1, source_target_pairs={{24,8},{28,12},{25,9},{29,13},{26,10},{30,14},{27,11},{31,15}} | collective-permute-start | bytes 393224 | tf_op jit(solution)/shard_map/ppermute | solution.py:341
  87.6 2.3 %collective-permute-start.30 = (f32[64,512]{1,0:T(8,128)S(1)}, f32[64,512]{1,0:T(8,128)S(1)}, u32[]{:S(2)}, u32[]{:S(2)}) collective-permute-start(f32[64,512]{1,0:T(8,128)S(1)} %get-tuple-element.159), channel_id=1, source_target_pairs={{16,8},{20,12},{17,9},{21,13},{18,10},{22,14},{19,11},{23,15}} | collective-permute-start | bytes 393224 | tf_op jit(solution)/shard_map/ppermute | solution.py:341
  88.6 8.3 %collective-permute-start.31 = (f32[64,512]{1,0:T(8,128)S(1)}, f32[64,512]{1,0:T(8,128)S(1)}, u32[]{:S(2)}, u32[]{:S(2)}) collective-permute-start(f32[64,512]{1,0:T(8,128)S(1)} %far_terms.27.refs_0_), channel_id=1, source_target_pairs={{16,0},{20,4},{17,1},{21,5},{18,2},{22,6},{19,3},{23,7}} | collective-permute-start | bytes 393224 | tf_op jit(solution)/shard_map/ppermute | solution.py:341
  90.2 11.0 %collective-permute-start.32 = (f32[64,512]{1,0:T(8,128)S(1)}, f32[64,512]{1,0:T(8,128)S(1)}, u32[]{:S(2)}, u32[]{:S(2)}) collective-permute-start(f32[64,512]{1,0:T(8,128)S(1)} %get-tuple-element.161), channel_id=1, source_target_pairs={{8,0},{12,4},{9,1},{13,5},{10,2},{14,6},{11,3},{15,7}} | collective-permute-start | bytes 393224 | tf_op jit(solution)/shard_map/ppermute | solution.py:341
  91.5 10.8 %collective-permute-start.39 = (f32[64,256]{1,0:T(8,128)S(1)}, f32[64,256]{1,0:T(8,128)S(1)}, u32[]{:S(2)}, u32[]{:S(2)}) collective-permute-start(f32[64,256]{1,0:T(8,128)S(1)} %get-tuple-element.174), channel_id=1, source_target_pairs={{0,4},{4,0},{8,12},{12,8},{16,20},{20,16},{24,28},{28,24},{1,5},{5... | collective-permute-start | bytes 196616 | tf_op jit(solution)/shard_map/ppermute | solution.py:330
  91.6 10.8 %collective-permute-start.38 = (f32[64,256]{1,0:T(8,128)S(1)}, f32[64,256]{1,0:T(8,128)S(1)}, u32[]{:S(2)}, u32[]{:S(2)}) collective-permute-start(f32[64,256]{1,0:T(8,128)S(1)} %get-tuple-element.173), channel_id=1, source_target_pairs={{0,4},{4,0},{8,12},{12,8},{16,20},{20,16},{24,28},{28,24},{1,5},{5... | collective-permute-start | bytes 196616 | tf_op jit(solution)/shard_map/ppermute | solution.py:330
  92.1 13.2 %collective-permute-start.37 = (f32[64,256]{1,0:T(8,128)S(1)}, f32[64,256]{1,0:T(8,128)S(1)}, u32[]{:S(2)}, u32[]{:S(2)}) collective-permute-start(f32[64,256]{1,0:T(8,128)S(1)} %get-tuple-element.172), channel_id=1, source_target_pairs={{0,4},{4,0},{8,12},{12,8},{16,20},{20,16},{24,28},{28,24},{1,5},{5... | collective-permute-start | bytes 196616 | tf_op jit(solution)/shard_map/ppermute | solution.py:330
  102.1 3.1 %collective-permute-start.36 = (f32[64,256]{1,0:T(8,128)S(1)}, f32[64,256]{1,0:T(8,128)S(1)}, u32[]{:S(2)}, u32[]{:S(2)}) collective-permute-start(f32[64,256]{1,0:T(8,128)S(1)} %get-tuple-element.171), channel_id=1, source_target_pairs={{0,4},{4,0},{8,12},{12,8},{16,20},{20,16},{24,28},{28,24},{1,5},{5... | collective-permute-start | bytes 196616 | tf_op jit(solution)/shard_map/ppermute | solution.py:330
  102.2 5.0 %collective-permute-start.33 = (f32[64,128]{1,0:T(8,128)S(1)}, f32[64,128]{1,0:T(8,128)S(1)}, u32[]{:S(2)}, u32[]{:S(2)}) collective-permute-start(f32[64,128]{1,0:T(8,128)S(1)} %get-tuple-element.164), channel_id=1, source_target_pairs={{0,8},{4,12},{8,16},{12,20},{16,24},{20,28},{24,0},{28,4},{1,9},{5... | collective-permute-start | bytes 98312 | tf_op jit(solution)/shard_map/ppermute | solution.py:333
  102.3 5.0 %collective-permute-start.34 = (f32[64,128]{1,0:T(8,128)S(1)}, f32[64,128]{1,0:T(8,128)S(1)}, u32[]{:S(2)}, u32[]{:S(2)}) collective-permute-start(f32[64,128]{1,0:T(8,128)S(1)} %get-tuple-element.165), channel_id=1, source_target_pairs={{0,16},{4,20},{8,24},{12,28},{16,0},{20,4},{24,8},{28,12},{1,17},{... | collective-permute-start | bytes 98312 | tf_op jit(solution)/shard_map/ppermute | solution.py:333
  102.4 5.3 %collective-permute-start.35 = (f32[64,128]{1,0:T(8,128)S(1)}, f32[64,128]{1,0:T(8,128)S(1)}, u32[]{:S(2)}, u32[]{:S(2)}) collective-permute-start(f32[64,128]{1,0:T(8,128)S(1)} %get-tuple-element.166), channel_id=1, source_target_pairs={{0,24},{4,28},{8,0},{12,4},{16,8},{20,12},{24,16},{28,20},{1,25},{... | collective-permute-start | bytes 98312 | tf_op jit(solution)/shard_map/ppermute | solution.py:333
  107.7 1.2 %collective-permute-start.40 = (f32[32,128]{1,0:T(8,128)S(1)}, f32[32,128]{1,0:T(8,128)S(1)}, u32[]{:S(2)}, u32[]{:S(2)}) collective-permute-start(f32[32,128]{1,0:T(8,128)S(1)} %get-tuple-element.181), channel_id=1, source_target_pairs={{0,4},{4,0},{8,12},{12,8},{16,20},{20,16},{24,28},{28,24},{1,5},{5... | collective-permute-start | bytes 49160 | tf_op jit(solution)/shard_map/ppermute | solution.py:330

commit v3 on v2

--- a/solution.py
+++ b/solution.py
@@ -263,26 +263,21 @@
         return
     held = outs.pop()
     held[...] = sums
-    rows = NDIST // pairs
-    for by, part in enumerate(outs):
-        to = lax.rem(chip + by, pairs)
+    rows = NDIST // (2 * pairs)
+    core = jnp.where(is_a, 1, 0)
+    for i, part in enumerate(outs):
+        to = 2 * lax.rem(chip + i // 2, pairs) + (core if i % 2 == 0 else 1 - core)
         part[...] = held[pl.ds(pl.multiple_of(to * rows, rows), rows), :]
 
 
-def add_kernel(*refs):
-    mine, theirs = refs[-2:]
-    total = refs[0][...]
-    for part in refs[1:-2]:
-        total = total + part[...]
-    rows = mine.shape[0]
-    is_a = upper_here()
-    mine[...] = jnp.where(is_a, total[rows:], total[:rows])
-    theirs[...] = jnp.where(is_a, total[:rows], total[rows:])
-
-
-def mean_kernel(mine, got, out):
+def mean_kernel(*refs):
+    *parts, out = refs
     half = out.shape[1] // 2
-    own, oth = (x[:, :half] / x[:, half:] for x in (mine, got))
+    own, oth = parts[0][...], parts[1][...]
+    for i in range(2, len(parts), 2):
+        own = own + parts[i][...]
+        oth = oth + parts[i + 1][...]
+    own, oth = (x[:, :half] / x[:, half:] for x in (own, oth))
     is_a = upper_here()
     out[...] = jnp.concatenate(
         [jnp.where(is_a, oth, own), jnp.where(is_a, own, oth)], axis=1
@@ -329,8 +324,9 @@
     def swap(x):
         return lax.ppermute(x, "blk", [(i, i ^ 1) for i in range(n)])
 
-    def shift(x, by):
-        return lax.ppermute(x, "blk", [(i, (i + 2 * by) % n) for i in range(n)])
+    def send(x, by, flip):
+        perm = [(i, (i + 2 * by) % n ^ flip) for i in range(n)]
+        return lax.ppermute(x, "blk", perm)
 
     def pass_on(x, lead, by):
         perm = []
@@ -385,7 +381,7 @@
         window = values[first : first + pairs + 2 * (pieces - 1)]
         is_last = r == 0
         outs = (shaped(half, bs), shaped(half, bs))
-        outs += (shaped(NDIST // pairs, columns),) * pairs if is_last else (shaped(NDIST, columns),)
+        outs += (shaped(NDIST // n, columns),) * n if is_last else (shaped(NDIST, columns),)
         extra = () if total is None else (total,)
         return call(
             functools.partial(
@@ -465,7 +461,7 @@
 
     keeps[0], give, *parts = finish(0, values, total)
     gots[0] = swap(give)
-    parts = [parts[0]] + [shift(parts[by], by) for by in range(1, pairs)]
+    parts = [parts[0]] + [send(parts[i], i // 2, i % 2) for i in range(1, n)]
     order = range(rows_here)
     field = call(
         functools.partial(field_kernel, rows_here),
@@ -477,9 +473,7 @@
         8 * rows_here * bs * columns,
     )
     parts, field = lax.optimization_barrier((parts, field))
-    held = shaped(NDIST // n, columns)
-    mine, theirs = call(add_kernel, "district_add", (held, held), tuple(parts), 4)
-    mean = call(mean_kernel, "district_mean", held, (mine, swap(theirs)), 4)
+    mean = call(mean_kernel, "district_mean", shaped(NDIST // n, columns), tuple(parts), 4)
     return field, mean
 
 

time: 111 us -> 113 us (1.018)
  starting transfers between devices: 33.6 us -> 35.4 us
    ppermute x3 -> x7, starting transfers between devices: 3 us -> 4.86 us  [send(): return lax.ppermute(x, 'blk', perm)]
    ppermute x3 -> x7, waiting for transfers between devices: 1.39 us -> 3.08 us  [send(): return lax.ppermute(x, 'blk', perm)]
    ppermute x9 -> x8, waiting for transfers between devices: 1.19 us -> 0.02 us  [swap(): return lax.ppermute(x, 'blk', [(i, i ^ 1) for i in range(n)])]
    pallas_call x47 -> x46, Pallas kernels: 29.8 us -> 29.8 us  [call(): pl.pallas_call(kernel, out_shape=outs, in_specs=more.pop('in_specs', [VME...]
  transfers between devices with their start and end apart: 41 -> 44, of which waited for: 11 -> 10; matrix products, arithmetic and copies ran while one was open for 0% -> 0% of each run, Pallas kernels for 24% -> 23%
where the time goes in v3:
time: 113 us; the launch traced here: 112 us
  waiting for transfers between devices  45.3 us (40%)
  starting transfers between devices  35.4 us (31%)
  Pallas kernels  29.8 us (26%)
  between operations  1.47 us (1%)
    ppermute x29, waiting for transfers between devices, pass_on(): return lax.ppermute(x, 'blk', perm)  42.2 us
    pallas_call x46, Pallas kernels, call(): pl.pallas_call(kernel, out_shape=outs, in_specs=more.pop('in_specs', [VME...  29.8 us
    ppermute x29, starting transfers between devices, pass_on(): return lax.ppermute(x, 'blk', perm)  28.5 us
    ppermute x7, starting transfers between devices, send(): return lax.ppermute(x, 'blk', perm)  4.86 us
    ppermute x7, waiting for transfers between devices, send(): return lax.ppermute(x, 'blk', perm)  3.08 us
  transfers between devices with their start and end apart: 44, of which 10 were waited for; matrix products, arithmetic and copies ran while one was open for 0% of the time, Pallas kernels for 23%

profile of v3, /device:TPU:0, one launch (start us, length us, event | category | flops | bytes accessed | tf_op | source)
XLA Modules:
  0.0 111.9 jit_solution(4979798592932694206)
XLA Ops:
  0.6 2.9 %pack.2.own.refs_6_ = f32[1192,256]{1,0:T(8,128)} custom-call(s32[3,1,4]{2,1,0:T(1,128)} %bitcast.1, f32[4,1,256]{2,1,0:T(1,128)} %turnout.2, s32[4,1,256]{2,1,0:T(1,128)} %district.3, f32[4,1,3,256,256]{4,3,2,1,0:T(8,128)} %l_ref.3, f32[4,1,256,256]{3,2,1,0:T(8,128)} %d_ref.3, f32[4,1,256,128]{3,2,1,0:T(8,128)} %r_ref.3), custom_call_target="tpu_custom_call" | custom-call | bytes 2441216 | tf_op jit(solution)/shard_map/pack/pallas_call | solution.py:313
  4.0 3.8 %pack.3 = (f32[1192,256]{1,0:T(8,128)}, f32[1192,256]{1,0:T(8,128)}, f32[1192,256]{1,0:T(8,128)}) custom-call(s32[3,1,4]{2,1,0:T(1,128)} %bitcast.2, f32[4,1,256]{2,1,0:T(1,128)} %turnout.2, s32[4,1,256]{2,1,0:T(1,128)} %district.3, f32[4,1,3,256,256]{4,3,2,1,0:T(8,128)} %l_ref.3, f32[4,1,256,256]{3,2,1,0:T(8,128)} %d_ref.3, f32[4,1,256,128]{3,2,1,0:T(8,128)} %r_ref.3), custom_call_target="tpu_custom_call" | custom-call | bytes 7323648 | tf_op jit(solution)/shard_map/pack/pallas_call | solution.py:313
  8.5 1.2 %near_setup.4 = (bf16[512,512]{1,0:T(8,128)(2,1)S(1)}, bf16[512,512]{1,0:T(8,128)(2,1)S(1)}, bf16[4,256,256]{2,1,0:T(8,128)(2,1)S(1)}, bf16[4,256,256]{2,1,0:T(8,128)(2,1)S(1)}, f32[64,512]{1,0:T(8,128)S(1)}) custom-call(f32[1192,256]{1,0:T(8,128)S(1)} %copy-done, f32[1192,256]{1,0:T(8,128)S(1)} %collective-permute-done.oth.refs_7_), custom_call_target="tpu_custom_call" | custom-call | flops 704643072 | bytes 6291456 | tf_op jit(solution)/shard_map/near_setup/pallas_call | solution.py:313
  10.0 0.7 collective-permute-start.1
  10.6 1.2 %far_setup.4 = (bf16[512,512]{1,0:T(8,128)(2,1)S(1)}, bf16[512,512]{1,0:T(8,128)(2,1)S(1)}) custom-call(f32[1192,256]{1,0:T(8,128)S(1)} %copy-done, f32[1192,256]{1,0:T(8,128)S(1)} %collective-permute-done.oth.refs_7_, bf16[4,256,256]{2,1,0:T(8,128)(2,1)S(1)} %get-tuple-element.102.mh.refs_4_, bf16[4,256,256]{2,1,0:T(8,128)(2,1)S(1)} %get-tuple-element.103.ml.refs_5_), custom_call_target="tpu_custom_call" | custom-call | flops 503316480 | bytes 6291456 | tf_op jit(solution)/shard_map/far_setup/pallas_call | solution.py:313
  12.1 0.7 collective-permute-start.2
  13.1 0.7 collective-permute-start.3
  14.1 1.4 %collective-permute-start.4 = (f32[64,512]{1,0:T(8,128)S(1)}, f32[64,512]{1,0:T(8,128)S(1)}, u32[]{:S(2)}, u32[]{:S(2)}) collective-permute-start(f32[64,512]{1,0:T(8,128)S(1)} %far_terms.15.refs_0_), channel_id=1, source_target_pairs={{16,0},{20,4},{17,1},{21,5},{18,2},{22,6},{19,3},{23,7}} | collective-permute-start | bytes 393224 | tf_op jit(solution)/shard_map/ppermute | solution.py:337
  15.8 1.3 %collective-permute-start.5 = (f32[64,512]{1,0:T(8,128)S(1)}, f32[64,512]{1,0:T(8,128)S(1)}, u32[]{:S(2)}, u32[]{:S(2)}) collective-permute-start(f32[64,512]{1,0:T(8,128)S(1)} %get-tuple-element.110), channel_id=1, source_target_pairs={{8,0},{12,4},{9,1},{13,5},{10,2},{14,6},{11,3},{15,7}} | collective-permute-start | bytes 393224 | tf_op jit(solution)/shard_map/ppermute | solution.py:337
  17.7 9.1 %collective-permute-done.4.refs_1_ = f32[64,512]{1,0:T(8,128)S(1)} collective-permute-done((f32[64,512]{1,0:T(8,128)S(1)}, f32[64,512]{1,0:T(8,128)S(1)}, u32[]{:S(2)}, u32[]{:S(2)}) %collective-permute-start.4) | collective-permute-done | bytes 131104 | tf_op jit(solution)/shard_map/ppermute | solution.py:337
  26.8 4.2 %collective-permute-done.5.refs_2_ = f32[64,512]{1,0:T(8,128)S(1)} collective-permute-done((f32[64,512]{1,0:T(8,128)S(1)}, f32[64,512]{1,0:T(8,128)S(1)}, u32[]{:S(2)}, u32[]{:S(2)}) %collective-permute-start.5) | collective-permute-done | bytes 131104 | tf_op jit(solution)/shard_map/ppermute | solution.py:337
  31.3 1.3 %collective-permute-start.7 = (f32[64,512]{1,0:T(8,128)S(1)}, f32[64,512]{1,0:T(8,128)S(1)}, u32[]{:S(2)}, u32[]{:S(2)}) collective-permute-start(f32[64,512]{1,0:T(8,128)S(1)} %get-tuple-element.112), channel_id=1, source_target_pairs={{0,24},{4,28},{1,25},{5,29},{2,26},{6,30},{3,27},{7,31}} | collective-permute-start | bytes 393224 | tf_op jit(solution)/shard_map/ppermute | solution.py:337
  32.6 0.7 collective-permute-start.6
  33.3 1.2 %near_setup.5 = (bf16[512,512]{1,0:T(8,128)(2,1)S(1)}, bf16[512,512]{1,0:T(8,128)(2,1)S(1)}, bf16[4,256,256]{2,1,0:T(8,128)(2,1)S(1)}, bf16[4,256,256]{2,1,0:T(8,128)(2,1)S(1)}, f32[64,512]{1,0:T(8,128)S(1)}) custom-call(f32[1192,256]{1,0:T(8,128)S(1)} %copy-done.3, f32[1192,256]{1,0:T(8,128)S(1)} %collective-permute-done.8.oth.refs_7_), custom_call_target="tpu_custom_call" | custom-call | flops 704643072 | bytes 6291456 | tf_op jit(solution)/shard_map/near_setup/pallas_call | solution.py:313
  34.8 1.3 %collective-permute-start.9 = (f32[64,512]{1,0:T(8,128)S(1)}, f32[64,512]{1,0:T(8,128)S(1)}, u32[]{:S(2)}, u32[]{:S(2)}) collective-permute-start(f32[64,512]{1,0:T(8,128)S(1)} %far_terms.17.refs_0_), channel_id=1, source_target_pairs={{0,16},{4,20},{1,17},{5,21},{2,18},{6,22},{3,19},{7,23}} | collective-permute-start | bytes 393224 | tf_op jit(solution)/shard_map/ppermute | solution.py:337
  36.1 0.9 finish.4
  38.0 1.2 %far_setup.5 = (bf16[512,512]{1,0:T(8,128)(2,1)S(1)}, bf16[512,512]{1,0:T(8,128)(2,1)S(1)}) custom-call(f32[1192,256]{1,0:T(8,128)S(1)} %copy-done.3, f32[1192,256]{1,0:T(8,128)S(1)} %collective-permute-done.8.oth.refs_7_, bf16[4,256,256]{2,1,0:T(8,128)(2,1)S(1)} %get-tuple-element.121.mh.refs_4_, bf16[4,256,256]{2,1,0:T(8,128)(2,1)S(1)} %get-tuple-element.122.ml.refs_5_), custom_call_target="tpu_custom_call" | custom-call | flops 503316480 | bytes 6291456 | tf_op jit(solution)/shard_map/far_setup/pallas_call | solution.py:313
  41.4 1.3 %collective-permute-start.13 = (f32[64,512]{1,0:T(8,128)S(1)}, f32[64,512]{1,0:T(8,128)S(1)}, u32[]{:S(2)}, u32[]{:S(2)}) collective-permute-start(f32[64,512]{1,0:T(8,128)S(1)} %far_terms.19.refs_0_), channel_id=1, source_target_pairs={{16,0},{20,4},{17,1},{21,5},{18,2},{22,6},{19,3},{23,7}} | collective-permute-start | bytes 393224 | tf_op jit(solution)/shard_map/ppermute | solution.py:337
  43.1 1.3 %collective-permute-start.14 = (f32[64,512]{1,0:T(8,128)S(1)}, f32[64,512]{1,0:T(8,128)S(1)}, u32[]{:S(2)}, u32[]{:S(2)}) collective-permute-start(f32[64,512]{1,0:T(8,128)S(1)} %get-tuple-element.129), channel_id=1, source_target_pairs={{8,0},{12,4},{9,1},{13,5},{10,2},{14,6},{11,3},{15,7}} | collective-permute-start | bytes 393224 | tf_op jit(solution)/shard_map/ppermute | solution.py:337
  44.7 5.7 %collective-permute-done.13.refs_1_ = f32[64,512]{1,0:T(8,128)S(1)} collective-permute-done((f32[64,512]{1,0:T(8,128)S(1)}, f32[64,512]{1,0:T(8,128)S(1)}, u32[]{:S(2)}, u32[]{:S(2)}) %collective-permute-start.13) | collective-permute-done | bytes 131104 | tf_op jit(solution)/shard_map/ppermute | solution.py:337
  50.4 4.4 %collective-permute-done.14.refs_2_ = f32[64,512]{1,0:T(8,128)S(1)} collective-permute-done((f32[64,512]{1,0:T(8,128)S(1)}, f32[64,512]{1,0:T(8,128)S(1)}, u32[]{:S(2)}, u32[]{:S(2)}) %collective-permute-start.14) | collective-permute-done | bytes 131104 | tf_op jit(solution)/shard_map/ppermute | solution.py:337
  55.1 1.3 %collective-permute-start.16 = (f32[64,512]{1,0:T(8,128)S(1)}, f32[64,512]{1,0:T(8,128)S(1)}, u32[]{:S(2)}, u32[]{:S(2)}) collective-permute-start(f32[64,512]{1,0:T(8,128)S(1)} %get-tuple-element.131), channel_id=1, source_target_pairs={{0,24},{4,28},{1,25},{5,29},{2,26},{6,30},{3,27},{7,31}} | collective-permute-start | bytes 393224 | tf_op jit(solution)/shard_map/ppermute | solution.py:337
  57.1 1.2 %near_setup.6 = (bf16[512,512]{1,0:T(8,128)(2,1)S(1)}, bf16[512,512]{1,0:T(8,128)(2,1)S(1)}, bf16[4,256,256]{2,1,0:T(8,128)(2,1)S(1)}, bf16[4,256,256]{2,1,0:T(8,128)(2,1)S(1)}, f32[64,512]{1,0:T(8,128)S(1)}) custom-call(f32[1192,256]{1,0:T(8,128)S(1)} %copy-done.2, f32[1192,256]{1,0:T(8,128)S(1)} %collective-permute-done.17.oth.refs_7_), custom_call_target="tpu_custom_call" | custom-call | flops 704643072 | bytes 6291456 | tf_op jit(solution)/shard_map/near_setup/pallas_call | solution.py:313
  58.6 1.3 %collective-permute-start.18 = (f32[64,512]{1,0:T(8,128)S(1)}, f32[64,512]{1,0:T(8,128)S(1)}, u32[]{:S(2)}, u32[]{:S(2)}) collective-permute-start(f32[64,512]{1,0:T(8,128)S(1)} %far_terms.21.refs_0_), channel_id=1, source_target_pairs={{0,16},{4,20},{1,17},{5,21},{2,18},{6,22},{3,19},{7,23}} | collective-permute-start | bytes 393224 | tf_op jit(solution)/shard_map/ppermute | solution.py:337
  59.9 0.9 finish.5
  61.1 0.7 collective-permute-start.19
  61.7 1.2 %far_setup.6 = (bf16[512,512]{1,0:T(8,128)(2,1)S(1)}, bf16[512,512]{1,0:T(8,128)(2,1)S(1)}) custom-call(f32[1192,256]{1,0:T(8,128)S(1)} %copy-done.2, f32[1192,256]{1,0:T(8,128)S(1)} %collective-permute-done.17.oth.refs_7_, bf16[4,256,256]{2,1,0:T(8,128)(2,1)S(1)} %get-tuple-element.140.mh.refs_4_, bf16[4,256,256]{2,1,0:T(8,128)(2,1)S(1)} %get-tuple-element.141.ml.refs_5_), custom_call_target="tpu_custom_call" | custom-call | flops 503316480 | bytes 6291456 | tf_op jit(solution)/shard_map/far_setup/pallas_call | solution.py:313
  65.2 1.3 %collective-permute-start.22 = (f32[64,512]{1,0:T(8,128)S(1)}, f32[64,512]{1,0:T(8,128)S(1)}, u32[]{:S(2)}, u32[]{:S(2)}) collective-permute-start(f32[64,512]{1,0:T(8,128)S(1)} %far_terms.23.refs_0_), channel_id=1, source_target_pairs={{16,0},{20,4},{17,1},{21,5},{18,2},{22,6},{19,3},{23,7}} | collective-permute-start | bytes 393224 | tf_op jit(solution)/shard_map/ppermute | solution.py:337
  66.8 1.3 %collective-permute-start.23 = (f32[64,512]{1,0:T(8,128)S(1)}, f32[64,512]{1,0:T(8,128)S(1)}, u32[]{:S(2)}, u32[]{:S(2)}) collective-permute-start(f32[64,512]{1,0:T(8,128)S(1)} %get-tuple-element.148), channel_id=1, source_target_pairs={{8,0},{12,4},{9,1},{13,5},{10,2},{14,6},{11,3},{15,7}} | collective-permute-start | bytes 393224 | tf_op jit(solution)/shard_map/ppermute | solution.py:337
  68.4 5.2 %collective-permute-done.22.refs_1_ = f32[64,512]{1,0:T(8,128)S(1)} collective-permute-done((f32[64,512]{1,0:T(8,128)S(1)}, f32[64,512]{1,0:T(8,128)S(1)}, u32[]{:S(2)}, u32[]{:S(2)}) %collective-permute-start.22) | collective-permute-done | bytes 131104 | tf_op jit(solution)/shard_map/ppermute | solution.py:337
  73.6 4.4 %collective-permute-done.23.refs_2_ = f32[64,512]{1,0:T(8,128)S(1)} collective-permute-done((f32[64,512]{1,0:T(8,128)S(1)}, f32[64,512]{1,0:T(8,128)S(1)}, u32[]{:S(2)}, u32[]{:S(2)}) %collective-permute-start.23) | collective-permute-done | bytes 131104 | tf_op jit(solution)/shard_map/ppermute | solution.py:337
  78.3 1.3 %collective-permute-start.25 = (f32[64,512]{1,0:T(8,128)S(1)}, f32[64,512]{1,0:T(8,128)S(1)}, u32[]{:S(2)}, u32[]{:S(2)}) collective-permute-start(f32[64,512]{1,0:T(8,128)S(1)} %get-tuple-element.150), channel_id=1, source_target_pairs={{0,24},{4,28},{1,25},{5,29},{2,26},{6,30},{3,27},{7,31}} | collective-permute-start | bytes 393224 | tf_op jit(solution)/shard_map/ppermute | solution.py:337
  79.6 0.8 collective-permute-start.24
  80.5 1.2 %near_setup.7 = (bf16[512,512]{1,0:T(8,128)(2,1)S(1)}, bf16[512,512]{1,0:T(8,128)(2,1)S(1)}, bf16[4,256,256]{2,1,0:T(8,128)(2,1)S(1)}, bf16[4,256,256]{2,1,0:T(8,128)(2,1)S(1)}, f32[64,512]{1,0:T(8,128)S(1)}) custom-call(f32[1192,256]{1,0:T(8,128)S(1)} %copy-done.1, f32[1192,256]{1,0:T(8,128)S(1)} %collective-permute-done.26.oth.refs_7_), custom_call_target="tpu_custom_call" | custom-call | flops 704643072 | bytes 6291456 | tf_op jit(solution)/shard_map/near_setup/pallas_call | solution.py:313
  82.0 1.3 %collective-permute-start.27 = (f32[64,512]{1,0:T(8,128)S(1)}, f32[64,512]{1,0:T(8,128)S(1)}, u32[]{:S(2)}, u32[]{:S(2)}) collective-permute-start(f32[64,512]{1,0:T(8,128)S(1)} %far_terms.25.refs_0_), channel_id=1, source_target_pairs={{0,16},{4,20},{1,17},{5,21},{2,18},{6,22},{3,19},{7,23}} | collective-permute-start | bytes 393224 | tf_op jit(solution)/shard_map/ppermute | solution.py:337
  83.3 0.9 finish.6
  85.1 1.2 %far_setup.7 = (bf16[512,512]{1,0:T(8,128)(2,1)S(1)}, bf16[512,512]{1,0:T(8,128)(2,1)S(1)}) custom-call(f32[1192,256]{1,0:T(8,128)S(1)} %copy-done.1, f32[1192,256]{1,0:T(8,128)S(1)} %collective-permute-done.26.oth.refs_7_, bf16[4,256,256]{2,1,0:T(8,128)(2,1)S(1)} %get-tuple-element.159.mh.refs_4_, bf16[4,256,256]{2,1,0:T(8,128)(2,1)S(1)} %get-tuple-element.160.ml.refs_5_), custom_call_target="tpu_custom_call" | custom-call | flops 503316480 | bytes 6291456 | tf_op jit(solution)/shard_map/far_setup/pallas_call | solution.py:313
  88.6 1.3 %collective-permute-start.31 = (f32[64,512]{1,0:T(8,128)S(1)}, f32[64,512]{1,0:T(8,128)S(1)}, u32[]{:S(2)}, u32[]{:S(2)}) collective-permute-start(f32[64,512]{1,0:T(8,128)S(1)} %far_terms.27.refs_0_), channel_id=1, source_target_pairs={{16,0},{20,4},{17,1},{21,5},{18,2},{22,6},{19,3},{23,7}} | collective-permute-start | bytes 393224 | tf_op jit(solution)/shard_map/ppermute | solution.py:337
  90.2 1.3 %collective-permute-start.32 = (f32[64,512]{1,0:T(8,128)S(1)}, f32[64,512]{1,0:T(8,128)S(1)}, u32[]{:S(2)}, u32[]{:S(2)}) collective-permute-start(f32[64,512]{1,0:T(8,128)S(1)} %get-tuple-element.167), channel_id=1, source_target_pairs={{8,0},{12,4},{9,1},{13,5},{10,2},{14,6},{11,3},{15,7}} | collective-permute-start | bytes 393224 | tf_op jit(solution)/shard_map/ppermute | solution.py:337
  92.1 4.7 %collective-permute-done.31.refs_0_ = f32[64,512]{1,0:T(8,128)S(1)} collective-permute-done((f32[64,512]{1,0:T(8,128)S(1)}, f32[64,512]{1,0:T(8,128)S(1)}, u32[]{:S(2)}, u32[]{:S(2)}) %collective-permute-start.31) | collective-permute-done | bytes 131104 | tf_op jit(solution)/shard_map/ppermute | solution.py:337
  96.8 4.4 %collective-permute-done.32.refs_1_ = f32[64,512]{1,0:T(8,128)S(1)} collective-permute-done((f32[64,512]{1,0:T(8,128)S(1)}, f32[64,512]{1,0:T(8,128)S(1)}, u32[]{:S(2)}, u32[]{:S(2)}) %collective-permute-start.32) | collective-permute-done | bytes 131104 | tf_op jit(solution)/shard_map/ppermute | solution.py:337
  101.2 0.9 finish.7
  102.8 2.8 %collective-permute-start.36 = (f32[32,128]{1,0:T(8,128)S(1)}, f32[32,128]{1,0:T(8,128)S(1)}, u32[]{:S(2)}, u32[]{:S(2)}) collective-permute-start(f32[32,128]{1,0:T(8,128)S(1)} %get-tuple-element.173), channel_id=1, source_target_pairs={{0,16},{4,20},{8,24},{12,28},{16,0},{20,4},{24,8},{28,12},{1,17},{... | collective-permute-start | bytes 49160 | tf_op jit(solution)/shard_map/ppermute | solution.py:329
  106.0 1.4 %collective-permute-done.34.refs_2_ = f32[32,128]{1,0:T(8,128)S(1)} collective-permute-done((f32[32,128]{1,0:T(8,128)S(1)}, f32[32,128]{1,0:T(8,128)S(1)}, u32[]{:S(2)}, u32[]{:S(2)}) %collective-permute-start.34) | collective-permute-done | bytes 16416 | tf_op jit(solution)/shard_map/ppermute | solution.py:329
  107.4 1.1 collective-permute-start.39
  108.5 1.0 field.1
  109.5 1.6 %collective-permute-done.38.refs_6_ = f32[32,128]{1,0:T(8,128)S(1)} collective-permute-done((f32[32,128]{1,0:T(8,128)S(1)}, f32[32,128]{1,0:T(8,128)S(1)}, u32[]{:S(2)}, u32[]{:S(2)}) %collective-permute-start.38) | collective-permute-done | bytes 16416 | tf_op jit(solution)/shard_map/ppermute | solution.py:329
  111.2 0.8 district_mean.1
  (94 shorter events, 17.4 us)
Async XLA Ops:
  3.5 5.0 %copy-start = (f32[1192,256]{1,0:T(8,128)S(1)}, f32[1192,256]{1,0:T(8,128)}, u32[]{:S(2)}) copy-start(f32[1192,256]{1,0:T(8,128)} %pack.2.own.refs_6_) | copy-start | bytes 3661828
  3.5 4.9 %collective-permute-start = (f32[1192,256]{1,0:T(8,128)}, f32[1192,256]{1,0:T(8,128)S(1)}, u32[]{:S(2)}, u32[]{:S(2)}) collective-permute-start(f32[1192,256]{1,0:T(8,128)} %pack.2.own.refs_6_), channel_id=1, source_target_pairs={{0,4},{4,0},{8,12},{12,8},{16,20},{20,16},{24,28},{28,24},{1,5},{5... | collective-permute-start | bytes 3661832 | tf_op jit(solution)/shard_map/ppermute | solution.py:325
  7.9 25.4 %collective-permute-start.8 = (f32[1192,256]{1,0:T(8,128)}, f32[1192,256]{1,0:T(8,128)S(1)}, u32[]{:S(2)}, u32[]{:S(2)}) collective-permute-start(f32[1192,256]{1,0:T(8,128)} %get-tuple-element.116.own.refs_6_), channel_id=1, source_target_pairs={{0,4},{4,0},{8,12},{12,8},{16,20},{20,16},{24,28},{28,24},{1,5},{5... | collective-permute-start | bytes 3661832 | tf_op jit(solution)/shard_map/ppermute | solution.py:325
  8.1 48.9 %collective-permute-start.17 = (f32[1192,256]{1,0:T(8,128)}, f32[1192,256]{1,0:T(8,128)S(1)}, u32[]{:S(2)}, u32[]{:S(2)}) collective-permute-start(f32[1192,256]{1,0:T(8,128)} %get-tuple-element.135.own.refs_6_), channel_id=1, source_target_pairs={{0,4},{4,0},{8,12},{12,8},{16,20},{20,16},{24,28},{28,24},{1,5},{5... | collective-permute-start | bytes 3661832 | tf_op jit(solution)/shard_map/ppermute | solution.py:325
  10.0 2.9 %collective-permute-start.1 = (f32[64,512]{1,0:T(8,128)S(1)}, f32[64,512]{1,0:T(8,128)S(1)}, u32[]{:S(2)}, u32[]{:S(2)}) collective-permute-start(f32[64,512]{1,0:T(8,128)S(1)} %get-tuple-element.106), channel_id=1, source_target_pairs={{24,16},{28,20},{25,17},{29,21},{26,18},{30,22},{27,19},{31,23}} | collective-permute-start | bytes 393224 | tf_op jit(solution)/shard_map/ppermute | solution.py:337
  12.1 3.4 %collective-permute-start.2 = (f32[64,512]{1,0:T(8,128)S(1)}, f32[64,512]{1,0:T(8,128)S(1)}, u32[]{:S(2)}, u32[]{:S(2)}) collective-permute-start(f32[64,512]{1,0:T(8,128)S(1)} %far_terms.14.refs_0_), channel_id=1, source_target_pairs={{24,8},{28,12},{25,9},{29,13},{26,10},{30,14},{27,11},{31,15}} | collective-permute-start | bytes 393224 | tf_op jit(solution)/shard_map/ppermute | solution.py:337
  13.1 2.4 %collective-permute-start.3 = (f32[64,512]{1,0:T(8,128)S(1)}, f32[64,512]{1,0:T(8,128)S(1)}, u32[]{:S(2)}, u32[]{:S(2)}) collective-permute-start(f32[64,512]{1,0:T(8,128)S(1)} %get-tuple-element.108), channel_id=1, source_target_pairs={{16,8},{20,12},{17,9},{21,13},{18,10},{22,14},{19,11},{23,15}} | collective-permute-start | bytes 393224 | tf_op jit(solution)/shard_map/ppermute | solution.py:337
  13.8 3.3 %copy-start.1 = (f32[1192,256]{1,0:T(8,128)S(1)}, f32[1192,256]{1,0:T(8,128)}, u32[]{:S(2)}) copy-start(f32[1192,256]{1,0:T(8,128)} %get-tuple-element.154.own.refs_6_) | copy-start | bytes 3661828
  14.1 12.7 %collective-permute-start.4 = (f32[64,512]{1,0:T(8,128)S(1)}, f32[64,512]{1,0:T(8,128)S(1)}, u32[]{:S(2)}, u32[]{:S(2)}) collective-permute-start(f32[64,512]{1,0:T(8,128)S(1)} %far_terms.15.refs_0_), channel_id=1, source_target_pairs={{16,0},{20,4},{17,1},{21,5},{18,2},{22,6},{19,3},{23,7}} | collective-permute-start | bytes 393224 | tf_op jit(solution)/shard_map/ppermute | solution.py:337
  15.8 15.2 %collective-permute-start.5 = (f32[64,512]{1,0:T(8,128)S(1)}, f32[64,512]{1,0:T(8,128)S(1)}, u32[]{:S(2)}, u32[]{:S(2)}) collective-permute-start(f32[64,512]{1,0:T(8,128)S(1)} %get-tuple-element.110), channel_id=1, source_target_pairs={{8,0},{12,4},{9,1},{13,5},{10,2},{14,6},{11,3},{15,7}} | collective-permute-start | bytes 393224 | tf_op jit(solution)/shard_map/ppermute | solution.py:337
  17.2 63.3 %collective-permute-start.26 = (f32[1192,256]{1,0:T(8,128)S(1)}, f32[1192,256]{1,0:T(8,128)S(1)}, u32[]{:S(2)}, u32[]{:S(2)}) collective-permute-start(f32[1192,256]{1,0:T(8,128)S(1)} %copy-done.1), channel_id=1, source_target_pairs={{0,4},{4,0},{8,12},{12,8},{16,20},{20,16},{24,28},{28,24},{1,5},{5... | collective-permute-start | bytes 3661832 | tf_op jit(solution)/shard_map/ppermute | solution.py:325
  17.4 15.9 %copy-start.3 = (f32[1192,256]{1,0:T(8,128)S(1)}, f32[1192,256]{1,0:T(8,128)}, u32[]{:S(2)}) copy-start(f32[1192,256]{1,0:T(8,128)} %get-tuple-element.116.own.refs_6_) | copy-start | bytes 3661828
  31.3 5.7 %collective-permute-start.7 = (f32[64,512]{1,0:T(8,128)S(1)}, f32[64,512]{1,0:T(8,128)S(1)}, u32[]{:S(2)}, u32[]{:S(2)}) collective-permute-start(f32[64,512]{1,0:T(8,128)S(1)} %get-tuple-element.112), channel_id=1, source_target_pairs={{0,24},{4,28},{1,25},{5,29},{2,26},{6,30},{3,27},{7,31}} | collective-permute-start | bytes 393224 | tf_op jit(solution)/shard_map/ppermute | solution.py:337
  32.6 4.4 %collective-permute-start.6 = (f32[64,512]{1,0:T(8,128)S(1)}, f32[64,512]{1,0:T(8,128)S(1)}, u32[]{:S(2)}, u32[]{:S(2)}) collective-permute-start(f32[64,512]{1,0:T(8,128)S(1)} %far_terms.16.refs_0_), channel_id=1, source_target_pairs={{8,24},{12,28},{9,25},{13,29},{10,26},{14,30},{11,27},{15,31}} | collective-permute-start | bytes 393224 | tf_op jit(solution)/shard_map/ppermute | solution.py:337
  34.8 5.3 %collective-permute-start.9 = (f32[64,512]{1,0:T(8,128)S(1)}, f32[64,512]{1,0:T(8,128)S(1)}, u32[]{:S(2)}, u32[]{:S(2)}) collective-permute-start(f32[64,512]{1,0:T(8,128)S(1)} %far_terms.17.refs_0_), channel_id=1, source_target_pairs={{0,16},{4,20},{1,17},{5,21},{2,18},{6,22},{3,19},{7,23}} | collective-permute-start | bytes 393224 | tf_op jit(solution)/shard_map/ppermute | solution.py:337
  37.3 2.8 %collective-permute-start.10 = (f32[64,512]{1,0:T(8,128)S(1)}, f32[64,512]{1,0:T(8,128)S(1)}, u32[]{:S(2)}, u32[]{:S(2)}) collective-permute-start(f32[64,512]{1,0:T(8,128)S(1)} %get-tuple-element.125), channel_id=1, source_target_pairs={{24,16},{28,20},{25,17},{29,21},{26,18},{30,22},{27,19},{31,23}} | collective-permute-start | bytes 393224 | tf_op jit(solution)/shard_map/ppermute | solution.py:337
  39.5 3.3 %collective-permute-start.11 = (f32[64,512]{1,0:T(8,128)S(1)}, f32[64,512]{1,0:T(8,128)S(1)}, u32[]{:S(2)}, u32[]{:S(2)}) collective-permute-start(f32[64,512]{1,0:T(8,128)S(1)} %far_terms.18.refs_0_), channel_id=1, source_target_pairs={{24,8},{28,12},{25,9},{29,13},{26,10},{30,14},{27,11},{31,15}} | collective-permute-start | bytes 393224 | tf_op jit(solution)/shard_map/ppermute | solution.py:337
  40.5 2.3 %collective-permute-start.12 = (f32[64,512]{1,0:T(8,128)S(1)}, f32[64,512]{1,0:T(8,128)S(1)}, u32[]{:S(2)}, u32[]{:S(2)}) collective-permute-start(f32[64,512]{1,0:T(8,128)S(1)} %get-tuple-element.127), channel_id=1, source_target_pairs={{16,8},{20,12},{17,9},{21,13},{18,10},{22,14},{19,11},{23,15}} | collective-permute-start | bytes 393224 | tf_op jit(solution)/shard_map/ppermute | solution.py:337
  41.4 9.0 %collective-permute-start.13 = (f32[64,512]{1,0:T(8,128)S(1)}, f32[64,512]{1,0:T(8,128)S(1)}, u32[]{:S(2)}, u32[]{:S(2)}) collective-permute-start(f32[64,512]{1,0:T(8,128)S(1)} %far_terms.19.refs_0_), channel_id=1, source_target_pairs={{16,0},{20,4},{17,1},{21,5},{18,2},{22,6},{19,3},{23,7}} | collective-permute-start | bytes 393224 | tf_op jit(solution)/shard_map/ppermute | solution.py:337
  43.1 11.7 %collective-permute-start.14 = (f32[64,512]{1,0:T(8,128)S(1)}, f32[64,512]{1,0:T(8,128)S(1)}, u32[]{:S(2)}, u32[]{:S(2)}) collective-permute-start(f32[64,512]{1,0:T(8,128)S(1)} %get-tuple-element.129), channel_id=1, source_target_pairs={{8,0},{12,4},{9,1},{13,5},{10,2},{14,6},{11,3},{15,7}} | collective-permute-start | bytes 393224 | tf_op jit(solution)/shard_map/ppermute | solution.py:337
  44.4 12.7 %copy-start.2 = (f32[1192,256]{1,0:T(8,128)S(1)}, f32[1192,256]{1,0:T(8,128)}, u32[]{:S(2)}) copy-start(f32[1192,256]{1,0:T(8,128)} %get-tuple-element.135.own.refs_6_) | copy-start | bytes 3661828
  55.1 5.7 %collective-permute-start.16 = (f32[64,512]{1,0:T(8,128)S(1)}, f32[64,512]{1,0:T(8,128)S(1)}, u32[]{:S(2)}, u32[]{:S(2)}) collective-permute-start(f32[64,512]{1,0:T(8,128)S(1)} %get-tuple-element.131), channel_id=1, source_target_pairs={{0,24},{4,28},{1,25},{5,29},{2,26},{6,30},{3,27},{7,31}} | collective-permute-start | bytes 393224 | tf_op jit(solution)/shard_map/ppermute | solution.py:337
  56.4 4.4 %collective-permute-start.15 = (f32[64,512]{1,0:T(8,128)S(1)}, f32[64,512]{1,0:T(8,128)S(1)}, u32[]{:S(2)}, u32[]{:S(2)}) collective-permute-start(f32[64,512]{1,0:T(8,128)S(1)} %far_terms.20.refs_0_), channel_id=1, source_target_pairs={{8,24},{12,28},{9,25},{13,29},{10,26},{14,30},{11,27},{15,31}} | collective-permute-start | bytes 393224 | tf_op jit(solution)/shard_map/ppermute | solution.py:337
  58.6 5.3 %collective-permute-start.18 = (f32[64,512]{1,0:T(8,128)S(1)}, f32[64,512]{1,0:T(8,128)S(1)}, u32[]{:S(2)}, u32[]{:S(2)}) collective-permute-start(f32[64,512]{1,0:T(8,128)S(1)} %far_terms.21.refs_0_), channel_id=1, source_target_pairs={{0,16},{4,20},{1,17},{5,21},{2,18},{6,22},{3,19},{7,23}} | collective-permute-start | bytes 393224 | tf_op jit(solution)/shard_map/ppermute | solution.py:337
  61.1 2.8 %collective-permute-start.19 = (f32[64,512]{1,0:T(8,128)S(1)}, f32[64,512]{1,0:T(8,128)S(1)}, u32[]{:S(2)}, u32[]{:S(2)}) collective-permute-start(f32[64,512]{1,0:T(8,128)S(1)} %get-tuple-element.144), channel_id=1, source_target_pairs={{24,16},{28,20},{25,17},{29,21},{26,18},{30,22},{27,19},{31,23}} | collective-permute-start | bytes 393224 | tf_op jit(solution)/shard_map/ppermute | solution.py:337
  63.2 3.3 %collective-permute-start.20 = (f32[64,512]{1,0:T(8,128)S(1)}, f32[64,512]{1,0:T(8,128)S(1)}, u32[]{:S(2)}, u32[]{:S(2)}) collective-permute-start(f32[64,512]{1,0:T(8,128)S(1)} %far_terms.22.refs_0_), channel_id=1, source_target_pairs={{24,8},{28,12},{25,9},{29,13},{26,10},{30,14},{27,11},{31,15}} | collective-permute-start | bytes 393224 | tf_op jit(solution)/shard_map/ppermute | solution.py:337
  64.2 2.3 %collective-permute-start.21 = (f32[64,512]{1,0:T(8,128)S(1)}, f32[64,512]{1,0:T(8,128)S(1)}, u32[]{:S(2)}, u32[]{:S(2)}) collective-permute-start(f32[64,512]{1,0:T(8,128)S(1)} %get-tuple-element.146), channel_id=1, source_target_pairs={{16,8},{20,12},{17,9},{21,13},{18,10},{22,14},{19,11},{23,15}} | collective-permute-start | bytes 393224 | tf_op jit(solution)/shard_map/ppermute | solution.py:337
  65.2 8.4 %collective-permute-start.22 = (f32[64,512]{1,0:T(8,128)S(1)}, f32[64,512]{1,0:T(8,128)S(1)}, u32[]{:S(2)}, u32[]{:S(2)}) collective-permute-start(f32[64,512]{1,0:T(8,128)S(1)} %far_terms.23.refs_0_), channel_id=1, source_target_pairs={{16,0},{20,4},{17,1},{21,5},{18,2},{22,6},{19,3},{23,7}} | collective-permute-start | bytes 393224 | tf_op jit(solution)/shard_map/ppermute | solution.py:337
  66.8 11.2 %collective-permute-start.23 = (f32[64,512]{1,0:T(8,128)S(1)}, f32[64,512]{1,0:T(8,128)S(1)}, u32[]{:S(2)}, u32[]{:S(2)}) collective-permute-start(f32[64,512]{1,0:T(8,128)S(1)} %get-tuple-element.148), channel_id=1, source_target_pairs={{8,0},{12,4},{9,1},{13,5},{10,2},{14,6},{11,3},{15,7}} | collective-permute-start | bytes 393224 | tf_op jit(solution)/shard_map/ppermute | solution.py:337
  78.3 5.8 %collective-permute-start.25 = (f32[64,512]{1,0:T(8,128)S(1)}, f32[64,512]{1,0:T(8,128)S(1)}, u32[]{:S(2)}, u32[]{:S(2)}) collective-permute-start(f32[64,512]{1,0:T(8,128)S(1)} %get-tuple-element.150), channel_id=1, source_target_pairs={{0,24},{4,28},{1,25},{5,29},{2,26},{6,30},{3,27},{7,31}} | collective-permute-start | bytes 393224 | tf_op jit(solution)/shard_map/ppermute | solution.py:337
  79.6 4.6 %collective-permute-start.24 = (f32[64,512]{1,0:T(8,128)S(1)}, f32[64,512]{1,0:T(8,128)S(1)}, u32[]{:S(2)}, u32[]{:S(2)}) collective-permute-start(f32[64,512]{1,0:T(8,128)S(1)} %far_terms.24.refs_0_), channel_id=1, source_target_pairs={{8,24},{12,28},{9,25},{13,29},{10,26},{14,30},{11,27},{15,31}} | collective-permute-start | bytes 393224 | tf_op jit(solution)/shard_map/ppermute | solution.py:337
  82.0 5.3 %collective-permute-start.27 = (f32[64,512]{1,0:T(8,128)S(1)}, f32[64,512]{1,0:T(8,128)S(1)}, u32[]{:S(2)}, u32[]{:S(2)}) collective-permute-start(f32[64,512]{1,0:T(8,128)S(1)} %far_terms.25.refs_0_), channel_id=1, source_target_pairs={{0,16},{4,20},{1,17},{5,21},{2,18},{6,22},{3,19},{7,23}} | collective-permute-start | bytes 393224 | tf_op jit(solution)/shard_map/ppermute | solution.py:337
  84.4 2.8 %collective-permute-start.28 = (f32[64,512]{1,0:T(8,128)S(1)}, f32[64,512]{1,0:T(8,128)S(1)}, u32[]{:S(2)}, u32[]{:S(2)}) collective-permute-start(f32[64,512]{1,0:T(8,128)S(1)} %get-tuple-element.163), channel_id=1, source_target_pairs={{24,16},{28,20},{25,17},{29,21},{26,18},{30,22},{27,19},{31,23}} | collective-permute-start | bytes 393224 | tf_op jit(solution)/shard_map/ppermute | solution.py:337
  86.6 3.3 %collective-permute-start.29 = (f32[64,512]{1,0:T(8,128)S(1)}, f32[64,512]{1,0:T(8,128)S(1)}, u32[]{:S(2)}, u32[]{:S(2)}) collective-permute-start(f32[64,512]{1,0:T(8,128)S(1)} %far_terms.26.refs_0_), channel_id=1, source_target_pairs={{24,8},{28,12},{25,9},{29,13},{26,10},{30,14},{27,11},{31,15}} | collective-permute-start | bytes 393224 | tf_op jit(solution)/shard_map/ppermute | solution.py:337
  87.6 2.3 %collective-permute-start.30 = (f32[64,512]{1,0:T(8,128)S(1)}, f32[64,512]{1,0:T(8,128)S(1)}, u32[]{:S(2)}, u32[]{:S(2)}) collective-permute-start(f32[64,512]{1,0:T(8,128)S(1)} %get-tuple-element.165), channel_id=1, source_target_pairs={{16,8},{20,12},{17,9},{21,13},{18,10},{22,14},{19,11},{23,15}} | collective-permute-start | bytes 393224 | tf_op jit(solution)/shard_map/ppermute | solution.py:337
  88.6 8.3 %collective-permute-start.31 = (f32[64,512]{1,0:T(8,128)S(1)}, f32[64,512]{1,0:T(8,128)S(1)}, u32[]{:S(2)}, u32[]{:S(2)}) collective-permute-start(f32[64,512]{1,0:T(8,128)S(1)} %far_terms.27.refs_0_), channel_id=1, source_target_pairs={{16,0},{20,4},{17,1},{21,5},{18,2},{22,6},{19,3},{23,7}} | collective-permute-start | bytes 393224 | tf_op jit(solution)/shard_map/ppermute | solution.py:337
  90.2 11.0 %collective-permute-start.32 = (f32[64,512]{1,0:T(8,128)S(1)}, f32[64,512]{1,0:T(8,128)S(1)}, u32[]{:S(2)}, u32[]{:S(2)}) collective-permute-start(f32[64,512]{1,0:T(8,128)S(1)} %get-tuple-element.167), channel_id=1, source_target_pairs={{8,0},{12,4},{9,1},{13,5},{10,2},{14,6},{11,3},{15,7}} | collective-permute-start | bytes 393224 | tf_op jit(solution)/shard_map/ppermute | solution.py:337
  91.5 11.2 %collective-permute-start.43 = (f32[64,256]{1,0:T(8,128)S(1)}, f32[64,256]{1,0:T(8,128)S(1)}, u32[]{:S(2)}, u32[]{:S(2)}) collective-permute-start(f32[64,256]{1,0:T(8,128)S(1)} %get-tuple-element.184), channel_id=1, source_target_pairs={{0,4},{4,0},{8,12},{12,8},{16,20},{20,16},{24,28},{28,24},{1,5},{5... | collective-permute-start | bytes 196616 | tf_op jit(solution)/shard_map/ppermute | solution.py:325
  91.6 11.1 %collective-permute-start.42 = (f32[64,256]{1,0:T(8,128)S(1)}, f32[64,256]{1,0:T(8,128)S(1)}, u32[]{:S(2)}, u32[]{:S(2)}) collective-permute-start(f32[64,256]{1,0:T(8,128)S(1)} %get-tuple-element.183), channel_id=1, source_target_pairs={{0,4},{4,0},{8,12},{12,8},{16,20},{20,16},{24,28},{28,24},{1,5},{5... | collective-permute-start | bytes 196616 | tf_op jit(solution)/shard_map/ppermute | solution.py:325
  92.1 10.7 %collective-permute-start.41 = (f32[64,256]{1,0:T(8,128)S(1)}, f32[64,256]{1,0:T(8,128)S(1)}, u32[]{:S(2)}, u32[]{:S(2)}) collective-permute-start(f32[64,256]{1,0:T(8,128)S(1)} %get-tuple-element.182), channel_id=1, source_target_pairs={{0,4},{4,0},{8,12},{12,8},{16,20},{20,16},{24,28},{28,24},{1,5},{5... | collective-permute-start | bytes 196616 | tf_op jit(solution)/shard_map/ppermute | solution.py:325
  102.1 5.3 %collective-permute-start.40 = (f32[64,256]{1,0:T(8,128)S(1)}, f32[64,256]{1,0:T(8,128)S(1)}, u32[]{:S(2)}, u32[]{:S(2)}) collective-permute-start(f32[64,256]{1,0:T(8,128)S(1)} %get-tuple-element.181), channel_id=1, source_target_pairs={{0,4},{4,0},{8,12},{12,8},{16,20},{20,16},{24,28},{28,24},{1,5},{5... | collective-permute-start | bytes 196616 | tf_op jit(solution)/shard_map/ppermute | solution.py:325
  102.2 3.4 %collective-permute-start.33 = (f32[32,128]{1,0:T(8,128)S(1)}, f32[32,128]{1,0:T(8,128)S(1)}, u32[]{:S(2)}, u32[]{:S(2)}) collective-permute-start(f32[32,128]{1,0:T(8,128)S(1)} %get-tuple-element.170), channel_id=1, source_target_pairs={{0,4},{4,0},{8,12},{12,8},{16,20},{20,16},{24,28},{28,24},{1,5},{5... | collective-permute-start | bytes 49160 | tf_op jit(solution)/shard_map/ppermute | solution.py:329
  102.7 4.7 %collective-permute-start.34 = (f32[32,128]{1,0:T(8,128)S(1)}, f32[32,128]{1,0:T(8,128)S(1)}, u32[]{:S(2)}, u32[]{:S(2)}) collective-permute-start(f32[32,128]{1,0:T(8,128)S(1)} %get-tuple-element.171), channel_id=1, source_target_pairs={{0,8},{4,12},{8,16},{12,20},{16,24},{20,28},{24,0},{28,4},{1,9},{5... | collective-permute-start | bytes 49160 | tf_op jit(solution)/shard_map/ppermute | solution.py:329
  102.7 6.8 %collective-permute-start.35 = (f32[32,128]{1,0:T(8,128)S(1)}, f32[32,128]{1,0:T(8,128)S(1)}, u32[]{:S(2)}, u32[]{:S(2)}) collective-permute-start(f32[32,128]{1,0:T(8,128)S(1)} %get-tuple-element.172), channel_id=1, source_target_pairs={{0,12},{4,8},{8,20},{12,16},{16,28},{20,24},{24,4},{28,0},{1,13},{... | collective-permute-start | bytes 49160 | tf_op jit(solution)/shard_map/ppermute | solution.py:329
  102.8 6.8 %collective-permute-start.36 = (f32[32,128]{1,0:T(8,128)S(1)}, f32[32,128]{1,0:T(8,128)S(1)}, u32[]{:S(2)}, u32[]{:S(2)}) collective-permute-start(f32[32,128]{1,0:T(8,128)S(1)} %get-tuple-element.173), channel_id=1, source_target_pairs={{0,16},{4,20},{8,24},{12,28},{16,0},{20,4},{24,8},{28,12},{1,17},{... | collective-permute-start | bytes 49160 | tf_op jit(solution)/shard_map/ppermute | solution.py:329
  105.6 3.9 %collective-permute-start.37 = (f32[32,128]{1,0:T(8,128)S(1)}, f32[32,128]{1,0:T(8,128)S(1)}, u32[]{:S(2)}, u32[]{:S(2)}) collective-permute-start(f32[32,128]{1,0:T(8,128)S(1)} %get-tuple-element.174), channel_id=1, source_target_pairs={{0,20},{4,16},{8,28},{12,24},{16,4},{20,0},{24,12},{28,8},{1,21},{... | collective-permute-start | bytes 49160 | tf_op jit(solution)/shard_map/ppermute | solution.py:329
  107.4 3.7 %collective-permute-start.38 = (f32[32,128]{1,0:T(8,128)S(1)}, f32[32,128]{1,0:T(8,128)S(1)}, u32[]{:S(2)}, u32[]{:S(2)}) collective-permute-start(f32[32,128]{1,0:T(8,128)S(1)} %get-tuple-element.175), channel_id=1, source_target_pairs={{0,24},{4,28},{8,0},{12,4},{16,8},{20,12},{24,16},{28,20},{1,25},{... | collective-permute-start | bytes 49160 | tf_op jit(solution)/shard_map/ppermute | solution.py:329
  107.4 3.7 %collective-permute-start.39 = (f32[32,128]{1,0:T(8,128)S(1)}, f32[32,128]{1,0:T(8,128)S(1)}, u32[]{:S(2)}, u32[]{:S(2)}) collective-permute-start(f32[32,128]{1,0:T(8,128)S(1)} %get-tuple-element.176), channel_id=1, source_target_pairs={{0,28},{4,24},{8,4},{12,0},{16,12},{20,8},{24,20},{28,16},{1,29},{... | collective-permute-start | bytes 49160 | tf_op jit(solution)/shard_map/ppermute | solution.py:329

commit v4 on v2

--- a/solution.py
+++ b/solution.py
@@ -465,7 +465,7 @@
 
     keeps[0], give, *parts = finish(0, values, total)
     gots[0] = swap(give)
-    parts = [parts[0]] + [shift(parts[by], by) for by in range(1, pairs)]
+    parts = [parts[0]] + [shift(parts[by], by) for by in range(pairs - 1, 0, -1)]
     order = range(rows_here)
     field = call(
         functools.partial(field_kernel, rows_here),

time: 111 us -> 111 us (level)
  waiting for transfers between devices: 44.8 us -> 46.2 us
    ppermute x3, waiting for transfers between devices: 1.39 us -> 2.77 us  [shift(): return lax.ppermute(x, 'blk', [(i, (i + 2 * by) % n) for i in range(n)])]
  transfers between devices with their start and end apart: 41 -> 41, of which waited for: 11 -> 12; matrix products, arithmetic and copies ran while one was open for 0% -> 0% of each run, Pallas kernels for 24% -> 24%
where the time goes in v4:
time: 111 us; the launch traced here: 110 us
  waiting for transfers between devices  46.2 us (42%)
  starting transfers between devices  32.7 us (29%)
  Pallas kernels  29.8 us (27%)
  between operations  1.47 us (1%)
    ppermute x29, waiting for transfers between devices, pass_on(): return lax.ppermute(x, 'blk', perm)  42.2 us
    pallas_call x47, Pallas kernels, call(): pl.pallas_call(kernel, out_shape=outs, in_specs=more.pop('in_specs', [VME...  29.8 us
    ppermute x29, starting transfers between devices, pass_on(): return lax.ppermute(x, 'blk', perm)  28.5 us
    ppermute x3, waiting for transfers between devices, shift(): return lax.ppermute(x, 'blk', [(i, (i + 2 * by) % n) for i in range(n)])  2.77 us
  transfers between devices with their start and end apart: 41, of which 12 were waited for; matrix products, arithmetic and copies ran while one was open for 0% of the time, Pallas kernels for 24%

profile of v4, /device:TPU:0, one launch (start us, length us, event | category | flops | bytes accessed | tf_op | source)
XLA Modules:
  0.0 110.1 jit_solution(11428770071501774803)
XLA Ops:
  0.6 2.9 %pack.2.own.refs_6_ = f32[1192,256]{1,0:T(8,128)} custom-call(s32[3,1,4]{2,1,0:T(1,128)} %bitcast.1, f32[4,1,256]{2,1,0:T(1,128)} %turnout.2, s32[4,1,256]{2,1,0:T(1,128)} %district.3, f32[4,1,3,256,256]{4,3,2,1,0:T(8,128)} %l_ref.3, f32[4,1,256,256]{3,2,1,0:T(8,128)} %d_ref.3, f32[4,1,256,128]{3,2,1,0:T(8,128)} %r_ref.3), custom_call_target="tpu_custom_call" | custom-call | bytes 2441216 | tf_op jit(solution)/shard_map/pack/pallas_call | solution.py:318
  4.1 3.8 %pack.3 = (f32[1192,256]{1,0:T(8,128)}, f32[1192,256]{1,0:T(8,128)}, f32[1192,256]{1,0:T(8,128)}) custom-call(s32[3,1,4]{2,1,0:T(1,128)} %bitcast.2, f32[4,1,256]{2,1,0:T(1,128)} %turnout.2, s32[4,1,256]{2,1,0:T(1,128)} %district.3, f32[4,1,3,256,256]{4,3,2,1,0:T(8,128)} %l_ref.3, f32[4,1,256,256]{3,2,1,0:T(8,128)} %d_ref.3, f32[4,1,256,128]{3,2,1,0:T(8,128)} %r_ref.3), custom_call_target="tpu_custom_call" | custom-call | bytes 7323648 | tf_op jit(solution)/shard_map/pack/pallas_call | solution.py:318
  8.5 1.2 %near_setup.4 = (bf16[512,512]{1,0:T(8,128)(2,1)S(1)}, bf16[512,512]{1,0:T(8,128)(2,1)S(1)}, bf16[4,256,256]{2,1,0:T(8,128)(2,1)S(1)}, bf16[4,256,256]{2,1,0:T(8,128)(2,1)S(1)}, f32[64,512]{1,0:T(8,128)S(1)}) custom-call(f32[1192,256]{1,0:T(8,128)S(1)} %copy-done, f32[1192,256]{1,0:T(8,128)S(1)} %collective-permute-done.oth.refs_7_), custom_call_target="tpu_custom_call" | custom-call | flops 704643072 | bytes 6291456 | tf_op jit(solution)/shard_map/near_setup/pallas_call | solution.py:318
  10.0 0.7 collective-permute-start.1
  10.6 1.2 %far_setup.4 = (bf16[512,512]{1,0:T(8,128)(2,1)S(1)}, bf16[512,512]{1,0:T(8,128)(2,1)S(1)}) custom-call(f32[1192,256]{1,0:T(8,128)S(1)} %copy-done, f32[1192,256]{1,0:T(8,128)S(1)} %collective-permute-done.oth.refs_7_, bf16[4,256,256]{2,1,0:T(8,128)(2,1)S(1)} %get-tuple-element.96.mh.refs_4_, bf16[4,256,256]{2,1,0:T(8,128)(2,1)S(1)} %get-tuple-element.97.ml.refs_5_), custom_call_target="tpu_custom_call" | custom-call | flops 503316480 | bytes 6291456 | tf_op jit(solution)/shard_map/far_setup/pallas_call | solution.py:318
  12.2 0.7 collective-permute-start.2
  14.1 1.4 %collective-permute-start.4 = (f32[64,512]{1,0:T(8,128)S(1)}, f32[64,512]{1,0:T(8,128)S(1)}, u32[]{:S(2)}, u32[]{:S(2)}) collective-permute-start(f32[64,512]{1,0:T(8,128)S(1)} %far_terms.15.refs_0_), channel_id=1, source_target_pairs={{16,0},{20,4},{17,1},{21,5},{18,2},{22,6},{19,3},{23,7}} | collective-permute-start | bytes 393224 | tf_op jit(solution)/shard_map/ppermute | solution.py:341
  15.9 1.3 %collective-permute-start.5 = (f32[64,512]{1,0:T(8,128)S(1)}, f32[64,512]{1,0:T(8,128)S(1)}, u32[]{:S(2)}, u32[]{:S(2)}) collective-permute-start(f32[64,512]{1,0:T(8,128)S(1)} %get-tuple-element.104), channel_id=1, source_target_pairs={{8,0},{12,4},{9,1},{13,5},{10,2},{14,6},{11,3},{15,7}} | collective-permute-start | bytes 393224 | tf_op jit(solution)/shard_map/ppermute | solution.py:341
  17.7 9.1 %collective-permute-done.4.refs_1_ = f32[64,512]{1,0:T(8,128)S(1)} collective-permute-done((f32[64,512]{1,0:T(8,128)S(1)}, f32[64,512]{1,0:T(8,128)S(1)}, u32[]{:S(2)}, u32[]{:S(2)}) %collective-permute-start.4) | collective-permute-done | bytes 131104 | tf_op jit(solution)/shard_map/ppermute | solution.py:341
  26.8 4.2 %collective-permute-done.5.refs_2_ = f32[64,512]{1,0:T(8,128)S(1)} collective-permute-done((f32[64,512]{1,0:T(8,128)S(1)}, f32[64,512]{1,0:T(8,128)S(1)}, u32[]{:S(2)}, u32[]{:S(2)}) %collective-permute-start.5) | collective-permute-done | bytes 131104 | tf_op jit(solution)/shard_map/ppermute | solution.py:341
  31.4 1.3 %collective-permute-start.7 = (f32[64,512]{1,0:T(8,128)S(1)}, f32[64,512]{1,0:T(8,128)S(1)}, u32[]{:S(2)}, u32[]{:S(2)}) collective-permute-start(f32[64,512]{1,0:T(8,128)S(1)} %get-tuple-element.106), channel_id=1, source_target_pairs={{0,24},{4,28},{1,25},{5,29},{2,26},{6,30},{3,27},{7,31}} | collective-permute-start | bytes 393224 | tf_op jit(solution)/shard_map/ppermute | solution.py:341
  33.4 1.2 %near_setup.5 = (bf16[512,512]{1,0:T(8,128)(2,1)S(1)}, bf16[512,512]{1,0:T(8,128)(2,1)S(1)}, bf16[4,256,256]{2,1,0:T(8,128)(2,1)S(1)}, bf16[4,256,256]{2,1,0:T(8,128)(2,1)S(1)}, f32[64,512]{1,0:T(8,128)S(1)}) custom-call(f32[1192,256]{1,0:T(8,128)S(1)} %copy-done.3, f32[1192,256]{1,0:T(8,128)S(1)} %collective-permute-done.8.oth.refs_7_), custom_call_target="tpu_custom_call" | custom-call | flops 704643072 | bytes 6291456 | tf_op jit(solution)/shard_map/near_setup/pallas_call | solution.py:318
  34.9 1.3 %collective-permute-start.9 = (f32[64,512]{1,0:T(8,128)S(1)}, f32[64,512]{1,0:T(8,128)S(1)}, u32[]{:S(2)}, u32[]{:S(2)}) collective-permute-start(f32[64,512]{1,0:T(8,128)S(1)} %far_terms.17.refs_0_), channel_id=1, source_target_pairs={{0,16},{4,20},{1,17},{5,21},{2,18},{6,22},{3,19},{7,23}} | collective-permute-start | bytes 393224 | tf_op jit(solution)/shard_map/ppermute | solution.py:341
  36.2 0.9 finish.4
  38.0 1.2 %far_setup.5 = (bf16[512,512]{1,0:T(8,128)(2,1)S(1)}, bf16[512,512]{1,0:T(8,128)(2,1)S(1)}) custom-call(f32[1192,256]{1,0:T(8,128)S(1)} %copy-done.3, f32[1192,256]{1,0:T(8,128)S(1)} %collective-permute-done.8.oth.refs_7_, bf16[4,256,256]{2,1,0:T(8,128)(2,1)S(1)} %get-tuple-element.115.mh.refs_4_, bf16[4,256,256]{2,1,0:T(8,128)(2,1)S(1)} %get-tuple-element.116.ml.refs_5_), custom_call_target="tpu_custom_call" | custom-call | flops 503316480 | bytes 6291456 | tf_op jit(solution)/shard_map/far_setup/pallas_call | solution.py:318
  40.5 0.7 collective-permute-start.12
  41.4 1.3 %collective-permute-start.13 = (f32[64,512]{1,0:T(8,128)S(1)}, f32[64,512]{1,0:T(8,128)S(1)}, u32[]{:S(2)}, u32[]{:S(2)}) collective-permute-start(f32[64,512]{1,0:T(8,128)S(1)} %far_terms.19.refs_0_), channel_id=1, source_target_pairs={{16,0},{20,4},{17,1},{21,5},{18,2},{22,6},{19,3},{23,7}} | collective-permute-start | bytes 393224 | tf_op jit(solution)/shard_map/ppermute | solution.py:341
  43.1 1.3 %collective-permute-start.14 = (f32[64,512]{1,0:T(8,128)S(1)}, f32[64,512]{1,0:T(8,128)S(1)}, u32[]{:S(2)}, u32[]{:S(2)}) collective-permute-start(f32[64,512]{1,0:T(8,128)S(1)} %get-tuple-element.123), channel_id=1, source_target_pairs={{8,0},{12,4},{9,1},{13,5},{10,2},{14,6},{11,3},{15,7}} | collective-permute-start | bytes 393224 | tf_op jit(solution)/shard_map/ppermute | solution.py:341
  44.7 5.7 %collective-permute-done.13.refs_1_ = f32[64,512]{1,0:T(8,128)S(1)} collective-permute-done((f32[64,512]{1,0:T(8,128)S(1)}, f32[64,512]{1,0:T(8,128)S(1)}, u32[]{:S(2)}, u32[]{:S(2)}) %collective-permute-start.13) | collective-permute-done | bytes 131104 | tf_op jit(solution)/shard_map/ppermute | solution.py:341
  50.4 4.4 %collective-permute-done.14.refs_2_ = f32[64,512]{1,0:T(8,128)S(1)} collective-permute-done((f32[64,512]{1,0:T(8,128)S(1)}, f32[64,512]{1,0:T(8,128)S(1)}, u32[]{:S(2)}, u32[]{:S(2)}) %collective-permute-start.14) | collective-permute-done | bytes 131104 | tf_op jit(solution)/shard_map/ppermute | solution.py:341
  55.1 1.3 %collective-permute-start.16 = (f32[64,512]{1,0:T(8,128)S(1)}, f32[64,512]{1,0:T(8,128)S(1)}, u32[]{:S(2)}, u32[]{:S(2)}) collective-permute-start(f32[64,512]{1,0:T(8,128)S(1)} %get-tuple-element.125), channel_id=1, source_target_pairs={{0,24},{4,28},{1,25},{5,29},{2,26},{6,30},{3,27},{7,31}} | collective-permute-start | bytes 393224 | tf_op jit(solution)/shard_map/ppermute | solution.py:341
  56.4 0.7 collective-permute-start.15
  57.1 1.2 %near_setup.6 = (bf16[512,512]{1,0:T(8,128)(2,1)S(1)}, bf16[512,512]{1,0:T(8,128)(2,1)S(1)}, bf16[4,256,256]{2,1,0:T(8,128)(2,1)S(1)}, bf16[4,256,256]{2,1,0:T(8,128)(2,1)S(1)}, f32[64,512]{1,0:T(8,128)S(1)}) custom-call(f32[1192,256]{1,0:T(8,128)S(1)} %copy-done.2, f32[1192,256]{1,0:T(8,128)S(1)} %collective-permute-done.17.oth.refs_7_), custom_call_target="tpu_custom_call" | custom-call | flops 704643072 | bytes 6291456 | tf_op jit(solution)/shard_map/near_setup/pallas_call | solution.py:318
  58.6 1.3 %collective-permute-start.18 = (f32[64,512]{1,0:T(8,128)S(1)}, f32[64,512]{1,0:T(8,128)S(1)}, u32[]{:S(2)}, u32[]{:S(2)}) collective-permute-start(f32[64,512]{1,0:T(8,128)S(1)} %far_terms.21.refs_0_), channel_id=1, source_target_pairs={{0,16},{4,20},{1,17},{5,21},{2,18},{6,22},{3,19},{7,23}} | collective-permute-start | bytes 393224 | tf_op jit(solution)/shard_map/ppermute | solution.py:341
  59.9 0.9 finish.5
  61.8 1.2 %far_setup.6 = (bf16[512,512]{1,0:T(8,128)(2,1)S(1)}, bf16[512,512]{1,0:T(8,128)(2,1)S(1)}) custom-call(f32[1192,256]{1,0:T(8,128)S(1)} %copy-done.2, f32[1192,256]{1,0:T(8,128)S(1)} %collective-permute-done.17.oth.refs_7_, bf16[4,256,256]{2,1,0:T(8,128)(2,1)S(1)} %get-tuple-element.134.mh.refs_4_, bf16[4,256,256]{2,1,0:T(8,128)(2,1)S(1)} %get-tuple-element.135.ml.refs_5_), custom_call_target="tpu_custom_call" | custom-call | flops 503316480 | bytes 6291456 | tf_op jit(solution)/shard_map/far_setup/pallas_call | solution.py:318
  65.2 1.3 %collective-permute-start.22 = (f32[64,512]{1,0:T(8,128)S(1)}, f32[64,512]{1,0:T(8,128)S(1)}, u32[]{:S(2)}, u32[]{:S(2)}) collective-permute-start(f32[64,512]{1,0:T(8,128)S(1)} %far_terms.23.refs_0_), channel_id=1, source_target_pairs={{16,0},{20,4},{17,1},{21,5},{18,2},{22,6},{19,3},{23,7}} | collective-permute-start | bytes 393224 | tf_op jit(solution)/shard_map/ppermute | solution.py:341
  66.8 1.3 %collective-permute-start.23 = (f32[64,512]{1,0:T(8,128)S(1)}, f32[64,512]{1,0:T(8,128)S(1)}, u32[]{:S(2)}, u32[]{:S(2)}) collective-permute-start(f32[64,512]{1,0:T(8,128)S(1)} %get-tuple-element.142), channel_id=1, source_target_pairs={{8,0},{12,4},{9,1},{13,5},{10,2},{14,6},{11,3},{15,7}} | collective-permute-start | bytes 393224 | tf_op jit(solution)/shard_map/ppermute | solution.py:341
  68.4 5.2 %collective-permute-done.22.refs_1_ = f32[64,512]{1,0:T(8,128)S(1)} collective-permute-done((f32[64,512]{1,0:T(8,128)S(1)}, f32[64,512]{1,0:T(8,128)S(1)}, u32[]{:S(2)}, u32[]{:S(2)}) %collective-permute-start.22) | collective-permute-done | bytes 131104 | tf_op jit(solution)/shard_map/ppermute | solution.py:341
  73.6 4.4 %collective-permute-done.23.refs_2_ = f32[64,512]{1,0:T(8,128)S(1)} collective-permute-done((f32[64,512]{1,0:T(8,128)S(1)}, f32[64,512]{1,0:T(8,128)S(1)}, u32[]{:S(2)}, u32[]{:S(2)}) %collective-permute-start.23) | collective-permute-done | bytes 131104 | tf_op jit(solution)/shard_map/ppermute | solution.py:341
  78.3 1.3 %collective-permute-start.25 = (f32[64,512]{1,0:T(8,128)S(1)}, f32[64,512]{1,0:T(8,128)S(1)}, u32[]{:S(2)}, u32[]{:S(2)}) collective-permute-start(f32[64,512]{1,0:T(8,128)S(1)} %get-tuple-element.144), channel_id=1, source_target_pairs={{0,24},{4,28},{1,25},{5,29},{2,26},{6,30},{3,27},{7,31}} | collective-permute-start | bytes 393224 | tf_op jit(solution)/shard_map/ppermute | solution.py:341
  79.6 0.8 collective-permute-start.24
  80.5 1.2 %near_setup.7 = (bf16[512,512]{1,0:T(8,128)(2,1)S(1)}, bf16[512,512]{1,0:T(8,128)(2,1)S(1)}, bf16[4,256,256]{2,1,0:T(8,128)(2,1)S(1)}, bf16[4,256,256]{2,1,0:T(8,128)(2,1)S(1)}, f32[64,512]{1,0:T(8,128)S(1)}) custom-call(f32[1192,256]{1,0:T(8,128)S(1)} %copy-done.1, f32[1192,256]{1,0:T(8,128)S(1)} %collective-permute-done.26.oth.refs_7_), custom_call_target="tpu_custom_call" | custom-call | flops 704643072 | bytes 6291456 | tf_op jit(solution)/shard_map/near_setup/pallas_call | solution.py:318
  82.0 1.3 %collective-permute-start.27 = (f32[64,512]{1,0:T(8,128)S(1)}, f32[64,512]{1,0:T(8,128)S(1)}, u32[]{:S(2)}, u32[]{:S(2)}) collective-permute-start(f32[64,512]{1,0:T(8,128)S(1)} %far_terms.25.refs_0_), channel_id=1, source_target_pairs={{0,16},{4,20},{1,17},{5,21},{2,18},{6,22},{3,19},{7,23}} | collective-permute-start | bytes 393224 | tf_op jit(solution)/shard_map/ppermute | solution.py:341
  83.3 0.9 finish.6
  85.1 1.2 %far_setup.7 = (bf16[512,512]{1,0:T(8,128)(2,1)S(1)}, bf16[512,512]{1,0:T(8,128)(2,1)S(1)}) custom-call(f32[1192,256]{1,0:T(8,128)S(1)} %copy-done.1, f32[1192,256]{1,0:T(8,128)S(1)} %collective-permute-done.26.oth.refs_7_, bf16[4,256,256]{2,1,0:T(8,128)(2,1)S(1)} %get-tuple-element.153.mh.refs_4_, bf16[4,256,256]{2,1,0:T(8,128)(2,1)S(1)} %get-tuple-element.154.ml.refs_5_), custom_call_target="tpu_custom_call" | custom-call | flops 503316480 | bytes 6291456 | tf_op jit(solution)/shard_map/far_setup/pallas_call | solution.py:318
  88.6 1.3 %collective-permute-start.31 = (f32[64,512]{1,0:T(8,128)S(1)}, f32[64,512]{1,0:T(8,128)S(1)}, u32[]{:S(2)}, u32[]{:S(2)}) collective-permute-start(f32[64,512]{1,0:T(8,128)S(1)} %far_terms.27.refs_0_), channel_id=1, source_target_pairs={{16,0},{20,4},{17,1},{21,5},{18,2},{22,6},{19,3},{23,7}} | collective-permute-start | bytes 393224 | tf_op jit(solution)/shard_map/ppermute | solution.py:341
  90.2 1.3 %collective-permute-start.32 = (f32[64,512]{1,0:T(8,128)S(1)}, f32[64,512]{1,0:T(8,128)S(1)}, u32[]{:S(2)}, u32[]{:S(2)}) collective-permute-start(f32[64,512]{1,0:T(8,128)S(1)} %get-tuple-element.161), channel_id=1, source_target_pairs={{8,0},{12,4},{9,1},{13,5},{10,2},{14,6},{11,3},{15,7}} | collective-permute-start | bytes 393224 | tf_op jit(solution)/shard_map/ppermute | solution.py:341
  92.1 4.7 %collective-permute-done.31.refs_0_ = f32[64,512]{1,0:T(8,128)S(1)} collective-permute-done((f32[64,512]{1,0:T(8,128)S(1)}, f32[64,512]{1,0:T(8,128)S(1)}, u32[]{:S(2)}, u32[]{:S(2)}) %collective-permute-start.31) | collective-permute-done | bytes 131104 | tf_op jit(solution)/shard_map/ppermute | solution.py:341
  96.8 4.4 %collective-permute-done.32.refs_1_ = f32[64,512]{1,0:T(8,128)S(1)} collective-permute-done((f32[64,512]{1,0:T(8,128)S(1)}, f32[64,512]{1,0:T(8,128)S(1)}, u32[]{:S(2)}, u32[]{:S(2)}) %collective-permute-start.32) | collective-permute-done | bytes 131104 | tf_op jit(solution)/shard_map/ppermute | solution.py:341
  101.2 0.9 finish.7
  102.3 1.0 collective-permute-start.34
  103.3 1.0 collective-permute-start.35
  104.3 1.0 field.1
  105.3 0.8 collective-permute-done.33.refs_1_
  106.3 1.8 %collective-permute-done.35.refs_3_ = f32[64,128]{1,0:T(8,128)S(1)} collective-permute-done((f32[64,128]{1,0:T(8,128)S(1)}, f32[64,128]{1,0:T(8,128)S(1)}, u32[]{:S(2)}, u32[]{:S(2)}) %collective-permute-start.35) | collective-permute-done | bytes 32800 | tf_op jit(solution)/shard_map/ppermute | solution.py:333
  108.2 1.2 %collective-permute-done.40.got = f32[32,128]{1,0:T(8,128)S(1)} collective-permute-done((f32[32,128]{1,0:T(8,128)S(1)}, f32[32,128]{1,0:T(8,128)S(1)}, u32[]{:S(2)}, u32[]{:S(2)}) %collective-permute-start.40) | collective-permute-done | bytes 16416 | tf_op jit(solution)/shard_map/ppermute | solution.py:330
  109.4 0.8 district_mean.1
  (89 shorter events, 17.4 us)
Async XLA Ops:
  3.5 5.0 %copy-start = (f32[1192,256]{1,0:T(8,128)S(1)}, f32[1192,256]{1,0:T(8,128)}, u32[]{:S(2)}) copy-start(f32[1192,256]{1,0:T(8,128)} %pack.2.own.refs_6_) | copy-start | bytes 3661828
  3.5 4.9 %collective-permute-start = (f32[1192,256]{1,0:T(8,128)}, f32[1192,256]{1,0:T(8,128)S(1)}, u32[]{:S(2)}, u32[]{:S(2)}) collective-permute-start(f32[1192,256]{1,0:T(8,128)} %pack.2.own.refs_6_), channel_id=1, source_target_pairs={{0,4},{4,0},{8,12},{12,8},{16,20},{20,16},{24,28},{28,24},{1,5},{5... | collective-permute-start | bytes 3661832 | tf_op jit(solution)/shard_map/ppermute | solution.py:330
  7.9 25.4 %collective-permute-start.8 = (f32[1192,256]{1,0:T(8,128)}, f32[1192,256]{1,0:T(8,128)S(1)}, u32[]{:S(2)}, u32[]{:S(2)}) collective-permute-start(f32[1192,256]{1,0:T(8,128)} %get-tuple-element.110.own.refs_6_), channel_id=1, source_target_pairs={{0,4},{4,0},{8,12},{12,8},{16,20},{20,16},{24,28},{28,24},{1,5},{5... | collective-permute-start | bytes 3661832 | tf_op jit(solution)/shard_map/ppermute | solution.py:330
  8.1 48.9 %collective-permute-start.17 = (f32[1192,256]{1,0:T(8,128)}, f32[1192,256]{1,0:T(8,128)S(1)}, u32[]{:S(2)}, u32[]{:S(2)}) collective-permute-start(f32[1192,256]{1,0:T(8,128)} %get-tuple-element.129.own.refs_6_), channel_id=1, source_target_pairs={{0,4},{4,0},{8,12},{12,8},{16,20},{20,16},{24,28},{28,24},{1,5},{5... | collective-permute-start | bytes 3661832 | tf_op jit(solution)/shard_map/ppermute | solution.py:330
  10.0 2.9 %collective-permute-start.1 = (f32[64,512]{1,0:T(8,128)S(1)}, f32[64,512]{1,0:T(8,128)S(1)}, u32[]{:S(2)}, u32[]{:S(2)}) collective-permute-start(f32[64,512]{1,0:T(8,128)S(1)} %get-tuple-element.100), channel_id=1, source_target_pairs={{24,16},{28,20},{25,17},{29,21},{26,18},{30,22},{27,19},{31,23}} | collective-permute-start | bytes 393224 | tf_op jit(solution)/shard_map/ppermute | solution.py:341
  12.2 3.4 %collective-permute-start.2 = (f32[64,512]{1,0:T(8,128)S(1)}, f32[64,512]{1,0:T(8,128)S(1)}, u32[]{:S(2)}, u32[]{:S(2)}) collective-permute-start(f32[64,512]{1,0:T(8,128)S(1)} %far_terms.14.refs_0_), channel_id=1, source_target_pairs={{24,8},{28,12},{25,9},{29,13},{26,10},{30,14},{27,11},{31,15}} | collective-permute-start | bytes 393224 | tf_op jit(solution)/shard_map/ppermute | solution.py:341
  13.1 2.4 %collective-permute-start.3 = (f32[64,512]{1,0:T(8,128)S(1)}, f32[64,512]{1,0:T(8,128)S(1)}, u32[]{:S(2)}, u32[]{:S(2)}) collective-permute-start(f32[64,512]{1,0:T(8,128)S(1)} %get-tuple-element.102), channel_id=1, source_target_pairs={{16,8},{20,12},{17,9},{21,13},{18,10},{22,14},{19,11},{23,15}} | collective-permute-start | bytes 393224 | tf_op jit(solution)/shard_map/ppermute | solution.py:341
  13.8 3.3 %copy-start.1 = (f32[1192,256]{1,0:T(8,128)S(1)}, f32[1192,256]{1,0:T(8,128)}, u32[]{:S(2)}) copy-start(f32[1192,256]{1,0:T(8,128)} %get-tuple-element.148.own.refs_6_) | copy-start | bytes 3661828
  14.1 12.7 %collective-permute-start.4 = (f32[64,512]{1,0:T(8,128)S(1)}, f32[64,512]{1,0:T(8,128)S(1)}, u32[]{:S(2)}, u32[]{:S(2)}) collective-permute-start(f32[64,512]{1,0:T(8,128)S(1)} %far_terms.15.refs_0_), channel_id=1, source_target_pairs={{16,0},{20,4},{17,1},{21,5},{18,2},{22,6},{19,3},{23,7}} | collective-permute-start | bytes 393224 | tf_op jit(solution)/shard_map/ppermute | solution.py:341
  15.9 15.2 %collective-permute-start.5 = (f32[64,512]{1,0:T(8,128)S(1)}, f32[64,512]{1,0:T(8,128)S(1)}, u32[]{:S(2)}, u32[]{:S(2)}) collective-permute-start(f32[64,512]{1,0:T(8,128)S(1)} %get-tuple-element.104), channel_id=1, source_target_pairs={{8,0},{12,4},{9,1},{13,5},{10,2},{14,6},{11,3},{15,7}} | collective-permute-start | bytes 393224 | tf_op jit(solution)/shard_map/ppermute | solution.py:341
  17.2 63.3 %collective-permute-start.26 = (f32[1192,256]{1,0:T(8,128)S(1)}, f32[1192,256]{1,0:T(8,128)S(1)}, u32[]{:S(2)}, u32[]{:S(2)}) collective-permute-start(f32[1192,256]{1,0:T(8,128)S(1)} %copy-done.1), channel_id=1, source_target_pairs={{0,4},{4,0},{8,12},{12,8},{16,20},{20,16},{24,28},{28,24},{1,5},{5... | collective-permute-start | bytes 3661832 | tf_op jit(solution)/shard_map/ppermute | solution.py:330
  17.4 15.9 %copy-start.3 = (f32[1192,256]{1,0:T(8,128)S(1)}, f32[1192,256]{1,0:T(8,128)}, u32[]{:S(2)}) copy-start(f32[1192,256]{1,0:T(8,128)} %get-tuple-element.110.own.refs_6_) | copy-start | bytes 3661828
  31.4 5.7 %collective-permute-start.7 = (f32[64,512]{1,0:T(8,128)S(1)}, f32[64,512]{1,0:T(8,128)S(1)}, u32[]{:S(2)}, u32[]{:S(2)}) collective-permute-start(f32[64,512]{1,0:T(8,128)S(1)} %get-tuple-element.106), channel_id=1, source_target_pairs={{0,24},{4,28},{1,25},{5,29},{2,26},{6,30},{3,27},{7,31}} | collective-permute-start | bytes 393224 | tf_op jit(solution)/shard_map/ppermute | solution.py:341
  32.7 4.4 %collective-permute-start.6 = (f32[64,512]{1,0:T(8,128)S(1)}, f32[64,512]{1,0:T(8,128)S(1)}, u32[]{:S(2)}, u32[]{:S(2)}) collective-permute-start(f32[64,512]{1,0:T(8,128)S(1)} %far_terms.16.refs_0_), channel_id=1, source_target_pairs={{8,24},{12,28},{9,25},{13,29},{10,26},{14,30},{11,27},{15,31}} | collective-permute-start | bytes 393224 | tf_op jit(solution)/shard_map/ppermute | solution.py:341
  34.9 5.3 %collective-permute-start.9 = (f32[64,512]{1,0:T(8,128)S(1)}, f32[64,512]{1,0:T(8,128)S(1)}, u32[]{:S(2)}, u32[]{:S(2)}) collective-permute-start(f32[64,512]{1,0:T(8,128)S(1)} %far_terms.17.refs_0_), channel_id=1, source_target_pairs={{0,16},{4,20},{1,17},{5,21},{2,18},{6,22},{3,19},{7,23}} | collective-permute-start | bytes 393224 | tf_op jit(solution)/shard_map/ppermute | solution.py:341
  37.3 2.8 %collective-permute-start.10 = (f32[64,512]{1,0:T(8,128)S(1)}, f32[64,512]{1,0:T(8,128)S(1)}, u32[]{:S(2)}, u32[]{:S(2)}) collective-permute-start(f32[64,512]{1,0:T(8,128)S(1)} %get-tuple-element.119), channel_id=1, source_target_pairs={{24,16},{28,20},{25,17},{29,21},{26,18},{30,22},{27,19},{31,23}} | collective-permute-start | bytes 393224 | tf_op jit(solution)/shard_map/ppermute | solution.py:341
  39.5 3.3 %collective-permute-start.11 = (f32[64,512]{1,0:T(8,128)S(1)}, f32[64,512]{1,0:T(8,128)S(1)}, u32[]{:S(2)}, u32[]{:S(2)}) collective-permute-start(f32[64,512]{1,0:T(8,128)S(1)} %far_terms.18.refs_0_), channel_id=1, source_target_pairs={{24,8},{28,12},{25,9},{29,13},{26,10},{30,14},{27,11},{31,15}} | collective-permute-start | bytes 393224 | tf_op jit(solution)/shard_map/ppermute | solution.py:341
  40.5 2.3 %collective-permute-start.12 = (f32[64,512]{1,0:T(8,128)S(1)}, f32[64,512]{1,0:T(8,128)S(1)}, u32[]{:S(2)}, u32[]{:S(2)}) collective-permute-start(f32[64,512]{1,0:T(8,128)S(1)} %get-tuple-element.121), channel_id=1, source_target_pairs={{16,8},{20,12},{17,9},{21,13},{18,10},{22,14},{19,11},{23,15}} | collective-permute-start | bytes 393224 | tf_op jit(solution)/shard_map/ppermute | solution.py:341
  41.4 9.0 %collective-permute-start.13 = (f32[64,512]{1,0:T(8,128)S(1)}, f32[64,512]{1,0:T(8,128)S(1)}, u32[]{:S(2)}, u32[]{:S(2)}) collective-permute-start(f32[64,512]{1,0:T(8,128)S(1)} %far_terms.19.refs_0_), channel_id=1, source_target_pairs={{16,0},{20,4},{17,1},{21,5},{18,2},{22,6},{19,3},{23,7}} | collective-permute-start | bytes 393224 | tf_op jit(solution)/shard_map/ppermute | solution.py:341
  43.1 11.7 %collective-permute-start.14 = (f32[64,512]{1,0:T(8,128)S(1)}, f32[64,512]{1,0:T(8,128)S(1)}, u32[]{:S(2)}, u32[]{:S(2)}) collective-permute-start(f32[64,512]{1,0:T(8,128)S(1)} %get-tuple-element.123), channel_id=1, source_target_pairs={{8,0},{12,4},{9,1},{13,5},{10,2},{14,6},{11,3},{15,7}} | collective-permute-start | bytes 393224 | tf_op jit(solution)/shard_map/ppermute | solution.py:341
  44.4 12.7 %copy-start.2 = (f32[1192,256]{1,0:T(8,128)S(1)}, f32[1192,256]{1,0:T(8,128)}, u32[]{:S(2)}) copy-start(f32[1192,256]{1,0:T(8,128)} %get-tuple-element.129.own.refs_6_) | copy-start | bytes 3661828
  55.1 5.7 %collective-permute-start.16 = (f32[64,512]{1,0:T(8,128)S(1)}, f32[64,512]{1,0:T(8,128)S(1)}, u32[]{:S(2)}, u32[]{:S(2)}) collective-permute-start(f32[64,512]{1,0:T(8,128)S(1)} %get-tuple-element.125), channel_id=1, source_target_pairs={{0,24},{4,28},{1,25},{5,29},{2,26},{6,30},{3,27},{7,31}} | collective-permute-start | bytes 393224 | tf_op jit(solution)/shard_map/ppermute | solution.py:341
  56.4 4.4 %collective-permute-start.15 = (f32[64,512]{1,0:T(8,128)S(1)}, f32[64,512]{1,0:T(8,128)S(1)}, u32[]{:S(2)}, u32[]{:S(2)}) collective-permute-start(f32[64,512]{1,0:T(8,128)S(1)} %far_terms.20.refs_0_), channel_id=1, source_target_pairs={{8,24},{12,28},{9,25},{13,29},{10,26},{14,30},{11,27},{15,31}} | collective-permute-start | bytes 393224 | tf_op jit(solution)/shard_map/ppermute | solution.py:341
  58.6 5.3 %collective-permute-start.18 = (f32[64,512]{1,0:T(8,128)S(1)}, f32[64,512]{1,0:T(8,128)S(1)}, u32[]{:S(2)}, u32[]{:S(2)}) collective-permute-start(f32[64,512]{1,0:T(8,128)S(1)} %far_terms.21.refs_0_), channel_id=1, source_target_pairs={{0,16},{4,20},{1,17},{5,21},{2,18},{6,22},{3,19},{7,23}} | collective-permute-start | bytes 393224 | tf_op jit(solution)/shard_map/ppermute | solution.py:341
  61.1 2.8 %collective-permute-start.19 = (f32[64,512]{1,0:T(8,128)S(1)}, f32[64,512]{1,0:T(8,128)S(1)}, u32[]{:S(2)}, u32[]{:S(2)}) collective-permute-start(f32[64,512]{1,0:T(8,128)S(1)} %get-tuple-element.138), channel_id=1, source_target_pairs={{24,16},{28,20},{25,17},{29,21},{26,18},{30,22},{27,19},{31,23}} | collective-permute-start | bytes 393224 | tf_op jit(solution)/shard_map/ppermute | solution.py:341
  63.2 3.3 %collective-permute-start.20 = (f32[64,512]{1,0:T(8,128)S(1)}, f32[64,512]{1,0:T(8,128)S(1)}, u32[]{:S(2)}, u32[]{:S(2)}) collective-permute-start(f32[64,512]{1,0:T(8,128)S(1)} %far_terms.22.refs_0_), channel_id=1, source_target_pairs={{24,8},{28,12},{25,9},{29,13},{26,10},{30,14},{27,11},{31,15}} | collective-permute-start | bytes 393224 | tf_op jit(solution)/shard_map/ppermute | solution.py:341
  64.2 2.3 %collective-permute-start.21 = (f32[64,512]{1,0:T(8,128)S(1)}, f32[64,512]{1,0:T(8,128)S(1)}, u32[]{:S(2)}, u32[]{:S(2)}) collective-permute-start(f32[64,512]{1,0:T(8,128)S(1)} %get-tuple-element.140), channel_id=1, source_target_pairs={{16,8},{20,12},{17,9},{21,13},{18,10},{22,14},{19,11},{23,15}} | collective-permute-start | bytes 393224 | tf_op jit(solution)/shard_map/ppermute | solution.py:341
  65.2 8.4 %collective-permute-start.22 = (f32[64,512]{1,0:T(8,128)S(1)}, f32[64,512]{1,0:T(8,128)S(1)}, u32[]{:S(2)}, u32[]{:S(2)}) collective-permute-start(f32[64,512]{1,0:T(8,128)S(1)} %far_terms.23.refs_0_), channel_id=1, source_target_pairs={{16,0},{20,4},{17,1},{21,5},{18,2},{22,6},{19,3},{23,7}} | collective-permute-start | bytes 393224 | tf_op jit(solution)/shard_map/ppermute | solution.py:341
  66.8 11.2 %collective-permute-start.23 = (f32[64,512]{1,0:T(8,128)S(1)}, f32[64,512]{1,0:T(8,128)S(1)}, u32[]{:S(2)}, u32[]{:S(2)}) collective-permute-start(f32[64,512]{1,0:T(8,128)S(1)} %get-tuple-element.142), channel_id=1, source_target_pairs={{8,0},{12,4},{9,1},{13,5},{10,2},{14,6},{11,3},{15,7}} | collective-permute-start | bytes 393224 | tf_op jit(solution)/shard_map/ppermute | solution.py:341
  78.3 5.8 %collective-permute-start.25 = (f32[64,512]{1,0:T(8,128)S(1)}, f32[64,512]{1,0:T(8,128)S(1)}, u32[]{:S(2)}, u32[]{:S(2)}) collective-permute-start(f32[64,512]{1,0:T(8,128)S(1)} %get-tuple-element.144), channel_id=1, source_target_pairs={{0,24},{4,28},{1,25},{5,29},{2,26},{6,30},{3,27},{7,31}} | collective-permute-start | bytes 393224 | tf_op jit(solution)/shard_map/ppermute | solution.py:341
  79.6 4.6 %collective-permute-start.24 = (f32[64,512]{1,0:T(8,128)S(1)}, f32[64,512]{1,0:T(8,128)S(1)}, u32[]{:S(2)}, u32[]{:S(2)}) collective-permute-start(f32[64,512]{1,0:T(8,128)S(1)} %far_terms.24.refs_0_), channel_id=1, source_target_pairs={{8,24},{12,28},{9,25},{13,29},{10,26},{14,30},{11,27},{15,31}} | collective-permute-start | bytes 393224 | tf_op jit(solution)/shard_map/ppermute | solution.py:341
  82.0 5.3 %collective-permute-start.27 = (f32[64,512]{1,0:T(8,128)S(1)}, f32[64,512]{1,0:T(8,128)S(1)}, u32[]{:S(2)}, u32[]{:S(2)}) collective-permute-start(f32[64,512]{1,0:T(8,128)S(1)} %far_terms.25.refs_0_), channel_id=1, source_target_pairs={{0,16},{4,20},{1,17},{5,21},{2,18},{6,22},{3,19},{7,23}} | collective-permute-start | bytes 393224 | tf_op jit(solution)/shard_map/ppermute | solution.py:341
  84.5 2.8 %collective-permute-start.28 = (f32[64,512]{1,0:T(8,128)S(1)}, f32[64,512]{1,0:T(8,128)S(1)}, u32[]{:S(2)}, u32[]{:S(2)}) collective-permute-start(f32[64,512]{1,0:T(8,128)S(1)} %get-tuple-element.157), channel_id=1, source_target_pairs={{24,16},{28,20},{25,17},{29,21},{26,18},{30,22},{27,19},{31,23}} | collective-permute-start | bytes 393224 | tf_op jit(solution)/shard_map/ppermute | solution.py:341
  86.6 3.3 %collective-permute-start.29 = (f32[64,512]{1,0:T(8,128)S(1)}, f32[64,512]{1,0:T(8,128)S(1)}, u32[]{:S(2)}, u32[]{:S(2)}) collective-permute-start(f32[64,512]{1,0:T(8,128)S(1)} %far_terms.26.refs_0_), channel_id=1, source_target_pairs={{24,8},{28,12},{25,9},{29,13},{26,10},{30,14},{27,11},{31,15}} | collective-permute-start | bytes 393224 | tf_op jit(solution)/shard_map/ppermute | solution.py:341
  87.6 2.3 %collective-permute-start.30 = (f32[64,512]{1,0:T(8,128)S(1)}, f32[64,512]{1,0:T(8,128)S(1)}, u32[]{:S(2)}, u32[]{:S(2)}) collective-permute-start(f32[64,512]{1,0:T(8,128)S(1)} %get-tuple-element.159), channel_id=1, source_target_pairs={{16,8},{20,12},{17,9},{21,13},{18,10},{22,14},{19,11},{23,15}} | collective-permute-start | bytes 393224 | tf_op jit(solution)/shard_map/ppermute | solution.py:341
  88.6 8.3 %collective-permute-start.31 = (f32[64,512]{1,0:T(8,128)S(1)}, f32[64,512]{1,0:T(8,128)S(1)}, u32[]{:S(2)}, u32[]{:S(2)}) collective-permute-start(f32[64,512]{1,0:T(8,128)S(1)} %far_terms.27.refs_0_), channel_id=1, source_target_pairs={{16,0},{20,4},{17,1},{21,5},{18,2},{22,6},{19,3},{23,7}} | collective-permute-start | bytes 393224 | tf_op jit(solution)/shard_map/ppermute | solution.py:341
  90.2 11.0 %collective-permute-start.32 = (f32[64,512]{1,0:T(8,128)S(1)}, f32[64,512]{1,0:T(8,128)S(1)}, u32[]{:S(2)}, u32[]{:S(2)}) collective-permute-start(f32[64,512]{1,0:T(8,128)S(1)} %get-tuple-element.161), channel_id=1, source_target_pairs={{8,0},{12,4},{9,1},{13,5},{10,2},{14,6},{11,3},{15,7}} | collective-permute-start | bytes 393224 | tf_op jit(solution)/shard_map/ppermute | solution.py:341
  91.5 10.8 %collective-permute-start.39 = (f32[64,256]{1,0:T(8,128)S(1)}, f32[64,256]{1,0:T(8,128)S(1)}, u32[]{:S(2)}, u32[]{:S(2)}) collective-permute-start(f32[64,256]{1,0:T(8,128)S(1)} %get-tuple-element.174), channel_id=1, source_target_pairs={{0,4},{4,0},{8,12},{12,8},{16,20},{20,16},{24,28},{28,24},{1,5},{5... | collective-permute-start | bytes 196616 | tf_op jit(solution)/shard_map/ppermute | solution.py:330
  91.6 11.7 %collective-permute-start.38 = (f32[64,256]{1,0:T(8,128)S(1)}, f32[64,256]{1,0:T(8,128)S(1)}, u32[]{:S(2)}, u32[]{:S(2)}) collective-permute-start(f32[64,256]{1,0:T(8,128)S(1)} %get-tuple-element.173), channel_id=1, source_target_pairs={{0,4},{4,0},{8,12},{12,8},{16,20},{20,16},{24,28},{28,24},{1,5},{5... | collective-permute-start | bytes 196616 | tf_op jit(solution)/shard_map/ppermute | solution.py:330
  92.1 12.3 %collective-permute-start.37 = (f32[64,256]{1,0:T(8,128)S(1)}, f32[64,256]{1,0:T(8,128)S(1)}, u32[]{:S(2)}, u32[]{:S(2)}) collective-permute-start(f32[64,256]{1,0:T(8,128)S(1)} %get-tuple-element.172), channel_id=1, source_target_pairs={{0,4},{4,0},{8,12},{12,8},{16,20},{20,16},{24,28},{28,24},{1,5},{5... | collective-permute-start | bytes 196616 | tf_op jit(solution)/shard_map/ppermute | solution.py:330
  102.1 2.2 %collective-permute-start.36 = (f32[64,256]{1,0:T(8,128)S(1)}, f32[64,256]{1,0:T(8,128)S(1)}, u32[]{:S(2)}, u32[]{:S(2)}) collective-permute-start(f32[64,256]{1,0:T(8,128)S(1)} %get-tuple-element.171), channel_id=1, source_target_pairs={{0,4},{4,0},{8,12},{12,8},{16,20},{20,16},{24,28},{28,24},{1,5},{5... | collective-permute-start | bytes 196616 | tf_op jit(solution)/shard_map/ppermute | solution.py:330
  102.2 4.0 %collective-permute-start.33 = (f32[64,128]{1,0:T(8,128)S(1)}, f32[64,128]{1,0:T(8,128)S(1)}, u32[]{:S(2)}, u32[]{:S(2)}) collective-permute-start(f32[64,128]{1,0:T(8,128)S(1)} %get-tuple-element.164), channel_id=1, source_target_pairs={{0,24},{4,28},{8,0},{12,4},{16,8},{20,12},{24,16},{28,20},{1,25},{... | collective-permute-start | bytes 98312 | tf_op jit(solution)/shard_map/ppermute | solution.py:333
  102.3 4.0 %collective-permute-start.34 = (f32[64,128]{1,0:T(8,128)S(1)}, f32[64,128]{1,0:T(8,128)S(1)}, u32[]{:S(2)}, u32[]{:S(2)}) collective-permute-start(f32[64,128]{1,0:T(8,128)S(1)} %get-tuple-element.165), channel_id=1, source_target_pairs={{0,16},{4,20},{8,24},{12,28},{16,0},{20,4},{24,8},{28,12},{1,17},{... | collective-permute-start | bytes 98312 | tf_op jit(solution)/shard_map/ppermute | solution.py:333
  103.3 4.8 %collective-permute-start.35 = (f32[64,128]{1,0:T(8,128)S(1)}, f32[64,128]{1,0:T(8,128)S(1)}, u32[]{:S(2)}, u32[]{:S(2)}) collective-permute-start(f32[64,128]{1,0:T(8,128)S(1)} %get-tuple-element.166), channel_id=1, source_target_pairs={{0,8},{4,12},{8,16},{12,20},{16,24},{20,28},{24,0},{28,4},{1,9},{5... | collective-permute-start | bytes 98312 | tf_op jit(solution)/shard_map/ppermute | solution.py:333
  108.1 1.2 %collective-permute-start.40 = (f32[32,128]{1,0:T(8,128)S(1)}, f32[32,128]{1,0:T(8,128)S(1)}, u32[]{:S(2)}, u32[]{:S(2)}) collective-permute-start(f32[32,128]{1,0:T(8,128)S(1)} %get-tuple-element.181), channel_id=1, source_target_pairs={{0,4},{4,0},{8,12},{12,8},{16,20},{20,16},{24,28},{28,24},{1,5},{5... | collective-permute-start | bytes 49160 | tf_op jit(solution)/shard_map/ppermute | solution.py:330
